TPU v7x, 32 devices: a whole 2x2x4 slice. The times are simulated.
32 devices in a mesh: dp: 8 (over y, x, core), tensor: 4 (over z).
Axes of the slice: x: 2, y: 2, z: 4, core: 2. Of those that a mesh axis runs over, the one named last changes fastest.
Arguments:
- tokens: bfloat16 [16384, 768], P('dp'), may hold values from -6 to 6
- lengths: int32 [16], P('dp'), may hold values from 256 to 1024
- cotangent: bfloat16 [16384, 768], P('dp'), may hold values from -6 to 6
- qkv_weight: bfloat16 [3, 768, 768], P(None, None, 'tensor'), may hold values from -0.21875 to 0.21875
- qv_bias: float32 [2, 768], P(None, 'tensor'), may hold values from -3 to 3
- out_weight: bfloat16 [768, 768], P('tensor'), may hold values from -0.875 to 0.875
- out_bias: float32 [768], replicated, may hold values from -3 to 3
- first_gain: float32 [768], replicated, may hold values from 0.5 to 1.5
- first_shift: float32 [768], replicated, may hold values from -2 to 2
- up_weight: bfloat16 [768, 3072], P(None, 'tensor'), may hold values from -0.21875 to 0.21875
- up_bias: float32 [3072], P('tensor'), may hold values from -3 to 3
- down_weight: bfloat16 [3072, 768], P('tensor'), may hold values from -0.15625 to 0.15625
- down_bias: float32 [768], replicated, may hold values from -3 to 3
- second_gain: float32 [768], replicated, may hold values from 0.5 to 1.5
- second_shift: float32 [768], replicated, may hold values from -2 to 2
Outputs:
- output: bfloat16 [16384, 768], P('dp')
- grad_tokens: float32 [16384, 768], P('dp', 'tensor')
- grad_qkv_weight: float32 [3, 768, 768], P(None, None, 'tensor')
- grad_qv_bias: float32 [2, 768], P(None, 'tensor')
- grad_out_weight: float32 [768, 768], P('tensor')
- grad_out_bias: float32 [768], replicated
- grad_first_gain: float32 [768], replicated
- grad_first_shift: float32 [768], replicated
- grad_up_weight: float32 [768, 3072], P(None, 'tensor')
- grad_up_bias: float32 [3072], P('tensor')
- grad_down_weight: float32 [3072, 768], P('tensor')
- grad_down_bias: float32 [768], replicated
- grad_second_gain: float32 [768], replicated
- grad_second_shift: float32 [768], replicated
All inputs are finite; a program needn't handle non-finite values.
Results may differ from a plain program's by a relative error of at most 0.014.
The roundings to bfloat16 on the way count: a program that leaves them out, or rounds other values in their place, can miss the bound.
Values sent between devices are 32-bit elements; how exact they have to be, the bound alone decides.
No kernel may reach another device: no remote copies, remote signals or barrier semaphores. Data moves between devices by JAX's collectives and lax.ppermute only.
A program may use at most 192 MiB of HBM per device.

v0:
```python
import jax
import jax.numpy as jnp
from jax import lax
from jax.sharding import PartitionSpec as P

HD = 64


EPS = 1e-05
MASKED = -1000000000.0


def layer_norm(hidden, gain, shift):
    center = hidden - jnp.mean(hidden, -1, keepdims=True)
    spread = jnp.mean(center * center, -1, keepdims=True)
    return center * lax.rsqrt(spread + EPS) * gain + shift


def exact_gelu(inputs):
    return jax.nn.gelu(inputs, approximate=False)


def masked_scores(queries, keys_low, valid, scale):
    scores = (
        jnp.einsum("bqhd,bkhd->bhqk", queries, keys_low, preferred_element_type=jnp.float32) * scale
    )
    return jnp.where(valid[:, None, None, :], scores, MASKED)


def on_device(
    tokens,
    lengths,
    cotangent,
    qkv_weight,
    qv_bias,
    out_weight,
    out_bias,
    first_gain,
    first_shift,
    up_weight,
    up_bias,
    down_weight,
    down_bias,
    second_gain,
    second_shift,
):
    batch = lengths.shape[0]
    rows = tokens.shape[0]
    seq_len = rows // batch
    width = tokens.shape[1]
    columns = qkv_weight.shape[2]
    local_heads = columns // HD
    scale = HD ** (-0.5)
    shape_heads = (batch, seq_len, local_heads, HD)
    project = jnp.einsum("nd,tdc->tnc", tokens, qkv_weight, preferred_element_type=jnp.float32)
    queries = (project[0] + qv_bias[0]).astype(jnp.bfloat16).reshape(shape_heads)
    keys_low = project[1].astype(jnp.bfloat16).reshape(shape_heads)
    values_low = (project[2] + qv_bias[1]).astype(jnp.bfloat16).reshape(shape_heads)
    positions = jnp.arange(seq_len, dtype=jnp.int32)
    valid = positions[None, :] < lengths[:, None]
    scores = masked_scores(queries, keys_low, valid, scale)
    highest = jnp.max(scores, -1, keepdims=True)
    expo = jnp.exp(scores - highest)
    totals = jnp.sum(expo, -1, keepdims=True)
    probs = expo / totals
    log_total = highest + jnp.log(totals)
    mixed = jnp.einsum(
        "bhqk,bkhd->bqhd",
        probs.astype(jnp.bfloat16),
        values_low,
        preferred_element_type=jnp.float32,
    )
    mixed = mixed.astype(jnp.bfloat16).reshape(rows, columns)
    attended = (
        lax.psum(jnp.dot(mixed, out_weight, preferred_element_type=jnp.float32), "tensor")
        + out_bias
    )
    first = tokens.astype(jnp.float32) + attended
    normed, first_back = jax.vjp(layer_norm, first, first_gain, first_shift)
    normed_low = normed.astype(jnp.bfloat16)
    hidden = jnp.dot(normed_low, up_weight, preferred_element_type=jnp.float32) + up_bias
    active_full, gelu_back = jax.vjp(exact_gelu, hidden)
    active = active_full.astype(jnp.bfloat16)
    branch = (
        lax.psum(jnp.dot(active, down_weight, preferred_element_type=jnp.float32), "tensor")
        + down_bias
    )
    second = normed + branch
    result, second_back = jax.vjp(layer_norm, second, second_gain, second_shift)
    d_second, grad_second_gain, grad_second_shift = second_back(cotangent.astype(jnp.float32))
    d_branch = d_second.astype(jnp.bfloat16)
    grad_down_weight = jnp.einsum("nf,nd->fd", active, d_branch, preferred_element_type=jnp.float32)
    grad_down_bias = jnp.sum(d_branch.astype(jnp.float32), 0)
    d_active = jnp.einsum("nd,fd->nf", d_branch, down_weight, preferred_element_type=jnp.float32)
    d_hidden = gelu_back(d_active)[0].astype(jnp.bfloat16)
    grad_up_weight = jnp.einsum(
        "nd,nf->df", normed_low, d_hidden, preferred_element_type=jnp.float32
    )
    grad_up_bias = jnp.sum(d_hidden.astype(jnp.float32), 0)
    mlp_grads = (
        grad_up_weight,
        grad_up_bias,
        grad_down_weight,
        grad_down_bias,
        grad_second_gain,
        grad_second_shift,
    )
    d_part = jnp.einsum("nf,df->nd", d_hidden, up_weight, preferred_element_type=jnp.float32)
    d_normed = lax.psum(d_part, "tensor") + d_second
    d_first, grad_first_gain, grad_first_shift = first_back(d_normed)
    d_attended = d_first.astype(jnp.bfloat16)
    grad_out_weight = jnp.einsum("nc,nd->cd", mixed, d_attended, preferred_element_type=jnp.float32)
    grad_out_bias = jnp.sum(d_attended.astype(jnp.float32), 0)
    d_mixed = jnp.einsum("nd,cd->nc", d_attended, out_weight, preferred_element_type=jnp.float32)
    d_mixed = d_mixed.astype(jnp.bfloat16).reshape(shape_heads)
    again = jnp.exp(masked_scores(queries, keys_low, valid, scale) - log_total)
    d_values = jnp.einsum(
        "bhqk,bqhd->bkhd", again.astype(jnp.bfloat16), d_mixed, preferred_element_type=jnp.float32
    )
    d_probs = jnp.einsum("bqhd,bkhd->bhqk", d_mixed, values_low, preferred_element_type=jnp.float32)
    row_dot = jnp.sum(d_probs * again, -1, keepdims=True)
    d_scores = (again * (d_probs - row_dot)).astype(jnp.bfloat16)
    d_queries = (
        jnp.einsum("bhqk,bkhd->bqhd", d_scores, keys_low, preferred_element_type=jnp.float32)
        * scale
    )
    d_keys = (
        jnp.einsum("bhqk,bqhd->bkhd", d_scores, queries, preferred_element_type=jnp.float32) * scale
    )
    d_project = jnp.stack(
        [
            d_queries.reshape(rows, columns),
            d_keys.reshape(rows, columns),
            d_values.reshape(rows, columns),
        ]
    ).astype(jnp.bfloat16)
    grad_qkv_weight = jnp.einsum(
        "nd,tnc->tdc", tokens, d_project, preferred_element_type=jnp.float32
    )
    bias_sums = jnp.sum(d_project.astype(jnp.float32), 1)
    grad_qv_bias = jnp.stack([bias_sums[0], bias_sums[2]])
    input_part = jnp.einsum(
        "tnc,tdc->nd", d_project, qkv_weight, preferred_element_type=jnp.float32
    )
    input_share = lax.psum_scatter(input_part, "tensor", scatter_dimension=1, tiled=True)
    piece = width // lax.axis_size("tensor")
    grad_tokens = input_share + lax.dynamic_slice_in_dim(
        d_first, lax.axis_index("tensor") * piece, piece, 1
    )
    attn_grads = (
        grad_qkv_weight,
        grad_qv_bias,
        grad_out_weight,
        grad_out_bias,
        grad_first_gain,
        grad_first_shift,
    )
    summed = lax.psum(attn_grads + mlp_grads, "dp")
    attn_grads = summed[:6]
    mlp_grads = summed[6:]
    return (
        result.astype(jnp.bfloat16),
        grad_tokens,
        attn_grads[0],
        attn_grads[1],
        attn_grads[2],
        attn_grads[3],
        attn_grads[4],
        attn_grads[5],
        mlp_grads[0],
        mlp_grads[1],
        mlp_grads[2],
        mlp_grads[3],
        mlp_grads[4],
        mlp_grads[5],
    )


def solution(mesh):
    placed = (
        P("dp", None),
        P("dp"),
        P("dp", None),
        P(None, None, "tensor"),
        P(None, "tensor"),
        P("tensor", None),
        P(),
        P(),
        P(),
        P(None, "tensor"),
        P("tensor"),
        P("tensor", None),
        P(),
        P(),
        P(),
    )
    return jax.shard_map(
        on_device,
        mesh=mesh,
        in_specs=placed,
        out_specs=(
            P("dp", None),
            P("dp", "tensor"),
            P(None, None, "tensor"),
            P(None, "tensor"),
            P("tensor", None),
            P(),
            P(),
            P(),
            P(None, "tensor"),
            P("tensor"),
            P("tensor", None),
            P(),
            P(),
            P(),
        ),
        check_vma=False,
    )
```

profile of v0, /device:TPU:0, one launch (start us, length us, event | category | flops | bytes accessed | tf_op | source)
XLA Modules:
  0.0 1137.0 jit_solution(2034057062222812998)
XLA Ops:
  7.2 4.3 convolution_bitcast_fusion.1
  21.9 10.9 fusion.6
  32.9 11.4 %fusion = f32[2,3,1024]{2,1,0:T(4,128)S(1)} fusion(f32[2,3,1024]{2,1,0:T(4,128)S(1)} %get-tuple-element.98, f32[2,3,1024,1024]{2,3,1,0:T(8,128)} %get-tuple-element.99, pred[2,1024]{1,0:T(4,128)(4,1)S(1)} %iota_compare_fusion), kind=kLoop, calls=%fused_computation.6 | loop fusion | flops 25159680 | bytes 25217024 | tf_op jit(solution)/shard_map/reduce_sum | solution.py:64
  44.3 11.6 %fusion.35 = bf16[2,1024,3,64]{1,3,2,0:T(8,128)(2,1)S(1)} fusion(f32[2,3,1024]{2,1,0:T(4,128)S(1)} %fusion, f32[2,3,1024]{2,1,0:T(4,128)S(1)} %get-tuple-element.98, f32[2,3,1024,1024]{2,3,1,0:T(8,128)} %get-tuple-element.99, pred[2,1024]{1,0:T(4,128)(4,1)S(1)} %iota_compare_fusion, f32[2,1024,3,64]{1,0,3,2:T(2,128)S(1)} %copy-done.12, f32[3,64]{1,0:T(4,128)S(1)} %add.137), kind=kOutput, calls=%fused_computation.74 | convolution fusion | flops 837943296 | bytes 27577088 | tf_op jit(solution)/shard_map/bhqk,bkhd->bqhd/dot_general | solution.py:67
  57.8 3.8 fusion.62
  61.7 225.7 %all-reduce.7.cloned.1.call-done = f32[2048,768]{1,0:T(8,128)} async-done(((f32[2048,768]{1,0:T(8,128)}), f32[2048,768]{1,0:T(8,128)}) %all-reduce.7.cloned.1.call-update) | async-done | bytes 6291472 | tf_op jit(solution)/shard_map/psum | solution.py:75
  287.3 4.6 fusion.59
  294.6 18.4 %multiply_convert_fusion.1 = (bf16[2048,768]{1,0:T(8,128)(2,1)S(1)}, f32[2048,768]{1,0:T(8,128)}, f32[2048,768]{1,0:T(8,128)}) fusion(f32[768]{0:T(1024)S(1)} %copy-done.37, bf16[2048,768]{1,0:T(8,128)(2,1)S(1)} %fusion.17, bf16[768,768]{1,0:T(8,128)(2,1)S(1)} %copy-done), kind=kOutput, calls=%fused_computation.32 | convolution fusion | flops 2519728128 | bytes 20057088 | tf_op jit(solution)/shard_map/dot_general | solution.py:81
  314.7 4.4 fusion.63
  319.2 221.9 %all-reduce.9.cloned.1.call-done = f32[2048,768]{1,0:T(8,128)} async-done(((f32[2048,768]{1,0:T(8,128)}), f32[2048,768]{1,0:T(8,128)}) %all-reduce.9.cloned.1.call-update) | async-done | bytes 6291472 | tf_op jit(solution)/shard_map/psum | solution.py:85
  541.1 6.0 fusion.57
  549.0 3.2 fusion.11
  552.3 4.3 fusion.56
  556.6 3.0 copy-done.4
  560.3 5.1 convert_reduce_fusion.2
  567.2 4.5 fusion.64
  572.4 221.2 %all-reduce.11.cloned.1.call-done = f32[2048,768]{1,0:T(8,128)} async-done(((f32[2048,768]{1,0:T(8,128)}), f32[2048,768]{1,0:T(8,128)}) %all-reduce.11.cloned.1.call-update) | async-done | bytes 6291472 | tf_op jit(solution)/shard_map/psum | solution.py:109
  793.7 8.2 multiply_reduce_fusion.1
  801.9 4.2 fusion.55
  811.1 11.9 %fusion.30 = bf16[2,1024,3,64]{1,3,2,0:T(8,128)(2,1)} fusion(f32[2,3,1024]{2,1,0:T(4,128)S(1)} %log_add_fusion, f32[2,3,1024,1024]{2,3,1,0:T(8,128)} %get-tuple-element.99, pred[2,1024]{1,0:T(4,128)(4,1)S(1)} %iota_compare_fusion, bf16[2,1024,3,64]{1,0,3,2:T(2,128)(2,1)S(1)} %reshape.147), kind=kOutput, calls=%fused_computation.71 | convolution fusion | flops 830865408 | bytes 26765312 | tf_op jit(solution)/shard_map/bhqk,bqhd->bkhd/dot_general | solution.py:117
  822.9 19.0 %multiply_reduce_fusion = (f32[2,3,1024]{2,1,0:T(4,128)S(1)}, f32[2,3,1024,1024]{2,3,1,0:T(8,128)}) fusion(f32[2,3,1024]{2,1,0:T(4,128)S(1)} %log_add_fusion, f32[2,3,1024,1024]{2,3,1,0:T(8,128)} %get-tuple-element.99, pred[2,1024]{1,0:T(4,128)(4,1)S(1)} %iota_compare_fusion, f32[2,1024,3,64]{1,0,3,2:T(2,128)S(1)} %copy-done.12, f32[3,64]{1,0:T(4,128)S(1)} %add.137, ...), kind=kOutput, calls=%fused_computation.1 | convolution fusion | flops 837543936 | bytes 52742912 | tf_op jit(solution)/shard_map/bqhd,bkhd->bhqk/dot_general | solution.py:120
  842.0 22.1 %multiply_convert_fusion = bf16[2,3,1024,1024]{2,3,1,0:T(8,128)(2,1)} fusion(f32[2,3,1024,1024]{2,3,1,0:T(8,128)} %get-tuple-element.102, f32[2,3,1024]{2,1,0:T(4,128)S(1)} %get-tuple-element.101, f32[2,3,1024]{2,1,0:T(4,128)S(1)} %log_add_fusion, f32[2,3,1024,1024]{2,3,1,0:T(8,128)} %get-tuple-element.99, pred[2,1024]{1,0:T(4,128)(4,1)S(1)} %iota_compare_fusion), kind=kLoop, calls=%fused_computation | loop fusion | flops 37748736 | bytes 62965760 | tf_op jit(solution)/shard_map/convert_element_type | solution.py:122
  864.1 8.6 fusion.34
  872.7 7.0 fusion.33
  888.1 5.7 convolution_bitcast_fusion
  894.2 7.1 fusion.66
  901.2 4.2 fusion.65
  907.5 3.2 fusion.23
  911.5 25.3 %all-reduce = (f32[2,192]{1,0:T(2,128)}, f32[768]{0:T(1024)}, f32[768]{0:T(1024)}, f32[768]{0:T(1024)}, f32[768]{0:T(1024)}, /*index=5*/f32[768]{0:T(1024)}, f32[768]{0:T(1024)}, f32[768]{0:T(1024)}) all-reduce(f32[2,192]{1,0:T(2,128)S(1)} %pad_maximum_fusion, ...), channel_id=1, replica_groups=mesh['dp'=8,'tensor'=4] {'dp'}, use_global_device_ids=true, to_apply=%region_17.18 | all-reduce | flops 5760 | bytes 46080 | tf_op jit(solution)/shard_map/psum | solution.py:158
  936.8 66.9 %reduce-scatter.4.cloned.1.call-done = f32[192,2048]{1,0:T(8,128)} async-done(((f32[768,2048]{1,0:T(8,128)}), f32[192,2048]{1,0:T(8,128)}) %reduce-scatter.4.cloned.1.call-update) | async-done | bytes 1572880
  1005.5 3.9 dynamic-slice_add_fusion
  1012.1 110.3 %all-reduce.13.cloned.1.call-done = (f32[3,768,192]{1,2,0:T(8,128)}, f32[192,768]{1,0:T(8,128)}, f32[768,768]{1,0:T(8,128)}, f32[768,768]{1,0:T(8,128)}) async-done(((f32[3,768,192]{1,2,0:T(8,128)}, f32[192,768]{1,0:T(8,128)}, f32[768,768]{1,0:T(8,128)}, f32[768,768]{1,0:T(8,128)}), (f32[3,768,192]{1,2,0:T(8,128)}, f32[192,768]{1,0:T(8,128)}, f32[768,768]{1,0:T(8,128)}, ...) | async-done | bytes 7077904 | tf_op jit(solution)/shard_map/psum | solution.py:158
  (152 shorter events, 50.5 us)
Async XLA Ops:
  7.2 287.5 %copy-start = (bf16[768,768]{1,0:T(8,128)(2,1)S(1)}, bf16[768,768]{1,0:T(8,128)(2,1)}, u32[]{:S(2)}) copy-start(bf16[768,768]{1,0:T(8,128)(2,1)} %param.24) | copy-start | bytes 3538948
  7.2 280.1 %all-reduce.7.cloned.1.call-start = ((), (), s32[]{:S(2)}) async-start(), calls=%async_computation.1 | async-start | bytes 12582912 | tf_op jit(solution)/shard_map/psum | solution.py:75
  14.1 18.7 %copy-start.24 = (f32[3,64]{1,0:T(4,128)}, f32[3,64]{1,0:T(4,128)S(1)}, u32[]{:S(2)}) copy-start(f32[3,64]{1,0:T(4,128)S(1)} %add.140) | copy-start | bytes 2308
  16.8 16.0 %copy-start.10 = (bf16[2,1024,3,64]{1,0,3,2:T(2,128)(2,1)}, bf16[2,1024,3,64]{1,0,3,2:T(2,128)(2,1)S(1)}, u32[]{:S(2)}) copy-start(bf16[2,1024,3,64]{1,0,3,2:T(2,128)(2,1)S(1)} %convert_element_type.71) | copy-start | bytes 2359300
  21.9 10.9 copy-start.5
  32.8 11.5 %copy-start.21 = (f32[2,3,1024]{2,1,0:T(4,128)}, f32[2,3,1024]{2,1,0:T(4,128)S(1)}, u32[]{:S(2)}) copy-start(f32[2,3,1024]{2,1,0:T(4,128)S(1)} %get-tuple-element.98) | copy-start | bytes 73732
  32.9 11.5 %copy-start.12 = (f32[2,1024,3,64]{1,0,3,2:T(2,128)S(1)}, f32[2,1024,3,64]{1,0,3,2:T(2,128)}, u32[]{:S(2)}) copy-start(f32[2,1024,3,64]{1,0,3,2:T(2,128)} %squeeze.7) | copy-start | bytes 4718596
  44.3 13.5 %copy-start.19 = (bf16[192,768]{1,0:T(8,128)(2,1)S(1)}, bf16[192,768]{1,0:T(8,128)(2,1)}, u32[]{:S(2)}) copy-start(bf16[192,768]{1,0:T(8,128)(2,1)} %param.20) | copy-start | bytes 884740
  57.8 229.5 %copy-start.31 = (f32[768]{0:T(1024)S(1)}, f32[768]{0:T(1024)}, u32[]{:S(2)}) copy-start(f32[768]{0:T(1024)} %param.21) | copy-start | bytes 9220
  61.6 479.5 %all-reduce.9.cloned.1.call-start = ((), (), s32[]{:S(2)}) async-start(), calls=%async_computation.2 | async-start | bytes 12582912 | tf_op jit(solution)/shard_map/psum | solution.py:85
  294.6 18.4 %copy-start.14 = (bf16[2048,768]{1,0:T(8,128)(2,1)}, bf16[2048,768]{1,0:T(8,128)(2,1)S(1)}, u32[]{:S(2)}) copy-start(bf16[2048,768]{1,0:T(8,128)(2,1)S(1)} %fusion.17) | copy-start | bytes 9437188
  294.6 20.0 %copy-start.35 = (bf16[768,768]{1,0:T(8,128)(2,1)S(1)}, bf16[768,768]{1,0:T(8,128)(2,1)}, u32[]{:S(2)}) copy-start(bf16[768,768]{1,0:T(8,128)(2,1)} %param.26) | copy-start | bytes 3538948
  319.1 222.0 %copy-start.32 = (f32[768]{0:T(1024)S(1)}, f32[768]{0:T(1024)}, u32[]{:S(2)}) copy-start(f32[768]{0:T(1024)} %param.27) | copy-start | bytes 9220
  319.1 474.6 %all-reduce.11.cloned.1.call-start = ((), (), s32[]{:S(2)}) async-start(), calls=%async_computation.3 | async-start | bytes 12582912 | tf_op jit(solution)/shard_map/psum | solution.py:109
  548.0 4.2 copy-start.29
  552.2 8.0 slice-start.2
  552.2 8.0 slice-start.4
  552.2 8.0 slice-start.3
  552.3 8.0 slice-start.5
  560.2 5.2 copy-start.13
  571.7 432.0 %reduce-scatter.4.cloned.1.call-start = ((), (), s32[]{:S(2)}) async-start(), calls=%async_computation.4 | async-start | bytes 7864320
  841.9 22.1 %copy-start.6 = (f32[2,1024,3,64]{1,0,3,2:T(2,128)S(1)}, f32[2,1024,3,64]{1,0,3,2:T(2,128)}, u32[]{:S(2)}) copy-start(f32[2,1024,3,64]{1,0,3,2:T(2,128)} %copy-done.5) | copy-start | bytes 4718596
  842.0 22.1 %copy-start.25 = (f32[3,64]{1,0:T(4,128)S(1)}, f32[3,64]{1,0:T(4,128)}, u32[]{:S(2)}) copy-start(f32[3,64]{1,0:T(4,128)} %copy-done.24) | copy-start | bytes 2308
  864.0 8.6 copy-start.11
  872.7 7.0 copy-start.20
  893.8 228.6 %all-reduce.13.cloned.1.call-start = ((), (), s32[]{:S(2)}) async-start(), calls=%async_computation.5 | async-start | bytes 14155776 | tf_op jit(solution)/shard_map/psum | solution.py:158
  894.1 7.1 copy-start.15
  894.1 7.1 copy-start.40
  894.2 11.3 slice-start
  1122.4 4.9 copy-start.18
  1122.4 6.3 copy-start.17
  1122.4 7.7 copy-start.1
  (20 other events, 41.4 us)
Sparse Core Ops, SparseCore 0:
  61.7 225.5 all-reduce.6
  319.2 221.7 all-reduce.8
  571.8 221.8 all-reduce.10
  894.0 109.6 reduce-scatter.3
  1008.3 113.9 all-reduce.12
where the time goes:
time: 1150 us; the launch traced here: 1140 us
  waiting for transfers between devices  846 us (74%)
  matrix products  132 us (11%)
  other arithmetic  72.5 us (6%)
  local copies, waits for them, and re-layouts  45.6 us (4%)
  blocking collectives  25.3 us (2%)
  between operations  14.9 us (1%)
    psum x1, waiting for transfers between devices, on_device(): lax.psum(jnp.dot(mixed, out_weight, preferred_element_type=jnp.float32),...  226 us
    psum x1, waiting for transfers between devices, on_device(): lax.psum(jnp.dot(active, down_weight, preferred_element_type=jnp.float32)...  222 us
    psum x1, waiting for transfers between devices, on_device(): d_normed = lax.psum(d_part, 'tensor') + d_second  221 us
    psum x1, waiting for transfers between devices, on_device(): summed = lax.psum(attn_grads + mlp_grads, 'dp')  110 us
    unnamed x6, waiting for transfers between devices  66.9 us
    unnamed x103, local copies, waits for them, and re-layouts  27.9 us
    psum x1, blocking collectives, on_device(): summed = lax.psum(attn_grads + mlp_grads, 'dp')  25.3 us
  transfers between devices with their start and end apart: 5, of which 5 were waited for; matrix products, arithmetic and copies ran while one was open for 2% of the time, Pallas kernels for 0%

commit v1 on v0

v1 whole, which is shorter than its diff:
```python
import jax
import jax.numpy as jnp
from jax import lax
from jax.experimental import pallas as pl
from jax.experimental.pallas import tpu as pltpu
from jax.sharding import PartitionSpec as P

HD = 64
EPS = 1e-05
MASKED = -1000000000.0
BITS = 3
INNER = 1 << BITS
F32 = jnp.float32
BF16 = jnp.bfloat16


def layer_norm(hidden, gain, shift):
    center = hidden - jnp.mean(hidden, -1, keepdims=True)
    spread = jnp.mean(center * center, -1, keepdims=True)
    return center * lax.rsqrt(spread + EPS) * gain + shift


def exact_gelu(inputs):
    return jax.nn.gelu(inputs, approximate=False)


def nn(left, right):
    return lax.dot_general(left, right, (((1,), (0,)), ((), ())), preferred_element_type=F32)


def nt(left, right):
    return lax.dot_general(left, right, (((1,), (1,)), ((), ())), preferred_element_type=F32)


def tn(left, right):
    return lax.dot_general(left, right, (((0,), (0,)), ((), ())), preferred_element_type=F32)


def flip(x, bit):
    size = lax.axis_size("dp")
    return lax.ppermute(x, "dp", [(i, i ^ (1 << bit)) for i in range(size)])


def from_next(x, step):
    size = lax.axis_size("tensor")
    return lax.ppermute(x, "tensor", [((i + step) % size, i) for i in range(size)])


def to_next(x, step):
    size = lax.axis_size("tensor")
    return lax.ppermute(x, "tensor", [(i, (i + step) % size) for i in range(size)])


ORDERS = ((1, 2), (2, 1))


def unit(lengths):
    return jnp.where(lengths[0] > 0, 1.0, 0.0).astype(F32)


def gather_pieces(piece):
    piece = lax.optimization_barrier(piece)
    places = [piece] + [from_next(piece, step) for step in (1, 2, 3)]
    halves = []
    for half, order in enumerate(ORDERS):
        held = jnp.concatenate(places[2 * half : 2 * half + 2], 0)
        for bit in order:
            held = jnp.concatenate([held, flip(held, bit)], 0)
        halves.append(lax.optimization_barrier((held, flip(held, 0))))
    return halves


def scatter_sums(halves):
    places = []
    for (own, other), order in zip(halves, ORDERS):
        held = own + flip(other, 0)
        for bit in reversed(order):
            count = held.shape[0] // 2
            held = held[:count] + flip(held[count:], bit)
        count = held.shape[0] // 2
        places += [held[:count], held[count:]]
    total = places[0]
    for step in (1, 2, 3):
        total = total + to_next(places[step], step)
    bit = BITS
    while (1 << bit) < lax.axis_size("dp"):
        total = total + flip(total, bit)
        bit += 1
    return total


def gather_in_order(piece, order):
    held = piece[None]
    for bit in (*order, 0):
        held = jnp.concatenate([held, flip(held, bit)], 0)
    me = lax.axis_index("dp") % INNER
    blocks = []
    for index in range(INNER):
        apart = me ^ index
        place = sum(((apart >> bit) & 1) << at for at, bit in enumerate((*order, 0)))
        blocks.append(lax.dynamic_index_in_dim(held, place, 0))
    return jnp.concatenate(blocks, 0)


def sum_everywhere(x):
    for axis in ("dp", "tensor"):
        size = lax.axis_size(axis)
        step = 1
        while step < size:
            x = x + lax.ppermute(x, axis, [(i, i ^ step) for i in range(size)])
            step *= 2
    return x


CHUNK = 256


def lane_masks(width):
    lane = lax.broadcasted_iota(jnp.int32, (1, width), 1)
    return [lane < HD, lane >= HD]


def keep(mask, x):
    return jnp.where(mask, x, jnp.zeros_like(x))


def forward_kernel(length_ref, q_ref, k_ref, v_ref, mixed_ref, lse_ref):
    keys = k_ref.shape[0]
    queries = q_ref.shape[0]
    valid = lax.broadcasted_iota(jnp.int32, (keys, 1), 0) < length_ref[0]
    masks = lane_masks(q_ref.shape[1])
    turned = v_ref[...].T
    for start in range(0, queries, CHUNK):
        rows = pl.ds(start, CHUNK)
        parts = []
        for head in range(2):
            scores = nt(k_ref[...], keep(masks[head], q_ref[rows, :]))
            scores = jnp.where(valid, scores, MASKED)
            highest = jnp.max(scores, 0, keepdims=True)
            expo = jnp.exp(scores - highest)
            totals = jnp.sum(expo, 0, keepdims=True)
            probs = (expo * (1.0 / totals)).astype(BF16)
            parts.append(nn(turned[head * HD : (head + 1) * HD, :], probs))
            lse_ref[0, head : head + 1, rows] = highest + jnp.log(totals)
        mixed_ref[rows, :] = jnp.concatenate(parts, 0).T.astype(BF16)


def backward_kernel(length_ref, q_ref, k_ref, v_ref, dm_ref, lse_ref, dq_ref, dk_ref, dv_ref, dk_sum, dv_sum):
    keys = k_ref.shape[0]
    queries = q_ref.shape[0]
    valid = lax.broadcasted_iota(jnp.int32, (keys, 1), 0) < length_ref[0]
    masks = lane_masks(q_ref.shape[1])
    turned = k_ref[...].T
    for start in range(0, queries, CHUNK):
        rows = pl.ds(start, CHUNK)
        parts = []
        for head in range(2):
            query = keep(masks[head], q_ref[rows, :])
            d_mixed = keep(masks[head], dm_ref[rows, :])
            scores = jnp.where(valid, nt(k_ref[...], query), MASKED)
            probs = jnp.exp(scores - lse_ref[0, head : head + 1, rows])
            d_values = nn(probs.astype(BF16), d_mixed)
            d_probs = nt(v_ref[...], d_mixed)
            row_dot = jnp.sum(d_probs * probs, 0, keepdims=True)
            d_scores = (probs * (d_probs - row_dot)).astype(BF16)
            d_keys = nn(d_scores, query)
            parts.append(nn(turned[head * HD : (head + 1) * HD, :], d_scores))
            if start == 0 and head == 0:
                dk_sum[...] = d_keys
                dv_sum[...] = d_values
            else:
                dk_sum[...] += d_keys
                dv_sum[...] += d_values
        dq_ref[rows, :] = (jnp.concatenate(parts, 0).T * HD ** (-0.5)).astype(BF16)
    dk_ref[...] = dk_sum[...].astype(BF16)
    dv_ref[...] = dv_sum[...].astype(BF16)


def attention_forward(length, queries, keys, values):
    count, width = queries.shape
    pairs = width // (2 * HD)
    columns = lambda rows: pl.BlockSpec((rows, 2 * HD), lambda j: (0, j))
    work = count * keys.shape[0] * width
    return pl.pallas_call(
        forward_kernel,
        grid=(pairs,),
        in_specs=[
            pl.BlockSpec(memory_space=pltpu.SMEM),
            columns(count),
            columns(keys.shape[0]),
            columns(keys.shape[0]),
        ],
        out_specs=[columns(count), pl.BlockSpec((1, 2, count), lambda j: (j, 0, 0))],
        out_shape=[
            jax.ShapeDtypeStruct((count, width), BF16),
            jax.ShapeDtypeStruct((pairs, 2, count), F32),
        ],
        compiler_params=pltpu.CompilerParams(vmem_limit_bytes=48 * 2**20),
        cost_estimate=pl.CostEstimate(flops=8 * work, bytes_accessed=4 * 2**20, transcendentals=work // HD),
    )(length, queries, keys, values)


def attention_backward(length, queries, keys, values, d_mixed, lse):
    count, width = queries.shape
    pairs = width // (2 * HD)
    long = keys.shape[0]
    columns = lambda rows: pl.BlockSpec((rows, 2 * HD), lambda j: (0, j))
    work = count * long * width
    return pl.pallas_call(
        backward_kernel,
        grid=(pairs,),
        in_specs=[
            pl.BlockSpec(memory_space=pltpu.SMEM),
            columns(count),
            columns(long),
            columns(long),
            columns(count),
            pl.BlockSpec((1, 2, count), lambda j: (j, 0, 0)),
        ],
        out_specs=[columns(count), columns(long), columns(long)],
        out_shape=[
            jax.ShapeDtypeStruct((count, width), BF16),
            jax.ShapeDtypeStruct((long, width), BF16),
            jax.ShapeDtypeStruct((long, width), BF16),
        ],
        scratch_shapes=[pltpu.VMEM((long, 2 * HD), F32)] * 2,
        compiler_params=pltpu.CompilerParams(vmem_limit_bytes=48 * 2**20),
        cost_estimate=pl.CostEstimate(flops=20 * work, bytes_accessed=8 * 2**20, transcendentals=work // HD),
    )(length, queries, keys, values, d_mixed, lse)


def share_input_grads(part):
    seq, width = part.shape
    piece = width // 4
    place = lax.axis_index("tensor")
    flipped = place >= 2
    quarters = [part[:, i * piece : (i + 1) * piece] for i in range(4)]
    near = [jnp.where(flipped, quarters[3 - i], quarters[i]) for i in range(4)]
    outer = (place == 0) | (place == 3)
    swap = [(0, 1), (1, 0), (2, 3), (3, 2)]
    inward = [(0, 1), (3, 2)]
    across = [(1, 2), (2, 1)]
    outward = [(2, 3), (1, 0)]
    first = lax.ppermute(jnp.where(outer, near[3], near[0]), "tensor", swap)
    far = lax.ppermute(near[3] + first, "tensor", across)
    second = lax.ppermute(near[2], "tensor", inward)
    third = lax.ppermute(near[1], "tensor", inward)
    middle = lax.ppermute(near[2] + second, "tensor", across)
    last = lax.ppermute(far, "tensor", outward)
    mine = jnp.where(outer, near[0] + first, near[1] + third)
    theirs = jnp.where(outer, last, middle)
    return jnp.concatenate([jnp.where(flipped, theirs, mine), jnp.where(flipped, mine, theirs)], 0)


def head_rows(array, heads):
    cols = array.shape[1]
    return array.reshape(heads, INNER, HD // INNER, cols).transpose(1, 0, 2, 3)


def on_device(
    tokens,
    lengths,
    cotangent,
    qkv_weight,
    qv_bias,
    out_weight,
    out_bias,
    first_gain,
    first_shift,
    up_weight,
    up_bias,
    down_weight,
    down_bias,
    second_gain,
    second_shift,
):
    rows, width = tokens.shape
    seq = rows // lengths.shape[0]
    columns = qkv_weight.shape[2]
    heads = columns // HD
    units = up_weight.shape[1]
    share = rows // 4
    sub = HD // INNER
    place = lax.axis_index("tensor")
    me = lax.axis_index("dp") % INNER
    one = unit(lengths)

    turned = jnp.concatenate([qkv_weight.transpose(0, 2, 1), out_weight[None]], 0)
    turned = turned.reshape(4, heads, INNER, sub, width)
    attn_piece = lax.dynamic_index_in_dim(turned, me, 2, keepdims=False).reshape(-1, width).astype(F32) * one
    count = units // INNER
    up_piece = lax.dynamic_slice_in_dim(up_weight.T, me * count, count, 0).astype(F32) * one
    down_piece = lax.dynamic_slice_in_dim(down_weight, me * count, count, 0).astype(F32) * one
    qv_piece = lax.dynamic_index_in_dim(qv_bias.reshape(2 * heads, INNER, sub), me, 1, keepdims=False)
    bias_piece = jnp.zeros((8, 128), F32)
    bias_piece = bias_piece.at[0, :count].set(lax.dynamic_slice_in_dim(up_bias, me * count, count, 0))
    bias_piece = bias_piece.at[1, : 2 * heads * sub].set(qv_piece.reshape(-1))

    bias_halves = gather_pieces(bias_piece)
    attn_halves = gather_pieces(attn_piece)
    up_halves = gather_pieces(up_piece)
    down_halves = gather_pieces(down_piece)

    def heads_together(own, other, kinds, trail):
        both = jnp.stack([own, other]).reshape((2, 2, 2, 2, kinds, heads, sub) + trail)
        both = both.transpose((4, 3, 5, 0, 1, 2, 6) + tuple(range(7, 7 + len(trail))))
        return both.reshape((kinds, 2 * heads * HD) + trail)

    def heads_apart(array, kinds, trail):
        both = array.reshape((kinds, 2, 2, heads, 2, 2, 2, sub) + trail)
        both = both.transpose((1, 4, 5, 6, 2, 0, 3, 7) + tuple(range(8, 8 + len(trail))))
        flat = both.reshape((2, 2, 4 * 2 * kinds * heads * sub) + trail)
        return [(flat[half, 0], flat[half, 1]) for half in range(2)]

    attn_full = jnp.concatenate(
        [(heads_together(own, other, 4, (width,)) * one).astype(BF16) for own, other in attn_halves], 1
    )
    q_rows, k_rows, v_rows, out_rows = attn_full
    qv_full = jnp.concatenate(
        [
            heads_together(
                own.reshape(8, 8, 128)[:, 1, : 2 * heads * sub],
                other.reshape(8, 8, 128)[:, 1, : 2 * heads * sub],
                2,
                (),
            )
            for own, other in bias_halves
        ],
        1,
    )
    up_bias_full = jnp.concatenate(
        [part.reshape(8, 8, 128)[:, 0, :count].reshape(-1) for pair in bias_halves for part in pair]
    )
    up_full = jnp.concatenate([part for pair in up_halves for part in pair], 0) * one
    down_full = jnp.concatenate([part for pair in down_halves for part in pair], 0) * one

    up_full = up_full.astype(BF16)
    down_full = down_full.astype(BF16)

    which = place // 2
    length = lax.dynamic_slice_in_dim(lengths, which, 1, 0)
    seq_tokens = lax.dynamic_slice_in_dim(tokens, which * seq, seq, 0)
    own_tokens = lax.dynamic_slice_in_dim(tokens, place * share, share, 0)
    own_cotangent = lax.dynamic_slice_in_dim(cotangent, place * share, share, 0)
    queries = (nt(own_tokens, q_rows) + qv_full[0]).astype(BF16) * jnp.asarray(HD ** (-0.5), BF16)
    keys = nt(seq_tokens, k_rows).astype(BF16)
    values = (nt(seq_tokens, v_rows) + qv_full[1]).astype(BF16)
    mixed, lse = attention_forward(length, queries, keys, values)
    attended = nn(mixed, out_rows) + out_bias
    first = own_tokens.astype(F32) + attended
    normed, first_back = jax.vjp(layer_norm, first, first_gain, first_shift)
    normed_low = normed.astype(BF16)
    hidden = nt(normed_low, up_full) + up_bias_full
    active_full, gelu_back = jax.vjp(exact_gelu, hidden)
    active = active_full.astype(BF16)
    second = normed + (nn(active, down_full) + down_bias)
    result, second_back = jax.vjp(layer_norm, second, second_gain, second_shift)
    output = (lax.all_gather(result, "tensor", axis=0, tiled=True) * one).astype(BF16)

    d_second, grad_second_gain, grad_second_shift = second_back(own_cotangent.astype(F32))
    d_branch = d_second.astype(BF16)
    grad_down_bias = jnp.sum(d_branch.astype(F32), 0)
    d_active = nt(d_branch, down_full)
    d_hidden = gelu_back(d_active)[0].astype(BF16)

    def unit_grads(left, right):
        parts = [tn(left[:, i * units : (i + 1) * units], right) for i in range(4)]
        return [(parts[0], parts[1]), (parts[2], parts[3])]

    down_sums = scatter_sums(unit_grads(active, d_branch))
    up_sums = scatter_sums(unit_grads(d_hidden, normed_low))
    grad_up_bias = jnp.sum(d_hidden.astype(F32), 0)
    d_normed = nn(d_hidden, up_full) + d_second
    d_first, grad_first_gain, grad_first_shift = first_back(d_normed)
    d_attended = d_first.astype(BF16)
    grad_out_rows = tn(mixed, d_attended)
    grad_out_bias = jnp.sum(d_attended.astype(F32), 0)
    d_mixed = nt(d_attended, out_rows).astype(BF16)
    d_queries, d_keys, d_values = attention_backward(length, queries, keys, values, d_mixed, lse)

    input_part = nn(d_keys, k_rows) + nn(d_values, v_rows)
    own_part = nn(d_queries, q_rows) + d_first
    offset = (place % 2) * share
    input_part = lax.dynamic_update_slice_in_dim(
        input_part, lax.dynamic_slice_in_dim(input_part, offset, share, 0) + own_part, offset, 0
    )
    grad_tokens = share_input_grads(input_part)

    attn_grads = jnp.stack(
        [tn(d_queries, own_tokens), tn(d_keys, seq_tokens), tn(d_values, seq_tokens), grad_out_rows]
    )
    attn_sums = scatter_sums(heads_apart(attn_grads, 4, (width,)))
    qv_sums = heads_apart(
        jnp.stack([jnp.sum(d_queries.astype(F32), 0), jnp.sum(d_values.astype(F32), 0)]), 2, ()
    )
    up_bias_parts = grad_up_bias.reshape(2, 2, 8, count)
    bias_parts = []
    for half in range(2):
        pair = []
        for core in range(2):
            block = jnp.zeros((8, 8, 128), F32)
            block = block.at[:, 0, :count].set(up_bias_parts[half, core])
            block = block.at[:, 1, : 2 * heads * sub].set(qv_sums[half][core].reshape(8, -1))
            pair.append(block.reshape(64, 128))
        bias_parts.append(tuple(pair))
    bias_sums = scatter_sums(bias_parts)

    bias_all = gather_in_order(bias_sums, (1, 2))
    down_all = gather_in_order(down_sums, (1, 2))
    up_all = gather_in_order(up_sums, (2, 1))
    attn_all = gather_in_order(attn_sums, (1, 2))
    attn_all = attn_all.reshape(INNER, 4, heads, sub, width).transpose(1, 2, 0, 3, 4)
    attn_all = attn_all.reshape(4, columns, width)
    qv_all = bias_all[:, 1, : 2 * heads * sub].reshape(INNER, 2, heads, sub)
    small = sum_everywhere(
        jnp.stack(
            [
                grad_out_bias,
                grad_first_gain,
                grad_first_shift,
                grad_down_bias,
                grad_second_gain,
                grad_second_shift,
            ]
        )
    )
    return (
        output,
        grad_tokens,
        attn_all[:3].transpose(0, 2, 1),
        qv_all.transpose(1, 2, 0, 3).reshape(2, columns),
        attn_all[3],
        small[0],
        small[1],
        small[2],
        up_all.reshape(units, width).T,
        bias_all[:, 0, :count].reshape(-1),
        down_all.reshape(units, width),
        small[3],
        small[4],
        small[5],
    )


def solution(mesh):
    placed = (
        P("dp", None),
        P("dp"),
        P("dp", None),
        P(None, None, "tensor"),
        P(None, "tensor"),
        P("tensor", None),
        P(),
        P(),
        P(),
        P(None, "tensor"),
        P("tensor"),
        P("tensor", None),
        P(),
        P(),
        P(),
    )
    return jax.shard_map(
        on_device,
        mesh=mesh,
        in_specs=placed,
        out_specs=(
            P("dp", None),
            P("dp", "tensor"),
            P(None, None, "tensor"),
            P(None, "tensor"),
            P("tensor", None),
            P(),
            P(),
            P(),
            P(None, "tensor"),
            P("tensor"),
            P("tensor", None),
            P(),
            P(),
            P(),
        ),
        check_vma=False,
    )
```

time: 1150 us -> 729 us (0.63)
  the two profiles are of different devices: /device:TPU:0 before, /device:TPU:25 now
where the time goes in v1:
time: 729 us; the launch traced here: 722 us
  waiting for transfers between devices  243 us (33%)
  starting transfers between devices  197 us (27%)
  matrix products  98.6 us (14%)
  local copies, waits for them, and re-layouts  68.1 us (9%)
  Pallas kernels  49.9 us (7%)
  other arithmetic  47.7 us (7%)
  between operations  17.3 us (2%)
    ppermute x60, waiting for transfers between devices, flip(): return lax.ppermute(x, 'dp', [(i, i ^ 1 << bit) for i in range(size)])  174 us
    ppermute x60, starting transfers between devices, flip(): return lax.ppermute(x, 'dp', [(i, i ^ 1 << bit) for i in range(size)])  98 us
    ppermute x12, waiting for transfers between devices, to_next(): lax.ppermute(x, 'tensor', [(i, (i + step) % size) for i in range(size)])  49.9 us
    ppermute x12, starting transfers between devices, to_next(): lax.ppermute(x, 'tensor', [(i, (i + step) % size) for i in range(size)])  41.7 us
    dot_general x6, matrix products, nt(): lax.dot_general(left, right, (((1,), (1,)), ((), ())), preferred_element_...  39.7 us
    ppermute x12, starting transfers between devices, from_next(): lax.ppermute(x, 'tensor', [((i + step) % size, i) for i in range(size)])  38.9 us
    dot_general x12, matrix products, tn(): lax.dot_general(left, right, (((0,), (0,)), ((), ())), preferred_element_...  34.8 us
    unnamed x174, local copies, waits for them, and re-layouts  33.1 us
  transfers between devices with their start and end apart: 96, of which 29 were waited for; matrix products, arithmetic and copies ran while one was open for 15% of the time, Pallas kernels for 0%

profile of v1, /device:TPU:25, one launch (start us, length us, event | category | flops | bytes accessed | tf_op | source)
XLA Modules:
  0.0 722.1 jit_solution(11931357468260909568)
XLA Ops:
  22.5 10.6 %collective-permute-done.22 = f32[96,768]{1,0:T(8,128)} collective-permute-done((f32[96,768]{1,0:T(8,128)S(1)}, f32[96,768]{1,0:T(8,128)}, u32[]{:S(2)}, u32[]{:S(2)}) %collective-permute-start.22) | collective-permute-done | bytes 294944 | tf_op jit(solution)/shard_map/ppermute | solution.py:46
  36.5 15.8 %collective-permute-start.27 = (f32[96,768]{1,0:T(8,128)S(1)}, f32[96,768]{1,0:T(8,128)S(1)}, u32[]{:S(2)}, u32[]{:S(2)}) collective-permute-start(f32[96,768]{1,0:T(8,128)S(1)} %convert_multiply_fusion.2), channel_id=1, source_target_pairs={{1,0},{2,1},{3,2},{0,3},{5,4},{6,5},{7,6},{4,7},{9,8},{10,9},{11,1... | collective-permute-start | bytes 884744 | tf_op jit(solution)/shard_map/ppermute | solution.py:46
  57.6 6.4 collective-permute-start.18
  74.8 6.8 collective-permute-done.33
  82.9 7.0 collective-permute-start
  100.4 32.3 %collective-permute-done.19 = f32[192,768]{1,0:T(8,128)S(1)} collective-permute-done((f32[192,768]{1,0:T(8,128)S(1)}, f32[192,768]{1,0:T(8,128)S(1)}, u32[]{:S(2)}, u32[]{:S(2)}) %collective-permute-start.19) | collective-permute-done | bytes 589856 | tf_op jit(solution)/shard_map/ppermute | solution.py:41
  134.4 10.9 %collective-permute-done.1 = f32[192,768]{1,0:T(8,128)S(1)} collective-permute-done((f32[192,768]{1,0:T(8,128)S(1)}, f32[192,768]{1,0:T(8,128)S(1)}, u32[]{:S(2)}, u32[]{:S(2)}) %collective-permute-start.1) | collective-permute-done | bytes 589856 | tf_op jit(solution)/shard_map/ppermute | solution.py:41
  152.8 16.2 %collective-permute-start.17 = (f32[64,128]{1,0:T(8,128)S(1)}, f32[64,128]{1,0:T(8,128)S(1)}, u32[]{:S(2)}, u32[]{:S(2)}) collective-permute-start(f32[64,128]{1,0:T(8,128)S(1)} %constant_dynamic-update-slice_fusion.4), channel_id=1, source_target_pairs={{0,4},{4,0},{8,12},{12,8},{16,20},{20,16},{24,28},{28,24},{1,5},{5... | collective-permute-start | bytes 98312 | tf_op jit(solution)/shard_map/ppermute | solution.py:41
  170.6 7.5 %collective-permute-done.20 = f32[384,768]{1,0:T(8,128)S(1)} collective-permute-done((f32[384,768]{1,0:T(8,128)S(1)}, f32[384,768]{1,0:T(8,128)S(1)}, u32[]{:S(2)}, u32[]{:S(2)}) %collective-permute-start.20) | collective-permute-done | bytes 1179680 | tf_op jit(solution)/shard_map/ppermute | solution.py:41
  178.1 16.2 %collective-permute-start.12 = (f32[64,128]{1,0:T(8,128)S(1)}, f32[64,128]{1,0:T(8,128)S(1)}, u32[]{:S(2)}, u32[]{:S(2)}) collective-permute-start(f32[64,128]{1,0:T(8,128)S(1)} %pad_maximum_fusion.27), channel_id=1, source_target_pairs={{0,4},{4,0},{8,12},{12,8},{16,20},{20,16},{24,28},{28,24},{1,5},{5... | collective-permute-start | bytes 98312 | tf_op jit(solution)/shard_map/ppermute | solution.py:41
  203.4 8.3 %collective-permute-start.30 = (f32[768,768]{1,0:T(8,128)}, f32[768,768]{1,0:T(8,128)}, u32[]{:S(2)}, u32[]{:S(2)}) collective-permute-start(f32[768,768]{1,0:T(8,128)} %pad_maximum_fusion.3), channel_id=1, source_target_pairs={{0,4},{4,0},{8,12},{12,8},{16,20},{20,16},{24,28},{28,24},{1,5},{5... | collective-permute-start | bytes 7077896 | tf_op jit(solution)/shard_map/ppermute | solution.py:41
  235.6 23.3 %shard_map.254 = (bf16[512,768]{1,0:T(8,128)(2,1)S(1)}, f32[6,2,512]{2,1,0:T(2,128)S(1)}) custom-call(s32[1]{0:T(128)} %get-tuple-element.299.length_ref, bf16[512,768]{1,0:T(8,128)(2,1)S(1)} %fusion.18.q_ref, bf16[1024,768]{1,0:T(8,128)(2,1)S(1)} %convolution_convert_fusion.k_ref, bf16[1024,768]{1,0:T(8,128)(2,1)S(1)} %add_convert_fusion.1.v_ref), custom_call_target="tpu_custom_call" | custom-call | flops 3221225472 | bytes 4194304 | tf_op jit(solution)/shard_map/pallas_call | solution.py:184
  262.3 22.9 %multiply_convert_fusion.1 = (bf16[512,3072]{1,0:T(8,128)(2,1)S(1)}, f32[512,3072]{1,0:T(8,128)}, f32[512,3072]{1,0:T(8,128)}) fusion(f32[3072]{0:T(1024)S(1)} %pad_maximum_fusion.32, bf16[512,768]{0,1:T(8,128)(2,1)S(1)} %fusion.19, f32[768,768]{1,0:T(8,128)S(1)} %copy-done.58, f32[768,768]{1,0:T(8,128)S(1)} %copy-done.51, ...), kind=kOutput, calls=%fused_computation.10 | convolution fusion | flops 2531524608 | bytes 25964548 | tf_op jit(solution)/shard_map/dot_general | solution.py:32
  285.2 6.6 fusion.91
  295.5 12.4 %convert_reduce_fusion = (f32[3072]{0:T(1024)S(1)}, bf16[512,3072]{1,0:T(8,128)(2,1)}) fusion(f32[512,3072]{1,0:T(8,128)} %get-tuple-element.275, bf16[512,768]{0,1:T(8,128)(2,1)} %get-tuple-element.267, f32[768,768]{1,0:T(8,128)} %collective-permute-done.35, f32[768,768]{1,0:T(8,128)} %constant_dynamic-update-slice_fusion.14, ...), kind=kOutput, calls=%fused_computation.7 | convolution fusion | flops 2454451200 | bytes 25976836 | tf_op jit(solution)/shard_map/dot_general | solution.py:32
  307.9 8.0 %multiply_reduce_fusion = (f32[768]{0:T(1024)S(1)}, f32[512]{0:T(512)S(1)}, f32[768]{0:T(1024)S(1)}, f32[512,768]{0,1:T(8,128)S(1)}) fusion(f32[512,768]{0,1:T(8,128)} %copy-done.27, f32[512]{0:T(512)S(1)} %fusion.64, f32[512]{0:T(512)S(1)} %broadcast_multiply_fusion.1, f32[768]{0:T(1024)S(1)} %copy-done.53, f32[512]{0:T(512)S(1)} %negate_multiply_fusion.2, ...), kind=kOutput, calls=%fused_computation.67 | convolution fusion | flops 2434398208 | bytes 18114564 | tf_op jit(solution)/shard_map/dot_general | solution.py:28
  319.1 26.6 %shard_map.255 = (bf16[512,768]{1,0:T(8,128)(2,1)S(1)}, bf16[1024,768]{1,0:T(8,128)(2,1)S(1)}, bf16[1024,768]{1,0:T(8,128)(2,1)S(1)}) custom-call(s32[1]{0:T(128)} %get-tuple-element.299.length_ref, bf16[512,768]{1,0:T(8,128)(2,1)S(1)} %copy-done.5, bf16[1024,768]{1,0:T(8,128)(2,1)} %copy-done.8, bf16[1024,768]{1,0:T(8,128)(2,1)} %copy-done.9, ...), custom_call_target="tpu_custom_call" | custom-call | flops 8053063680 | bytes 8388608 | tf_op jit(solution)/shard_map/pallas_call | solution.py:209
  378.6 10.6 %collective-permute-start.57 = (f32[8,128]{1,0:T(8,128)S(1)}, f32[8,128]{1,0:T(8,128)S(1)}, u32[]{:S(2)}, u32[]{:S(2)}) collective-permute-start(f32[8,128]{1,0:T(8,128)S(1)} %slice.643), channel_id=1, source_target_pairs={{0,1},{1,2},{2,3},{3,0},{4,5},{5,6},{6,7},{7,4},{8,9},{9,10},{10,1... | collective-permute-start | bytes 12296 | tf_op jit(solution)/shard_map/ppermute | solution.py:51
  467.3 14.8 %collective-permute-done.88 = f32[384,768]{1,0:T(8,128)S(1)} collective-permute-done((f32[384,768]{1,0:T(8,128)S(1)}, f32[384,768]{1,0:T(8,128)S(1)}, u32[]{:S(2)}, u32[]{:S(2)}) %collective-permute-start.88) | collective-permute-done | bytes 1179680 | tf_op jit(solution)/shard_map/ppermute | solution.py:41
  484.0 23.4 %collective-permute-done.47 = f32[384,768]{1,0:T(8,128)S(1)} collective-permute-done((f32[384,768]{1,0:T(8,128)S(1)}, f32[384,768]{1,0:T(8,128)S(1)}, u32[]{:S(2)}, u32[]{:S(2)}) %collective-permute-start.47) | collective-permute-done | bytes 1179680 | tf_op jit(solution)/shard_map/ppermute | solution.py:41
  508.8 23.9 %collective-permute-done.76 = f32[384,768]{1,0:T(8,128)S(1)} collective-permute-done((f32[384,768]{1,0:T(8,128)S(1)}, f32[384,768]{1,0:T(8,128)S(1)}, u32[]{:S(2)}, u32[]{:S(2)}) %collective-permute-start.76) | collective-permute-done | bytes 1179680 | tf_op jit(solution)/shard_map/ppermute | solution.py:41
  535.2 10.4 %collective-permute-done.89 = f32[192,768]{1,0:T(8,128)S(1)} collective-permute-done((f32[192,768]{1,0:T(8,128)S(1)}, f32[192,768]{1,0:T(8,128)S(1)}, u32[]{:S(2)}, u32[]{:S(2)}) %collective-permute-start.89) | collective-permute-done | bytes 589856 | tf_op jit(solution)/shard_map/ppermute | solution.py:41
  545.8 12.4 %collective-permute-done.48 = f32[192,768]{1,0:T(8,128)S(1)} collective-permute-done((f32[192,768]{1,0:T(8,128)S(1)}, f32[192,768]{1,0:T(8,128)S(1)}, u32[]{:S(2)}, u32[]{:S(2)}) %collective-permute-start.48) | collective-permute-done | bytes 589856 | tf_op jit(solution)/shard_map/ppermute | solution.py:41
  558.5 7.3 %collective-permute-start.49 = (f32[96,768]{1,0:T(8,128)S(1)}, f32[96,768]{1,0:T(8,128)S(1)}, u32[]{:S(2)}, u32[]{:S(2)}) collective-permute-start(f32[96,768]{1,0:T(8,128)S(1)} %get-tuple-element.288), channel_id=1, source_target_pairs={{0,2},{1,3},{2,0},{3,1},{4,6},{5,7},{6,4},{7,5},{8,10},{9,11},{10,... | collective-permute-start | bytes 884744 | tf_op jit(solution)/shard_map/ppermute | solution.py:51
  567.6 6.4 collective-permute-start.50
  588.0 9.0 %collective-permute-start.51 = (f32[1,96,768]{2,1,0:T(8,128)S(1)}, f32[1,96,768]{2,1,0:T(8,128)S(1)}, u32[]{:S(2)}, u32[]{:S(2)}) collective-permute-start(f32[1,96,768]{2,1,0:T(8,128)S(1)} %fusion.53), channel_id=1, source_target_pairs={{0,8},{4,12},{8,0},{12,4},{16,24},{20,28},{24,16},{28,20},{1,9},{5... | collective-permute-start | bytes 884744 | tf_op jit(solution)/shard_map/ppermute | solution.py:41
  597.1 8.0 %collective-permute-start.78 = (f32[96,768]{1,0:T(8,128)S(1)}, f32[96,768]{1,0:T(8,128)S(1)}, u32[]{:S(2)}, u32[]{:S(2)}) collective-permute-start(f32[96,768]{1,0:T(8,128)S(1)} %get-tuple-element.286), channel_id=1, source_target_pairs={{0,2},{1,3},{2,0},{3,1},{4,6},{5,7},{6,4},{7,5},{8,10},{9,11},{10,... | collective-permute-start | bytes 884744 | tf_op jit(solution)/shard_map/ppermute | solution.py:51
  605.1 7.4 %collective-permute-done.90 = f32[96,768]{1,0:T(8,128)S(1)} collective-permute-done((f32[96,768]{1,0:T(8,128)S(1)}, f32[96,768]{1,0:T(8,128)S(1)}, u32[]{:S(2)}, u32[]{:S(2)}) %collective-permute-start.90) | collective-permute-done | bytes 294944 | tf_op jit(solution)/shard_map/ppermute | solution.py:51
  612.6 7.0 collective-permute-start.41
  621.7 13.3 %collective-permute-done.78 = f32[96,768]{1,0:T(8,128)S(1)} collective-permute-done((f32[96,768]{1,0:T(8,128)S(1)}, f32[96,768]{1,0:T(8,128)S(1)}, u32[]{:S(2)}, u32[]{:S(2)}) %collective-permute-start.78) | collective-permute-done | bytes 294944 | tf_op jit(solution)/shard_map/ppermute | solution.py:51
  636.6 23.0 %collective-permute-done.74 = f32[96,768]{1,0:T(8,128)S(1)} collective-permute-done((f32[96,768]{1,0:T(8,128)S(1)}, f32[96,768]{1,0:T(8,128)S(1)}, u32[]{:S(2)}, u32[]{:S(2)}) %collective-permute-start.74) | collective-permute-done | bytes 294944 | tf_op jit(solution)/shard_map/ppermute | solution.py:51
  671.1 9.7 %collective-permute-done.81 = f32[2,96,768]{2,1,0:T(8,128)S(1)} collective-permute-done((f32[2,96,768]{2,1,0:T(8,128)S(1)}, f32[2,96,768]{2,1,0:T(8,128)S(1)}, u32[]{:S(2)}, u32[]{:S(2)}) %collective-permute-start.81) | collective-permute-done | bytes 589856 | tf_op jit(solution)/shard_map/ppermute | solution.py:41
  (560 shorter events, 280.5 us)
Async XLA Ops:
  7.2 697.7 %all-gather.2.cloned.1.call-start = ((), (), s32[]{:S(2)}) async-start(), calls=%async_computation | async-start | bytes 7864320 | tf_op jit(solution)/shard_map/all_gather | solution.py:358
  17.7 34.6 %collective-permute-start.9 = (f32[8,128]{1,0:T(8,128)S(1)}, f32[8,128]{1,0:T(8,128)S(1)}, u32[]{:S(2)}, u32[]{:S(2)}) collective-permute-start(f32[8,128]{1,0:T(8,128)S(1)} %scatter.35), channel_id=1, source_target_pairs={{1,0},{2,1},{3,2},{0,3},{5,4},{6,5},{7,6},{4,7},{9,8},{10,9},{11,1... | collective-permute-start | bytes 12296 | tf_op jit(solution)/shard_map/ppermute | solution.py:46
  20.3 43.7 %collective-permute-start.32 = (f32[96,768]{1,0:T(8,128)S(1)}, f32[96,768]{1,0:T(8,128)S(1)}, u32[]{:S(2)}, u32[]{:S(2)}) collective-permute-start(f32[96,768]{1,0:T(8,128)S(1)} %convert_multiply_fusion.2), channel_id=1, source_target_pairs={{3,0},{0,1},{1,2},{2,3},{7,4},{4,5},{5,6},{6,7},{11,8},{8,9},{9,10... | collective-permute-start | bytes 884744 | tf_op jit(solution)/shard_map/ppermute | solution.py:46
  36.5 37.0 %collective-permute-start.27 = (f32[96,768]{1,0:T(8,128)S(1)}, f32[96,768]{1,0:T(8,128)S(1)}, u32[]{:S(2)}, u32[]{:S(2)}) collective-permute-start(f32[96,768]{1,0:T(8,128)S(1)} %convert_multiply_fusion.2), channel_id=1, source_target_pairs={{1,0},{2,1},{3,2},{0,3},{5,4},{6,5},{7,6},{4,7},{9,8},{10,9},{11,1... | collective-permute-start | bytes 884744 | tf_op jit(solution)/shard_map/ppermute | solution.py:46
  57.2 32.7 %collective-permute-start.25 = (f32[384,768]{1,0:T(8,128)S(1)}, f32[384,768]{1,0:T(8,128)S(1)}, u32[]{:S(2)}, u32[]{:S(2)}) collective-permute-start(f32[384,768]{1,0:T(8,128)S(1)} %pad_maximum_fusion.12), channel_id=1, source_target_pairs={{0,8},{4,12},{8,0},{12,4},{16,24},{20,28},{24,16},{28,20},{1,9},{5... | collective-permute-start | bytes 3538952 | tf_op jit(solution)/shard_map/ppermute | solution.py:41
  89.9 55.6 %collective-permute-start.34 = (f32[384,768]{1,0:T(8,128)S(1)}, f32[384,768]{1,0:T(8,128)S(1)}, u32[]{:S(2)}, u32[]{:S(2)}) collective-permute-start(f32[384,768]{1,0:T(8,128)S(1)} %pad_maximum_fusion.14), channel_id=1, source_target_pairs={{0,8},{4,12},{8,0},{12,4},{16,24},{20,28},{24,16},{28,20},{1,9},{5... | collective-permute-start | bytes 3538952 | tf_op jit(solution)/shard_map/ppermute | solution.py:41
  90.5 42.3 %collective-permute-start.19 = (f32[192,768]{1,0:T(8,128)S(1)}, f32[192,768]{1,0:T(8,128)S(1)}, u32[]{:S(2)}, u32[]{:S(2)}) collective-permute-start(f32[192,768]{1,0:T(8,128)S(1)} %pad_maximum_fusion.20), channel_id=1, source_target_pairs={{0,8},{4,12},{8,0},{12,4},{16,24},{20,28},{24,16},{28,20},{1,9},{5... | collective-permute-start | bytes 1769480 | tf_op jit(solution)/shard_map/ppermute | solution.py:41
  93.5 119.8 %collective-permute-start.26 = (f32[768,768]{1,0:T(8,128)S(1)}, f32[768,768]{1,0:T(8,128)S(1)}, u32[]{:S(2)}, u32[]{:S(2)}) collective-permute-start(f32[768,768]{1,0:T(8,128)S(1)} %constant_dynamic-update-slice_fusion.10), channel_id=1, source_target_pairs={{0,4},{4,0},{8,12},{12,8},{16,20},{20,16},{24,28},{28,24},{1,5},{5... | collective-permute-start | bytes 7077896 | tf_op jit(solution)/shard_map/ppermute | solution.py:41
  97.4 35.4 %collective-permute-start.6 = (f32[192,768]{1,0:T(8,128)S(1)}, f32[192,768]{1,0:T(8,128)S(1)}, u32[]{:S(2)}, u32[]{:S(2)}) collective-permute-start(f32[192,768]{1,0:T(8,128)S(1)} %pad_maximum_fusion.19), channel_id=1, source_target_pairs={{0,16},{4,20},{8,24},{12,28},{16,0},{20,4},{24,8},{28,12},{1,17},{... | collective-permute-start | bytes 1769480 | tf_op jit(solution)/shard_map/ppermute | solution.py:41
  98.7 46.7 %collective-permute-start.1 = (f32[192,768]{1,0:T(8,128)S(1)}, f32[192,768]{1,0:T(8,128)S(1)}, u32[]{:S(2)}, u32[]{:S(2)}) collective-permute-start(f32[192,768]{1,0:T(8,128)S(1)} %pad_maximum_fusion.18), channel_id=1, source_target_pairs={{0,8},{4,12},{8,0},{12,4},{16,24},{20,28},{24,16},{28,20},{1,9},{5... | collective-permute-start | bytes 1769480 | tf_op jit(solution)/shard_map/ppermute | solution.py:41
  132.8 45.3 %collective-permute-start.20 = (f32[384,768]{1,0:T(8,128)S(1)}, f32[384,768]{1,0:T(8,128)S(1)}, u32[]{:S(2)}, u32[]{:S(2)}) collective-permute-start(f32[384,768]{1,0:T(8,128)S(1)} %pad_maximum_fusion.11), channel_id=1, source_target_pairs={{0,16},{4,20},{8,24},{12,28},{16,0},{20,4},{24,8},{28,12},{1,17},{... | collective-permute-start | bytes 3538952 | tf_op jit(solution)/shard_map/ppermute | solution.py:41
  145.4 50.5 %collective-permute-start.7 = (f32[384,768]{1,0:T(8,128)S(1)}, f32[384,768]{1,0:T(8,128)S(1)}, u32[]{:S(2)}, u32[]{:S(2)}) collective-permute-start(f32[384,768]{1,0:T(8,128)S(1)} %pad_maximum_fusion.10), channel_id=1, source_target_pairs={{0,8},{4,12},{8,0},{12,4},{16,24},{20,28},{24,16},{28,20},{1,9},{5... | collective-permute-start | bytes 3538952 | tf_op jit(solution)/shard_map/ppermute | solution.py:41
  145.5 57.9 %collective-permute-start.2 = (f32[384,768]{1,0:T(8,128)S(1)}, f32[384,768]{1,0:T(8,128)S(1)}, u32[]{:S(2)}, u32[]{:S(2)}) collective-permute-start(f32[384,768]{1,0:T(8,128)S(1)} %pad_maximum_fusion.9), channel_id=1, source_target_pairs={{0,16},{4,20},{8,24},{12,28},{16,0},{20,4},{24,8},{28,12},{1,17},{... | collective-permute-start | bytes 3538952 | tf_op jit(solution)/shard_map/ppermute | solution.py:41
  152.8 44.2 %collective-permute-start.17 = (f32[64,128]{1,0:T(8,128)S(1)}, f32[64,128]{1,0:T(8,128)S(1)}, u32[]{:S(2)}, u32[]{:S(2)}) collective-permute-start(f32[64,128]{1,0:T(8,128)S(1)} %constant_dynamic-update-slice_fusion.4), channel_id=1, source_target_pairs={{0,4},{4,0},{8,12},{12,8},{16,20},{20,16},{24,28},{28,24},{1,5},{5... | collective-permute-start | bytes 98312 | tf_op jit(solution)/shard_map/ppermute | solution.py:41
  393.7 48.1 %collective-permute-start.87 = (f32[768,768]{1,0:T(8,128)}, f32[768,768]{1,0:T(8,128)}, u32[]{:S(2)}, u32[]{:S(2)}) collective-permute-start(f32[768,768]{1,0:T(8,128)} %fusion.33), channel_id=1, source_target_pairs={{0,4},{4,0},{8,12},{12,8},{16,20},{20,16},{24,28},{28,24},{1,5},{5... | collective-permute-start | bytes 7077896 | tf_op jit(solution)/shard_map/ppermute | solution.py:41
  415.3 33.8 %collective-permute-start.83 = (f32[768,768]{1,0:T(8,128)}, f32[768,768]{1,0:T(8,128)}, u32[]{:S(2)}, u32[]{:S(2)}) collective-permute-start(f32[768,768]{1,0:T(8,128)} %fusion.36), channel_id=1, source_target_pairs={{0,4},{4,0},{8,12},{12,8},{16,20},{20,16},{24,28},{28,24},{1,5},{5... | collective-permute-start | bytes 7077896 | tf_op jit(solution)/shard_map/ppermute | solution.py:41
  449.1 138.9 %collective-permute-start.37 = (f32[1024,192]{0,1:T(8,128)}, f32[1024,192]{0,1:T(8,128)}, u32[]{:S(2)}, u32[]{:S(2)}) collective-permute-start(f32[1024,192]{0,1:T(8,128)} %get-tuple-element.281), channel_id=1, source_target_pairs={{1,2},{2,1},{5,6},{6,5},{9,10},{10,9},{13,14},{14,13},{17,18},{18,... | collective-permute-start | bytes 2359304 | tf_op jit(solution)/shard_map/ppermute | solution.py:245
  459.8 47.6 %collective-permute-start.47 = (f32[384,768]{1,0:T(8,128)S(1)}, f32[384,768]{1,0:T(8,128)S(1)}, u32[]{:S(2)}, u32[]{:S(2)}) collective-permute-start(f32[384,768]{1,0:T(8,128)S(1)} %slice.628), channel_id=1, source_target_pairs={{0,8},{4,12},{8,0},{12,4},{16,24},{20,28},{24,16},{28,20},{1,9},{5... | collective-permute-start | bytes 3538952 | tf_op jit(solution)/shard_map/ppermute | solution.py:41
  463.5 69.1 %collective-permute-start.76 = (f32[384,768]{1,0:T(8,128)S(1)}, f32[384,768]{1,0:T(8,128)S(1)}, u32[]{:S(2)}, u32[]{:S(2)}) collective-permute-start(f32[384,768]{1,0:T(8,128)S(1)} %slice.670), channel_id=1, source_target_pairs={{0,8},{4,12},{8,0},{12,4},{16,24},{20,28},{24,16},{28,20},{1,9},{5... | collective-permute-start | bytes 3538952 | tf_op jit(solution)/shard_map/ppermute | solution.py:41
  482.1 51.0 %collective-permute-start.72 = (f32[384,768]{1,0:T(8,128)S(1)}, f32[384,768]{1,0:T(8,128)S(1)}, u32[]{:S(2)}, u32[]{:S(2)}) collective-permute-start(f32[384,768]{1,0:T(8,128)S(1)} %slice.662), channel_id=1, source_target_pairs={{0,16},{4,20},{8,24},{12,28},{16,0},{20,4},{24,8},{28,12},{1,17},{... | collective-permute-start | bytes 3538952 | tf_op jit(solution)/shard_map/ppermute | solution.py:41
  483.5 51.2 %collective-permute-start.43 = (f32[384,768]{1,0:T(8,128)S(1)}, f32[384,768]{1,0:T(8,128)S(1)}, u32[]{:S(2)}, u32[]{:S(2)}) collective-permute-start(f32[384,768]{1,0:T(8,128)S(1)} %slice.620), channel_id=1, source_target_pairs={{0,16},{4,20},{8,24},{12,28},{16,0},{20,4},{24,8},{28,12},{1,17},{... | collective-permute-start | bytes 3538952 | tf_op jit(solution)/shard_map/ppermute | solution.py:41
  507.4 38.2 %collective-permute-start.89 = (f32[192,768]{1,0:T(8,128)S(1)}, f32[192,768]{1,0:T(8,128)S(1)}, u32[]{:S(2)}, u32[]{:S(2)}) collective-permute-start(f32[192,768]{1,0:T(8,128)S(1)} %slice.689), channel_id=1, source_target_pairs={{0,16},{4,20},{8,24},{12,28},{16,0},{20,4},{24,8},{28,12},{1,17},{... | collective-permute-start | bytes 1769480 | tf_op jit(solution)/shard_map/ppermute | solution.py:41
  534.7 39.4 %collective-permute-start.77 = (f32[192,768]{1,0:T(8,128)S(1)}, f32[192,768]{1,0:T(8,128)S(1)}, u32[]{:S(2)}, u32[]{:S(2)}) collective-permute-start(f32[192,768]{1,0:T(8,128)S(1)} %slice.672), channel_id=1, source_target_pairs={{0,16},{4,20},{8,24},{12,28},{16,0},{20,4},{24,8},{28,12},{1,17},{... | collective-permute-start | bytes 1769480 | tf_op jit(solution)/shard_map/ppermute | solution.py:41
  545.6 51.5 %collective-permute-start.73 = (f32[192,768]{1,0:T(8,128)S(1)}, f32[192,768]{1,0:T(8,128)S(1)}, u32[]{:S(2)}, u32[]{:S(2)}) collective-permute-start(f32[192,768]{1,0:T(8,128)S(1)} %slice.664), channel_id=1, source_target_pairs={{0,8},{4,12},{8,0},{12,4},{16,24},{20,28},{24,16},{28,20},{1,9},{5... | collective-permute-start | bytes 1769480 | tf_op jit(solution)/shard_map/ppermute | solution.py:41
  581.4 31.1 %collective-permute-start.90 = (f32[96,768]{1,0:T(8,128)S(1)}, f32[96,768]{1,0:T(8,128)S(1)}, u32[]{:S(2)}, u32[]{:S(2)}) collective-permute-start(f32[96,768]{1,0:T(8,128)S(1)} %get-tuple-element.284), channel_id=1, source_target_pairs={{0,2},{1,3},{2,0},{3,1},{4,6},{5,7},{6,4},{7,5},{8,10},{9,11},{10,... | collective-permute-start | bytes 884744 | tf_op jit(solution)/shard_map/ppermute | solution.py:51
  581.4 31.1 %collective-permute-start.91 = (f32[96,768]{1,0:T(8,128)S(1)}, f32[96,768]{1,0:T(8,128)S(1)}, u32[]{:S(2)}, u32[]{:S(2)}) collective-permute-start(f32[96,768]{1,0:T(8,128)S(1)} %get-tuple-element.285), channel_id=1, source_target_pairs={{0,3},{1,0},{2,1},{3,2},{4,7},{5,4},{6,5},{7,6},{8,11},{9,8},{10,9... | collective-permute-start | bytes 884744 | tf_op jit(solution)/shard_map/ppermute | solution.py:51
  587.9 31.7 %collective-permute-start.86 = (f32[96,768]{1,0:T(8,128)S(1)}, f32[96,768]{1,0:T(8,128)S(1)}, u32[]{:S(2)}, u32[]{:S(2)}) collective-permute-start(f32[96,768]{1,0:T(8,128)S(1)} %slice.683), channel_id=1, source_target_pairs={{0,1},{1,2},{2,3},{3,0},{4,5},{5,6},{6,7},{7,4},{8,9},{9,10},{10,1... | collective-permute-start | bytes 884744 | tf_op jit(solution)/shard_map/ppermute | solution.py:51
  588.0 32.3 %collective-permute-start.51 = (f32[1,96,768]{2,1,0:T(8,128)S(1)}, f32[1,96,768]{2,1,0:T(8,128)S(1)}, u32[]{:S(2)}, u32[]{:S(2)}) collective-permute-start(f32[1,96,768]{2,1,0:T(8,128)S(1)} %fusion.53), channel_id=1, source_target_pairs={{0,8},{4,12},{8,0},{12,4},{16,24},{20,28},{24,16},{28,20},{1,9},{5... | collective-permute-start | bytes 884744 | tf_op jit(solution)/shard_map/ppermute | solution.py:41
  597.1 38.0 %collective-permute-start.78 = (f32[96,768]{1,0:T(8,128)S(1)}, f32[96,768]{1,0:T(8,128)S(1)}, u32[]{:S(2)}, u32[]{:S(2)}) collective-permute-start(f32[96,768]{1,0:T(8,128)S(1)} %get-tuple-element.286), channel_id=1, source_target_pairs={{0,2},{1,3},{2,0},{3,1},{4,6},{5,7},{6,4},{7,5},{8,10},{9,11},{10,... | collective-permute-start | bytes 884744 | tf_op jit(solution)/shard_map/ppermute | solution.py:51
  612.6 48.2 %collective-permute-start.41 = (f32[1024,192]{0,1:T(8,128)S(1)}, f32[1024,192]{0,1:T(8,128)S(1)}, u32[]{:S(2)}, u32[]{:S(2)}) collective-permute-start(f32[1024,192]{0,1:T(8,128)S(1)} %copy-done.39), channel_id=1, source_target_pairs={{0,1},{3,2},{4,5},{7,6},{8,9},{11,10},{12,13},{15,14},{16,17},{19,... | collective-permute-start | bytes 2359304 | tf_op jit(solution)/shard_map/ppermute | solution.py:247
  619.7 42.5 %collective-permute-start.40 = (f32[1024,192]{0,1:T(8,128)S(1)}, f32[1024,192]{0,1:T(8,128)S(1)}, u32[]{:S(2)}, u32[]{:S(2)}) collective-permute-start(f32[1024,192]{0,1:T(8,128)S(1)} %copy-done.49), channel_id=1, source_target_pairs={{1,2},{2,1},{5,6},{6,5},{9,10},{10,9},{13,14},{14,13},{17,18},{18,... | collective-permute-start | bytes 2359304 | tf_op jit(solution)/shard_map/ppermute | solution.py:248
  620.4 41.8 %collective-permute-start.38 = (f32[1024,192]{0,1:T(8,128)}, f32[1024,192]{0,1:T(8,128)S(1)}, u32[]{:S(2)}, u32[]{:S(2)}) collective-permute-start(f32[1024,192]{0,1:T(8,128)} %collective-permute-done.37), channel_id=1, source_target_pairs={{2,3},{1,0},{6,7},{5,4},{10,11},{9,8},{14,15},{13,12},{18,19},{17,... | collective-permute-start | bytes 2359304 | tf_op jit(solution)/shard_map/ppermute | solution.py:249
  (128 other events, 1829.0 us)
Sparse Core Ops, SparseCore 0:
  432.6 129.3 all-gather.1

commit v2 on v1

v2 whole, which is shorter than its diff:
```python
import jax
import jax.numpy as jnp
from jax import lax
from jax.experimental import pallas as pl
from jax.experimental.pallas import tpu as pltpu
from jax.sharding import PartitionSpec as P

HD = 64
EPS = 1e-05
MASKED = -1000000000.0
BITS = 3
INNER = 1 << BITS
F32 = jnp.float32
BF16 = jnp.bfloat16


def layer_norm(hidden, gain, shift):
    center = hidden - jnp.mean(hidden, -1, keepdims=True)
    spread = jnp.mean(center * center, -1, keepdims=True)
    return center * lax.rsqrt(spread + EPS) * gain + shift


def exact_gelu(inputs):
    return jax.nn.gelu(inputs, approximate=False)


def nn(left, right):
    return lax.dot_general(left, right, (((1,), (0,)), ((), ())), preferred_element_type=F32)


def nt(left, right):
    return lax.dot_general(left, right, (((1,), (1,)), ((), ())), preferred_element_type=F32)


def tn(left, right):
    return lax.dot_general(left, right, (((0,), (0,)), ((), ())), preferred_element_type=F32)


APART = [c | (x << 1) | (y << 2) for c in (0, 1) for y in (0, 1) for x in (0, 1)]


def unit(lengths):
    return jnp.where(lengths[0] > 0, 1.0, 0.0).astype(F32)


def after(x, *others):
    return lax.optimization_barrier((x, others))[0]


def flip(x, bit):
    size = lax.axis_size("dp")
    return lax.ppermute(x, "dp", [(i, i ^ (1 << bit)) for i in range(size)])


def from_next(x, step):
    size = lax.axis_size("tensor")
    return lax.ppermute(x, "tensor", [((i + step) % size, i) for i in range(size)])


def to_next(x, step):
    size = lax.axis_size("tensor")
    return lax.ppermute(x, "tensor", [(i, (i + step) % size) for i in range(size)])


def relative(x, axis):
    me = lax.axis_index("dp") % INNER
    return jnp.concatenate([lax.dynamic_slice_in_dim(x, me ^ apart, 1, axis) for apart in APART], axis)


def apart_of(step):
    return (step // 4) | ((step % 2) << 1) | (((step // 2) % 2) << 2)


def relative_kernel(me_ref, *refs):
    count = len(refs) // 2
    for source, target in zip(refs[:count], refs[count:]):
        target[...] = source[...]


def relative_blocks(me, *arrays):
    def spec(array, index):
        lead = array.ndim - 3
        block = array.shape[:lead] + (1,) + array.shape[lead + 1 :]
        return pl.BlockSpec(block, lambda k, me_ref: (0,) * lead + (index(k, me_ref), 0, 0))

    return pl.pallas_call(
        relative_kernel,
        grid_spec=pltpu.PrefetchScalarGridSpec(
            num_scalar_prefetch=1,
            grid=(INNER,),
            in_specs=[spec(array, lambda k, me_ref: me_ref[0] ^ apart_of(k)) for array in arrays],
            out_specs=[spec(array, lambda k, me_ref: k) for array in arrays],
        ),
        out_shape=[jax.ShapeDtypeStruct(array.shape, array.dtype) for array in arrays],
        compiler_params=pltpu.CompilerParams(vmem_limit_bytes=48 * 2**20),
    )(me, *arrays)


def units_kernel(near_ref, a_ref, a_far_ref, b_ref, b_far_ref, out_ref):
    step = pl.program_id(0)
    half = a_ref.shape[2]
    out_ref[0, 0] = near_ref[0]

    @pl.when(step < 2)
    def _():
        out_ref[0, 1:, :half] = a_ref[0].astype(BF16)

    @pl.when(step >= 2)
    def _():
        out_ref[0, 1:, :half] = a_far_ref[0].astype(BF16)

    @pl.when(step % 2 == 0)
    def _():
        out_ref[0, 1:, half:] = b_ref[0].astype(BF16)

    @pl.when(step % 2 == 1)
    def _():
        out_ref[0, 1:, half:] = b_far_ref[0].astype(BF16)


def units_together(near, core, parts):
    count, width = near.shape[1:]
    half = count // 2
    by_x = pl.BlockSpec((1, 3, half, width), lambda k: (k % 2, 0, 0, 0))
    by_y = pl.BlockSpec((1, 3, half, width), lambda k: (k // 2, 0, 0, 0))
    full = pl.pallas_call(
        units_kernel,
        grid=(4,),
        in_specs=[pl.BlockSpec((1, count, width), lambda k: (4 * core + k, 0, 0)), by_x, by_x, by_y, by_y],
        out_specs=pl.BlockSpec((1, 4, count, width), lambda k: (k, 0, 0, 0)),
        out_shape=jax.ShapeDtypeStruct((4, 4, count, width), BF16),
        compiler_params=pltpu.CompilerParams(vmem_limit_bytes=48 * 2**20),
    )(near, *parts)
    return full.reshape(16 * count, width)


def gather_places(piece):
    return jnp.stack([from_next(piece, step) for step in (1, 2, 3)])


def gather_halves(piece):
    half = piece.shape[0] // 2
    places = [from_next(piece, step) for step in (1, 2, 3)]
    return [jnp.stack([place[:half] for place in places]), jnp.stack([place[half:] for place in places])]


def gather_first(held, route, recv=lambda x: x):
    return jnp.stack([held, recv(flip(held, 2 if route else 1))])


def gather_second(held, route, recv=lambda x: x):
    if route:
        return jnp.stack([held, recv(flip(held, 1))], 1)
    return jnp.stack([held, recv(flip(held, 2))])


def scatter_first(held, route, recv=lambda x: x):
    if route:
        got = recv(flip(held[:, 1], 1))
        return held[0, 0] + got[0], held[1, 0] + got[1]
    got = recv(flip(held[1], 2))
    return held[0, 0] + got[0], held[0, 1] + got[1]


def scatter_second(parts, route, recv=lambda x: x):
    return parts[0] + recv(flip(parts[1], 2 if route else 1))


def scatter_places(places, recv=lambda x: x):
    total = places[0]
    for step in (1, 2, 3):
        total = total + recv(to_next(places[step], step))
    bit = BITS
    while (1 << bit) < lax.axis_size("dp"):
        total = total + flip(total, bit)
        bit += 1
    return total


def gather_in_order(piece, order):
    held = piece[None]
    for bit in (*order, 0):
        held = jnp.concatenate([held, flip(held, bit)], 0)
    me = lax.axis_index("dp") % INNER
    blocks = []
    for index in range(INNER):
        apart = me ^ index
        place = sum(((apart >> bit) & 1) << at for at, bit in enumerate((*order, 0)))
        blocks.append(lax.dynamic_index_in_dim(held, place, 0))
    return jnp.concatenate(blocks, 0)


def sum_everywhere(x, others):
    others = list(others)
    for axis in ("dp", "tensor"):
        size = lax.axis_size(axis)
        step = 1
        while step < size:
            got = lax.ppermute(x, axis, [(i, i ^ step) for i in range(size)])
            x = x + (after(got, others.pop(0)) if others else got)
            step *= 2
    return x


CHUNK = 256


def lane_masks(width):
    lane = lax.broadcasted_iota(jnp.int32, (1, width), 1)
    return [(lane >= start) & (lane < start + HD) for start in range(0, width, HD)]


def keep(mask, x):
    return jnp.where(mask, x, jnp.zeros_like(x))


def softmax_turned(keys, query, valid):
    scores = jnp.where(valid, nt(keys, query), MASKED)
    expo = jnp.exp(scores - jnp.max(scores, 0, keepdims=True))
    return expo * (1.0 / jnp.sum(expo, 0, keepdims=True))


def forward_kernel(me_ref, lengths_ref, q_ref, k_ref, v_ref, mixed_ref):
    keys = k_ref.shape[0]
    queries = q_ref.shape[0]
    valid = lax.broadcasted_iota(jnp.int32, (keys, 1), 0) < lengths_ref[pl.program_id(0)]
    masks = lane_masks(q_ref.shape[1])
    turned = v_ref[...].T
    sub = HD // INNER
    spots = []
    for block in range(INNER):
        apart = me_ref[0] ^ block
        spots.append((apart & 1) * 4 + (apart >> 2) * 2 + ((apart >> 1) & 1))
    for start in range(0, queries, CHUNK):
        rows = pl.ds(start, CHUNK)
        for head, mask in enumerate(masks):
            probs = softmax_turned(k_ref[...], keep(mask, q_ref[rows, :]), valid).astype(BF16)
            part = nn(turned[head * HD : (head + 1) * HD, :], probs).astype(BF16).astype(F32)
            for block, spot in enumerate(spots):
                at = pl.multiple_of(head * HD + spot * sub, sub)
                mixed_ref[pl.ds(at, sub), rows] = part[block * sub : (block + 1) * sub, :]


def backward_kernel(last, scalars_ref, *refs):
    q_ref, k_ref, v_ref, dm_ref, mixed_ref, wq_ref, wk_ref, wv_ref, own_ref, seq_ref, da_ref = refs[:11]
    given, refs = (refs[11:13], refs[13:]) if last else (refs[11:12], refs[12:])
    near_ref, far_ref, sums_ref, own_part_ref, seq_part_ref, dk_sum, dv_sum, dq_all, dq_turned = refs
    keys = k_ref.shape[0]
    queries = q_ref.shape[0]
    step = pl.program_id(0)
    valid = lax.broadcasted_iota(jnp.int32, (keys, 1), 0) < scalars_ref[0]
    masks = lane_masks(q_ref.shape[1])
    turned = k_ref[...].T
    for start in range(0, queries, CHUNK):
        rows = pl.ds(start, CHUNK)
        parts = []
        for head, mask in enumerate(masks):
            query = keep(mask, q_ref[rows, :])
            d_mixed = keep(mask, dm_ref[rows, :])
            probs = softmax_turned(k_ref[...], query, valid)
            d_values = nn(probs.astype(BF16), d_mixed)
            d_probs = nt(v_ref[...], d_mixed)
            row_dot = jnp.sum(d_probs * probs, 0, keepdims=True)
            d_scores = (probs * (d_probs - row_dot)).astype(BF16)
            d_keys = nn(d_scores, query)
            parts.append(nn(turned[head * HD : (head + 1) * HD, :], d_scores))
            if start == 0 and head == 0:
                dk_sum[...] = d_keys
                dv_sum[...] = d_values
            else:
                dk_sum[...] += d_keys
                dv_sum[...] += d_values
        part = jnp.concatenate(parts, 0) * HD ** (-0.5)
        dq_turned[:, rows] = part.astype(BF16)
        dq_all[rows, :] = part.T.astype(BF16)
    d_queries = dq_all[...]
    d_keys = dk_sum[...].astype(BF16)
    d_values = dv_sum[...].astype(BF16)
    keys_turned, values_turned = d_keys.T, d_values.T
    sums_ref[0, 0:1] = jnp.sum(d_queries.astype(F32), 0, keepdims=True)
    sums_ref[0, 1:2] = jnp.sum(d_values.astype(F32), 0, keepdims=True)

    sub = HD // INNER
    heads = near_ref.shape[2] // (4 * sub)
    grads = [
        nn(dq_turned[...], own_ref[...]),
        nn(keys_turned, seq_ref[...]),
        nn(values_turned, seq_ref[...]),
        nn(mixed_ref[...], da_ref[...]),
    ]
    for which in range(2):
        head = 2 * step + which
        place = head // heads
        for kind, grad in enumerate(grads):
            rows = pl.ds(pl.multiple_of((kind * heads + head % heads) * sub, sub), sub)
            for block in range(INNER):
                target = near_ref if block < INNER // 2 else far_ref
                at = which * HD + block * sub
                target[block % (INNER // 2), place, rows, :] = grad[at : at + sub, :]

    own_part = tn(wq_ref[...], dq_turned[...])
    seq_part = tn(wk_ref[...], keys_turned) + tn(wv_ref[...], values_turned)

    @pl.when(step == 0)
    def _():
        own_part_ref[...] = own_part + (given[0][...] if last else given[0][...].T)
        seq_part_ref[...] = seq_part + given[1][...] if last else seq_part

    @pl.when(step > 0)
    def _():
        own_part_ref[...] += own_part
        seq_part_ref[...] += seq_part

    if last:

        @pl.when(step == pl.num_programs(0) - 1)
        def _():
            own = pl.ds(pl.multiple_of(scalars_ref[1], CHUNK), queries)
            seq_part_ref[:, own] += own_part_ref[...]


def attention_forward(me, lengths, queries, keys, values):
    count, width = queries.shape
    seq = count // lengths.shape[0]
    block = pl.BlockSpec((seq, width), lambda i: (i, 0))
    work = count * seq * width
    return pl.pallas_call(
        forward_kernel,
        grid=(lengths.shape[0],),
        in_specs=[pl.BlockSpec(memory_space=pltpu.SMEM)] * 2 + [block] * 3,
        out_specs=pl.BlockSpec((width, seq), lambda i: (0, i)),
        out_shape=jax.ShapeDtypeStruct((width, count), F32),
        compiler_params=pltpu.CompilerParams(vmem_limit_bytes=48 * 2**20),
        cost_estimate=pl.CostEstimate(flops=work, bytes_accessed=4 * 2**20, transcendentals=0),
    )(me, lengths, queries, keys, values)


def attention_backward(scalars, half, in_pairs, weights, whole, given):
    queries, keys, values, d_mixed, mixed = in_pairs
    count, width = queries.shape
    long = keys.shape[0]
    pairs = width // (4 * HD)
    begin = half * pairs
    places = 2
    rows = 4 * (width // 4) // INNER
    columns = lambda array: pl.BlockSpec((array.shape[0], 2 * HD), lambda j: (0, begin + j))
    of_rows = lambda array: pl.BlockSpec((2 * HD, array.shape[1]), lambda j: (begin + j, 0))
    full = lambda array: pl.BlockSpec(array.shape, lambda j: (0,) * len(array.shape))
    sent = jax.ShapeDtypeStruct((INNER // 2, places, rows, width), F32)
    parts = [jax.ShapeDtypeStruct((width, n), F32) for n in (count, long)]
    return pl.pallas_call(
        lambda *refs: backward_kernel(half == 1, *refs),
        grid=(pairs,),
        in_specs=[pl.BlockSpec(memory_space=pltpu.SMEM)]
        + [columns(array) for array in (queries, keys, values, d_mixed)]
        + [of_rows(array) for array in (mixed, *weights)]
        + [full(array) for array in (*whole, *given)],
        out_specs=[full(sent), full(sent), pl.BlockSpec((1, 2, 2 * HD), lambda j: (j, 0, 0))]
        + [full(part) for part in parts],
        out_shape=[sent, sent, jax.ShapeDtypeStruct((pairs, 2, 2 * HD), F32), *parts],
        scratch_shapes=[
            pltpu.VMEM((long, 2 * HD), F32),
            pltpu.VMEM((long, 2 * HD), F32),
            pltpu.VMEM((count, 2 * HD), BF16),
            pltpu.VMEM((2 * HD, count), BF16),
        ],
        compiler_params=pltpu.CompilerParams(vmem_limit_bytes=56 * 2**20),
        cost_estimate=pl.CostEstimate(flops=count * width, bytes_accessed=2**20, transcendentals=0),
    )(scalars, queries, keys, values, d_mixed, mixed, *weights, *whole, *given)


class ShareInputs:
    def __init__(self, part):
        quarters = part.reshape((4, part.shape[0] // 4, part.shape[1]))
        place = lax.axis_index("tensor")
        self.flipped = place >= 2
        end = jnp.where(self.flipped, 3, 0)
        near = lambda i: lax.dynamic_index_in_dim(quarters, jnp.abs(end - i), 0, keepdims=False)
        self.near = [near(i) for i in range(4)]
        self.outer = (place == 0) | (place == 3)
        swap = [(0, 1), (1, 0), (2, 3), (3, 2)]
        self.first = lax.ppermute(near(jnp.where(self.outer, 3, 0)), "tensor", swap)
        self.second = lax.ppermute(self.near[2], "tensor", [(0, 1), (3, 2)])

    def middle(self):
        across = [(1, 2), (2, 1)]
        self.far = lax.ppermute(self.near[3] + self.first, "tensor", across)
        self.third = lax.ppermute(self.near[1], "tensor", [(0, 1), (3, 2)])
        self.across = lax.ppermute(self.near[2] + self.second, "tensor", across)

    def result(self):
        last = lax.ppermute(self.far, "tensor", [(2, 3), (1, 0)])
        mine = jnp.where(self.outer, self.near[0] + self.first, self.near[1] + self.third)
        theirs = jnp.where(self.outer, last, self.across)
        return jnp.concatenate(
            [jnp.where(self.flipped, theirs, mine), jnp.where(self.flipped, mine, theirs)], 1
        )


def on_device(
    tokens,
    lengths,
    cotangent,
    qkv_weight,
    qv_bias,
    out_weight,
    out_bias,
    first_gain,
    first_shift,
    up_weight,
    up_bias,
    down_weight,
    down_bias,
    second_gain,
    second_shift,
):
    rows, width = tokens.shape
    seq = rows // lengths.shape[0]
    columns = qkv_weight.shape[2]
    heads = columns // HD
    units = up_weight.shape[1]
    share = rows // 4
    sub = HD // INNER
    count = units // INNER
    scale = jnp.asarray(HD ** (-0.5), BF16)
    place = lax.axis_index("tensor")
    me = lax.axis_index("dp") % INNER
    one = unit(lengths)

    few = heads * sub
    heads_of = lambda x: x.reshape(x.shape[:-2] + (heads, INNER, sub, width))
    out_heads = heads_of(out_weight)
    qkv_heads = heads_of(qkv_weight.transpose(0, 2, 1))
    qv_heads = qv_bias.reshape(2, heads, INNER, sub)
    up_turned = up_weight.T.reshape(INNER, count, width)
    down_blocks = down_weight.reshape(INNER, count, width)
    up_bias_blocks = up_bias.reshape(INNER, count)
    mine = lambda x, axis: lax.dynamic_index_in_dim(x, me, axis, keepdims=False)
    vectors = jnp.concatenate([mine(up_bias_blocks, 0), mine(qv_heads, 2).reshape(-1)])
    out_piece = jnp.concatenate(
        [
            mine(out_heads, 1).reshape(few, width).astype(F32) * one,
            jnp.pad(vectors[None], ((0, 7), (0, width - vectors.shape[0]))),
        ]
    )
    up_piece = mine(up_turned, 0).astype(F32) * one
    down_piece = mine(down_blocks, 0).astype(F32) * one
    qkv_piece = mine(qkv_heads, 2).reshape(3 * few, width).astype(F32) * one

    local_q = (nn(tokens, qkv_weight[0]) + qv_bias[0]).astype(BF16) * scale
    local_k = nn(tokens, qkv_weight[1]).astype(BF16)
    local_v = (nn(tokens, qkv_weight[2]) + qv_bias[1]).astype(BF16)

    out_places = gather_places(out_piece)
    up_places = gather_halves(after(up_piece, out_piece))
    down_places = gather_halves(after(down_piece, up_piece))
    out_first = gather_first(out_places, 0)
    local_mixed = attention_forward(me[None], lengths, local_q, local_k, local_v)

    def both_first(places, recv=lambda x: x):
        return [gather_first(held, route, recv) for route, held in enumerate(places)]

    def both_second(held, recv=lambda x: x):
        return [held[0], recv(flip(held[0], 2)), held[1], recv(flip(held[1], 1))]

    out_far = gather_second(out_first, 0)
    up_first = both_first(after(up_places, local_mixed))
    out_other = flip(after(out_far, up_first), 0)
    local_mixed = after(local_mixed, down_places) * one
    mixed_places = [lax.dynamic_slice_in_dim(local_mixed, place * share, share, 1)]
    for step in (1, 2, 3):
        theirs = lax.rem(place + 4 - step, 4)
        mixed_places.append(
            from_next(lax.dynamic_slice_in_dim(local_mixed, theirs * share, share, 1), step)
        )
    mixed_places = after(mixed_places, up_first, out_other)
    late = lambda x: after(x, mixed_places)
    up_far = both_second(up_first, late)
    down_first = both_first(after(down_places, up_first), late)
    up_other = [flip(part, 0) for part in up_far]
    down_far = both_second(down_first)
    qkv_places = gather_places(after(qkv_piece, mixed_places))

    def heads_together(near, pair, kinds):
        far = jnp.stack(pair).reshape(2, 2, 2, 3, kinds, heads, sub, width)
        far = (far.transpose(4, 3, 5, 0, 1, 2, 6, 7) * one).astype(BF16)
        far = far.reshape(kinds, 3 * columns, width)
        return jnp.concatenate([near.reshape(kinds, columns, width), far], 1)

    def heads_apart(array, places):
        trail = array.shape[1:]
        both = array.reshape((places, heads, 2, 2, 2, sub) + trail)
        both = both.transpose((2, 3, 4, 0, 1, 5) + tuple(range(6, 6 + len(trail))))
        return both.reshape((2, 2, 2, places, few) + trail)

    all_heads = jnp.concatenate([qkv_heads.reshape(3 * heads, INNER, sub, width), out_heads]).astype(F32)
    up_near, down_near, heads_near = relative_blocks(
        after(me[None], out_first), up_turned, down_blocks, all_heads
    )
    heads_near = heads_near.reshape(4, heads, INNER, sub, width).astype(BF16)
    qkv_near, out_near = heads_near[:3], heads_near[3]
    out_pair = (out_far, out_other)
    out_rows = heads_together(out_near[None], [far[:, :, :, :few] for far in out_pair], 1)[0]
    small_far = jnp.stack([far[:, :, :, few, : vectors.shape[0]] for far in out_pair])
    up_bias_near = relative(up_bias_blocks, 0).reshape(2, 2, 2, 1, count)
    up_bias_full = jnp.concatenate([up_bias_near, small_far[..., :count]], 3).reshape(2, 2 * units)
    qv_far = small_far[..., count:].reshape(2, 2, 2, 3, 2, heads, sub).transpose(4, 3, 5, 0, 1, 2, 6)
    qv_near = relative(qv_heads, 2)
    qv_full = jnp.concatenate([qv_near.reshape(2, columns), qv_far.reshape(2, 3 * columns)], 1)

    which = place // 2
    length = lax.dynamic_slice_in_dim(lengths, which, 1, 0)
    seq_tokens = lax.dynamic_slice_in_dim(tokens, which * seq, seq, 0)
    own_tokens = lax.dynamic_slice_in_dim(tokens, place * share, share, 0)
    own_cotangent = lax.dynamic_slice_in_dim(cotangent, place * share, share, 0)
    turned_mixed = (jnp.concatenate(mixed_places, 0) * one).astype(BF16)
    first = own_tokens.astype(F32) + (tn(turned_mixed, out_rows) + out_bias)
    normed, first_back = jax.vjp(layer_norm, first, first_gain, first_shift)
    normed_low = normed.astype(BF16)

    normed_low = after(normed_low, down_far)
    down_other = [flip(part, 0) for part in down_far]
    up_full = [units_together(up_near, 0, up_far), units_together(up_near, 1, up_other)]
    hidden, active, gelu_back = [], [], []
    for core in range(2):
        hidden.append(nt(normed_low, up_full[core]) + up_bias_full[core])
        value, back = jax.vjp(exact_gelu, hidden[core])
        active.append(value.astype(BF16))
        gelu_back.append(back)
        normed_low = after(normed_low, active[core], qkv_places)
    down_full = [units_together(down_near, 0, down_far)]
    qkv_first = gather_first(after(qkv_places, active[0]), 1)
    branch = nn(after(active[0], active[1], qkv_first), down_full[0])
    down_full.append(units_together(down_near, 1, after(down_other, branch)))
    branch = branch + nn(active[1], down_full[1])
    second = normed + (branch + down_bias)
    result, second_back = jax.vjp(layer_norm, second, second_gain, second_shift)
    output = (lax.all_gather(result, "tensor", axis=0, tiled=True) * one).astype(BF16)

    d_second, grad_second_gain, grad_second_shift = second_back(own_cotangent.astype(F32))
    d_branch = d_second.astype(BF16)
    grad_down_bias = jnp.sum(d_branch.astype(F32), 0)

    blocks = (2, 2, 4, count, width)
    down_sent = tn(active[1], d_branch).reshape(blocks)
    d_branch = after(d_branch, down_sent)
    d_hidden = [None, gelu_back[1](nt(d_branch, down_full[1]))[0].astype(BF16)]
    up_sent = tn(d_hidden[1], normed_low).reshape(blocks)
    qkv_far = gather_second(qkv_first, 1)
    d_branch = after(d_branch, up_sent, qkv_far)
    d_hidden[0] = gelu_back[0](nt(d_branch, down_full[0]))[0].astype(BF16)
    down_held = tn(active[0], after(d_branch, d_hidden[0])).reshape(blocks) + flip(down_sent, 0)
    up_held = tn(d_hidden[0], after(normed_low, down_held)).reshape(blocks) + flip(up_sent, 0)
    d_hidden = after(d_hidden, up_held)
    d_normed = nn(d_hidden[0], up_full[0]) + nn(d_hidden[1], up_full[1]) + d_second
    grad_up_bias = jnp.concatenate([jnp.sum(part.astype(F32), 0) for part in d_hidden])
    d_first, grad_first_gain, grad_first_shift = first_back(d_normed)
    d_attended = d_first.astype(BF16)
    grad_out_bias = jnp.sum(d_attended.astype(F32), 0)
    d_mixed = nt(d_attended, out_rows).astype(BF16)

    qkv_full = heads_together(qkv_near, (qkv_far, flip(qkv_far, 0)), 3)
    q_rows, k_rows, v_rows = qkv_full
    queries = (nt(own_tokens, q_rows) + qv_full[0]).astype(BF16) * scale
    keys = nt(seq_tokens, k_rows).astype(BF16)
    values = (nt(seq_tokens, v_rows) + qv_full[1]).astype(BF16)
    d_mixed = after(d_mixed, up_held, queries, keys, values)
    scalars = jnp.concatenate([length, ((place % 2) * share)[None]])
    attn_held, column_sums, given = [], [], (d_first,)
    for half in range(2):
        near, far, sums, *given = attention_backward(
            scalars,
            half,
            (queries, keys, values, d_mixed, turned_mixed),
            (q_rows, k_rows, v_rows),
            (own_tokens, seq_tokens, d_attended),
            given,
        )
        column_sums.append(sums)
        d_mixed = after(d_mixed, far)
        blocks = (2, 2) + near.shape[1:]
        attn_held.append(near.reshape(blocks) + flip(far, 0).reshape(blocks))
    input_part = given[1]
    late = lambda x: after(x, input_part, attn_held[0])
    down_held = scatter_first(down_held, 0, late)
    up_held = scatter_first(up_held, 1, late)

    attn_held[0] = scatter_first(attn_held[0], 0)
    attn_held[1] = scatter_first(attn_held[1], 1)
    share_inputs = ShareInputs(input_part)
    late = lambda x: after(x, share_inputs.first)
    down_held = scatter_second(down_held, 0, late)
    up_held = scatter_second(up_held, 1, late)
    mlp_places = jnp.concatenate([up_held, down_held], 1)
    share_inputs.middle()
    attn_held = [scatter_second(held, half) for half, held in enumerate(attn_held)]
    attn_places = [held[i] for held in attn_held for i in range(2)]
    late = lambda x: after(x, attn_places, share_inputs.third, share_inputs.across)
    mlp_sums = scatter_places(mlp_places, late)
    mlp_all = gather_in_order(mlp_sums, (1, 2))
    attn_sums = scatter_places(attn_places, lambda x: after(x, mlp_sums))
    attn_all = gather_in_order(after(attn_sums, output), (2, 1))
    grad_tokens = share_inputs.result().T
    attn_all = attn_all.reshape(INNER, 4, heads, sub, width).transpose(1, 2, 0, 3, 4)
    attn_all = attn_all.reshape(4, columns, width)

    qv_sums = jnp.concatenate(column_sums).transpose(0, 2, 1).reshape(width, 2)
    qv_sums = heads_apart(qv_sums, 4).transpose(0, 1, 2, 3, 5, 4).reshape(4 * INNER, 2 * few)
    vector_blocks = jnp.concatenate([grad_up_bias.reshape(4 * INNER, count), qv_sums], 1)
    index = jnp.arange(4 * INNER, dtype=jnp.int32)
    apart = (index % INNER) ^ me
    step = (index // INNER + 4 - place) % 4
    order = (apart & 1) * 16 + (apart >> 2) * 8 + ((apart >> 1) & 1) * 4 + step
    vector_blocks = jnp.take(vector_blocks, order, axis=0)
    vectors = [
        grad_out_bias,
        grad_first_gain,
        grad_first_shift,
        grad_down_bias,
        grad_second_gain,
        grad_second_shift,
    ]
    small = sum_everywhere(
        jnp.concatenate([vector_blocks.reshape(-1), *vectors]).reshape(-1, 128),
        (mlp_places, attn_places, mlp_sums, attn_sums),
    ).reshape(-1)
    blocks = small[: vector_blocks.size].reshape(4, INNER, -1)
    blocks = lax.dynamic_index_in_dim(blocks, place, 0, keepdims=False)
    qv_all = blocks[:, count:].reshape(INNER, 2, heads, sub)
    small = small[small.size - 6 * width :].reshape(6, width)
    return (
        output,
        grad_tokens,
        attn_all[:3].transpose(0, 2, 1),
        qv_all.transpose(1, 2, 0, 3).reshape(2, columns),
        attn_all[3],
        small[0],
        small[1],
        small[2],
        mlp_all[:, :count].reshape(units, width).T,
        blocks[:, :count].reshape(-1),
        mlp_all[:, count:].reshape(units, width),
        small[3],
        small[4],
        small[5],
    )


def solution(mesh):
    placed = (
        P("dp", None),
        P("dp"),
        P("dp", None),
        P(None, None, "tensor"),
        P(None, "tensor"),
        P("tensor", None),
        P(),
        P(),
        P(),
        P(None, "tensor"),
        P("tensor"),
        P("tensor", None),
        P(),
        P(),
        P(),
    )
    return jax.shard_map(
        on_device,
        mesh=mesh,
        in_specs=placed,
        out_specs=(
            P("dp", None),
            P("dp", "tensor"),
            P(None, None, "tensor"),
            P(None, "tensor"),
            P("tensor", None),
            P(),
            P(),
            P(),
            P(None, "tensor"),
            P("tensor"),
            P("tensor", None),
            P(),
            P(),
            P(),
        ),
        check_vma=False,
    )
```

time: 729 us -> 614 us (0.84)
  the two profiles are of different devices: /device:TPU:25 before, /device:TPU:0 now
where the time goes in v2:
time: 614 us; the launch traced here: 604 us
  waiting for transfers between devices  219 us (36%)
  Pallas kernels  95.1 us (15%)
  other arithmetic  79.6 us (13%)
  starting transfers between devices  72.1 us (12%)
  matrix products  65.5 us (11%)
  local copies, waits for them, and re-layouts  55.5 us (9%)
  between operations  16.8 us (3%)
    ppermute x40, waiting for transfers between devices, flip(): return lax.ppermute(x, 'dp', [(i, i ^ 1 << bit) for i in range(size)])  84.9 us
    pallas_call x2, Pallas kernels, attention_backward(): pl.pallas_call(lambda *refs: backward_kernel(half == 1, *refs), grid=(pai...  58.5 us
    ppermute x15, waiting for transfers between devices, from_next(): lax.ppermute(x, 'tensor', [((i + step) % size, i) for i in range(size)])  54.5 us
    ppermute x6, waiting for transfers between devices, to_next(): lax.ppermute(x, 'tensor', [(i, (i + step) % size) for i in range(size)])  53.1 us
    dot_general x8, matrix products, nt(): lax.dot_general(left, right, (((1,), (1,)), ((), ())), preferred_element_...  36 us
    ppermute x40, starting transfers between devices, flip(): return lax.ppermute(x, 'dp', [(i, i ^ 1 << bit) for i in range(size)])  31 us
    unnamed x211, local copies, waits for them, and re-layouts  20.6 us
    pallas_call x1, Pallas kernels, attention_forward(): pl.pallas_call(forward_kernel, grid=(lengths.shape[0],), in_specs=[pl.Blo...  17.3 us
  transfers between devices with their start and end apart: 73, of which 29 were waited for; matrix products, arithmetic and copies ran while one was open for 28% of the time, Pallas kernels for 16%

profile of v2, /device:TPU:0, one launch (start us, length us, event | category | flops | bytes accessed | tf_op | source)
XLA Modules:
  0.0 603.9 jit_solution(5277047988059709970)
XLA Ops:
  13.0 5.0 collective-permute-start
  39.6 17.3 %shard_map.254 = f32[192,2048]{1,0:T(8,128)S(1)} custom-call(s32[1]{0:T(128)} %bitcast.me_ref, s32[2]{0:T(128)S(1)} %copy-done.11, bf16[2048,192]{1,0:T(8,128)(2,1)S(1)} %copy-done.10, bf16[2048,192]{1,0:T(8,128)(2,1)S(1)} %copy-done.7, bf16[2048,192]{1,0:T(8,128)(2,1)S(1)} %copy-done.9), custom_call_target="tpu_custom_call" | custom-call | flops 402653184 | bytes 4194304 | tf_op jit(solution)/shard_map/pallas_call | solution.py:327
  72.0 18.2 %collective-permute-done.7 = f32[96,768]{1,0:T(8,128)S(1)} collective-permute-done((f32[96,768]{1,0:T(8,128)S(1)}, f32[96,768]{1,0:T(8,128)S(1)}, u32[]{:S(2)}, u32[]{:S(2)}) %collective-permute-start.7) | collective-permute-done | bytes 294944 | tf_op jit(solution)/shard_map/ppermute | solution.py:57
  95.1 9.3 %collective-permute-done.10 = f32[3,48,768]{2,1,0:T(8,128)S(1)} collective-permute-done((f32[3,48,768]{2,1,0:T(8,128)S(1)}, f32[3,48,768]{2,1,0:T(8,128)S(1)}, u32[]{:S(2)}, u32[]{:S(2)}) %collective-permute-start.10) | collective-permute-done | bytes 442400 | tf_op jit(solution)/shard_map/ppermute | solution.py:52
  106.4 8.1 %collective-permute-done.15 = f32[2,3,32,768]{3,2,1,0:T(8,128)S(1)} collective-permute-done((f32[2,3,32,768]{3,2,1,0:T(8,128)S(1)}, f32[2,3,32,768]{3,2,1,0:T(8,128)S(1)}, u32[]{:S(2)}, u32[]{:S(2)}) %collective-permute-start.15) | collective-permute-done | bytes 589856 | tf_op jit(solution)/shard_map/ppermute | solution.py:52
  119.7 9.8 %collective-permute-done.3 = f32[192,512]{1,0:T(8,128)} collective-permute-done((f32[192,512]{1,0:T(8,128)S(1)}, f32[192,512]{1,0:T(8,128)}, u32[]{:S(2)}, u32[]{:S(2)}) %collective-permute-start.3) | collective-permute-done | bytes 393248 | tf_op jit(solution)/shard_map/ppermute | solution.py:57
  130.4 20.9 %collective-permute-done.4 = f32[192,512]{1,0:T(8,128)} collective-permute-done((f32[192,512]{1,0:T(8,128)S(1)}, f32[192,512]{1,0:T(8,128)}, u32[]{:S(2)}, u32[]{:S(2)}) %collective-permute-start.4) | collective-permute-done | bytes 393248 | tf_op jit(solution)/shard_map/ppermute | solution.py:57
  158.1 5.8 shard_map.255
  174.6 5.2 collective-permute-done.17
  188.2 4.7 shard_map.256
  200.2 9.8 %multiply_convert_fusion.2 = (bf16[512,1536]{1,0:T(8,128)(2,1)}, f32[512,1536]{1,0:T(8,128)}, f32[512,1536]{1,0:T(8,128)}) fusion(f32[1536]{0:T(1024)S(1)} %add.626, bf16[512,768]{1,0:T(8,128)(2,1)S(1)} %fusion.24, bf16[1536,768]{1,0:T(8,128)(2,1)S(1)} %bitcast.361), kind=kOutput, calls=%fused_computation.42 | convolution fusion | flops 1259864064 | bytes 11016192 | tf_op jit(solution)/shard_map/dot_general | solution.py:32
  213.6 11.1 %multiply_convert_fusion.1 = (bf16[512,1536]{1,0:T(8,128)(2,1)}, f32[512,1536]{1,0:T(8,128)}, f32[512,1536]{1,0:T(8,128)}) fusion(f32[1536]{0:T(1024)S(1)} %add.629, bf16[512,768]{1,0:T(8,128)(2,1)S(1)} %fusion.24, bf16[1536,768]{1,0:T(8,128)(2,1)} %bitcast.363), kind=kOutput, calls=%fused_computation.29 | convolution fusion | flops 1259864064 | bytes 11016192 | tf_op jit(solution)/shard_map/dot_general | solution.py:32
  224.7 4.6 shard_map.258
  237.0 4.4 fusion.101
  268.6 5.1 add_convert_fusion
  288.4 5.2 add.648
  308.7 28.9 %shard_map.260 = (f32[4,2,96,768]{3,2,1,0:T(8,128)}, f32[4,2,96,768]{3,2,1,0:T(8,128)}, f32[3,2,128]{2,1,0:T(2,128)}, f32[768,512]{1,0:T(8,128)}, f32[768,1024]{1,0:T(8,128)}) custom-call(s32[2]{0:T(128)} %pad_add_fusion.refs_0_, bf16[512,768]{1,0:T(8,128)(2,1)} %fusion.23.refs_1_, bf16[1024,768]{1,0:T(8,128)(2,1)} %convolution_convert_fusion.1.refs_2_, ...), custom_call_target="tpu_custom_call" | custom-call | flops 393216 | bytes 1048576 | tf_op jit(solution)/shard_map/pallas_call | solution.py:351
  345.9 29.6 %shard_map.261 = (f32[4,2,96,768]{3,2,1,0:T(8,128)}, f32[4,2,96,768]{3,2,1,0:T(8,128)}, f32[3,2,128]{2,1,0:T(2,128)}, f32[768,512]{1,0:T(8,128)}, f32[768,1024]{1,0:T(8,128)}) custom-call(s32[2]{0:T(128)} %pad_add_fusion.refs_0_, bf16[512,768]{1,0:T(8,128)(2,1)} %fusion.23.refs_1_, bf16[1024,768]{1,0:T(8,128)(2,1)} %convolution_convert_fusion.1.refs_2_, ...), custom_call_target="tpu_custom_call" | custom-call | flops 393216 | bytes 1048576 | tf_op jit(solution)/shard_map/pallas_call | solution.py:351
  381.0 4.0 collective-permute-start.42
  387.7 7.0 %collective-permute-done.51 = f32[2,4,96,768]{3,2,1,0:T(8,128)} collective-permute-done((f32[2,4,96,768]{3,2,1,0:T(8,128)}, f32[2,4,96,768]{3,2,1,0:T(8,128)}, u32[]{:S(2)}, u32[]{:S(2)}) %collective-permute-start.51) | collective-permute-done | bytes 2359328 | tf_op jit(solution)/shard_map/ppermute | solution.py:52
  404.0 9.8 %collective-permute-done.42 = f32[192,1024]{1,0:T(8,128)S(1)} collective-permute-done((f32[192,1024]{1,0:T(8,128)}, f32[192,1024]{1,0:T(8,128)S(1)}, u32[]{:S(2)}, u32[]{:S(2)}) %collective-permute-start.42) | collective-permute-done | bytes 786464 | tf_op jit(solution)/shard_map/ppermute | solution.py:383
  414.4 4.3 collective-permute-start.44
  430.5 21.9 %collective-permute-done.55 = f32[2,2,96,768]{3,2,1,0:T(8,128)S(1)} collective-permute-done((f32[2,2,96,768]{3,2,1,0:T(8,128)S(1)}, f32[2,2,96,768]{3,2,1,0:T(8,128)S(1)}, u32[]{:S(2)}, u32[]{:S(2)}) %collective-permute-start.55) | collective-permute-done | bytes 1179680 | tf_op jit(solution)/shard_map/ppermute | solution.py:52
  455.1 7.9 %collective-permute-done.47 = f32[2,96,768]{2,1,0:T(8,128)S(1)} collective-permute-done((f32[2,96,768]{2,1,0:T(8,128)S(1)}, f32[2,96,768]{2,1,0:T(8,128)S(1)}, u32[]{:S(2)}, u32[]{:S(2)}) %collective-permute-start.47) | collective-permute-done | bytes 589856 | tf_op jit(solution)/shard_map/ppermute | solution.py:52
  468.3 4.9 collective-permute-done.53
  473.2 25.3 %collective-permute-done.57 = f32[192,768]{1,0:T(8,128)S(1)} collective-permute-done((f32[192,768]{1,0:T(8,128)S(1)}, f32[192,768]{1,0:T(8,128)S(1)}, u32[]{:S(2)}, u32[]{:S(2)}) %collective-permute-start.57) | collective-permute-done | bytes 589856 | tf_op jit(solution)/shard_map/ppermute | solution.py:62
  504.8 19.9 %collective-permute-done.59 = f32[96,768]{1,0:T(8,128)S(1)} collective-permute-done((f32[96,768]{1,0:T(8,128)S(1)}, f32[96,768]{1,0:T(8,128)S(1)}, u32[]{:S(2)}, u32[]{:S(2)}) %collective-permute-start.59) | collective-permute-done | bytes 294944 | tf_op jit(solution)/shard_map/ppermute | solution.py:62
  524.9 4.9 multiply_convert_fusion
  533.0 6.6 %collective-permute-done.61 = f32[1,96,768]{2,1,0:T(8,128)S(1)} collective-permute-done((f32[1,96,768]{2,1,0:T(8,128)S(1)}, f32[1,96,768]{2,1,0:T(8,128)S(1)}, u32[]{:S(2)}, u32[]{:S(2)}) %collective-permute-start.61) | collective-permute-done | bytes 294944 | tf_op jit(solution)/shard_map/ppermute | solution.py:52
  545.9 9.7 %collective-permute-done.65 = f32[72,128]{1,0:T(8,128)} collective-permute-done((f32[72,128]{1,0:T(8,128)S(1)}, f32[72,128]{1,0:T(8,128)}, u32[]{:S(2)}, u32[]{:S(2)}) %collective-permute-start.65) | collective-permute-done | bytes 36896 | tf_op jit(solution)/shard_map/ppermute | solution.py:199
  560.1 4.3 collective-permute-done.70
  566.0 4.2 collective-permute-done.41
  (516 shorter events, 249.2 us)
Async XLA Ops:
  7.2 517.6 %all-gather.2.cloned.1.call-start = ((), (), s32[]{:S(2)}) async-start(), calls=%async_computation | async-start | bytes 7864320 | tf_op jit(solution)/shard_map/all_gather | solution.py:538
  13.0 48.8 %collective-permute-start = (f32[96,768]{1,0:T(8,128)}, f32[96,768]{1,0:T(8,128)}, u32[]{:S(2)}, u32[]{:S(2)}) collective-permute-start(f32[96,768]{1,0:T(8,128)} %get-tuple-element.76), channel_id=1, source_target_pairs={{1,0},{2,1},{3,2},{0,3},{5,4},{6,5},{7,6},{4,7},{9,8},{10,9},{11,1... | collective-permute-start | bytes 884744 | tf_op jit(solution)/shard_map/ppermute | solution.py:57
  18.0 45.9 %collective-permute-start.1 = (f32[96,768]{1,0:T(8,128)}, f32[96,768]{1,0:T(8,128)S(1)}, u32[]{:S(2)}, u32[]{:S(2)}) collective-permute-start(f32[96,768]{1,0:T(8,128)} %get-tuple-element.76), channel_id=1, source_target_pairs={{2,0},{3,1},{0,2},{1,3},{6,4},{7,5},{4,6},{5,7},{10,8},{11,9},{8,1... | collective-permute-start | bytes 884744 | tf_op jit(solution)/shard_map/ppermute | solution.py:57
  21.7 35.2 %collective-permute-start.11 = (f32[32,768]{1,0:T(8,128)}, f32[32,768]{1,0:T(8,128)S(1)}, u32[]{:S(2)}, u32[]{:S(2)}) collective-permute-start(f32[32,768]{1,0:T(8,128)} %select_maximum_fusion), channel_id=1, source_target_pairs={{1,0},{2,1},{3,2},{0,3},{5,4},{6,5},{7,6},{4,7},{9,8},{10,9},{11,1... | collective-permute-start | bytes 294920 | tf_op jit(solution)/shard_map/ppermute | solution.py:57
  22.1 34.8 %collective-permute-start.12 = (f32[32,768]{1,0:T(8,128)}, f32[32,768]{1,0:T(8,128)}, u32[]{:S(2)}, u32[]{:S(2)}) collective-permute-start(f32[32,768]{1,0:T(8,128)} %select_maximum_fusion), channel_id=1, source_target_pairs={{2,0},{3,1},{0,2},{1,3},{6,4},{7,5},{4,6},{5,7},{10,8},{11,9},{8,1... | collective-permute-start | bytes 294920 | tf_op jit(solution)/shard_map/ppermute | solution.py:57
  24.6 36.2 %collective-permute-start.13 = (f32[32,768]{1,0:T(8,128)}, f32[32,768]{1,0:T(8,128)}, u32[]{:S(2)}, u32[]{:S(2)}) collective-permute-start(f32[32,768]{1,0:T(8,128)} %select_maximum_fusion), channel_id=1, source_target_pairs={{3,0},{0,1},{1,2},{2,3},{7,4},{4,5},{5,6},{6,7},{11,8},{8,9},{9,10... | collective-permute-start | bytes 294920 | tf_op jit(solution)/shard_map/ppermute | solution.py:57
  115.7 52.7 %collective-permute-start.16 = (f32[2,2,3,32,768]{4,3,2,1,0:T(8,128)}, f32[2,2,3,32,768]{4,3,2,1,0:T(8,128)}, u32[]{:S(2)}, u32[]{:S(2)}) collective-permute-start(f32[2,2,3,32,768]{4,3,2,1,0:T(8,128)} %pad_maximum_fusion.5), channel_id=1, source_target_pairs={{0,4},{4,0},{8,12},{12,8},{16,20},{20,16},{24,28},{28,24},{1,5},{5... | collective-permute-start | bytes 3538952 | tf_op jit(solution)/shard_map/ppermute | solution.py:52
  116.6 34.7 %collective-permute-start.4 = (f32[192,512]{1,0:T(8,128)S(1)}, f32[192,512]{1,0:T(8,128)}, u32[]{:S(2)}, u32[]{:S(2)}) collective-permute-start(f32[192,512]{1,0:T(8,128)S(1)} %get-tuple-element.234), channel_id=1, source_target_pairs={{2,0},{3,1},{0,2},{1,3},{6,4},{7,5},{4,6},{5,7},{10,8},{11,9},{8,1... | collective-permute-start | bytes 1179656 | tf_op jit(solution)/shard_map/ppermute | solution.py:57
  116.6 51.8 %collective-permute-start.22 = (f32[2,3,48,768]{3,2,1,0:T(8,128)}, f32[2,3,48,768]{3,2,1,0:T(8,128)}, u32[]{:S(2)}, u32[]{:S(2)}) collective-permute-start(f32[2,3,48,768]{3,2,1,0:T(8,128)} %pad_maximum_fusion.11.b_ref), channel_id=1, source_target_pairs={{0,8},{4,12},{8,0},{12,4},{16,24},{20,28},{24,16},{28,20},{1,9},{5... | collective-permute-start | bytes 2654216 | tf_op jit(solution)/shard_map/ppermute | solution.py:52
  118.2 50.4 %collective-permute-start.21 = (f32[2,3,48,768]{3,2,1,0:T(8,128)}, f32[2,3,48,768]{3,2,1,0:T(8,128)}, u32[]{:S(2)}, u32[]{:S(2)}) collective-permute-start(f32[2,3,48,768]{3,2,1,0:T(8,128)} %pad_maximum_fusion.10.a_ref), channel_id=1, source_target_pairs={{0,16},{4,20},{8,24},{12,28},{16,0},{20,4},{24,8},{28,12},{1,17},{... | collective-permute-start | bytes 2654216 | tf_op jit(solution)/shard_map/ppermute | solution.py:52
  129.5 37.2 %collective-permute-start.5 = (f32[192,512]{1,0:T(8,128)}, f32[192,512]{1,0:T(8,128)}, u32[]{:S(2)}, u32[]{:S(2)}) collective-permute-start(f32[192,512]{1,0:T(8,128)} %get-tuple-element.233), channel_id=1, source_target_pairs={{3,0},{0,1},{1,2},{2,3},{7,4},{4,5},{5,6},{6,7},{11,8},{8,9},{9,10... | collective-permute-start | bytes 1179656 | tf_op jit(solution)/shard_map/ppermute | solution.py:57
  200.2 34.5 %collective-permute-start.33 = (f32[2,3,48,768]{3,2,1,0:T(8,128)}, f32[2,3,48,768]{3,2,1,0:T(8,128)S(1)}, u32[]{:S(2)}, u32[]{:S(2)}) collective-permute-start(f32[2,3,48,768]{3,2,1,0:T(8,128)} %pad_maximum_fusion.13.b_ref), channel_id=1, source_target_pairs={{0,4},{4,0},{8,12},{12,8},{16,20},{20,16},{24,28},{28,24},{1,5},{5... | collective-permute-start | bytes 2654216 | tf_op jit(solution)/shard_map/ppermute | solution.py:52
  230.6 31.3 %collective-permute-start.35 = (f32[2,3,72,768]{3,2,1,0:T(8,128)}, f32[2,3,72,768]{3,2,1,0:T(8,128)S(1)}, u32[]{:S(2)}, u32[]{:S(2)}) collective-permute-start(f32[2,3,72,768]{3,2,1,0:T(8,128)} %get-tuple-element.238), channel_id=1, source_target_pairs={{0,8},{4,12},{8,0},{12,4},{16,24},{20,28},{24,16},{28,20},{1,9},{5... | collective-permute-start | bytes 3981320 | tf_op jit(solution)/shard_map/ppermute | solution.py:52
  250.1 38.2 %collective-permute-start.37 = (f32[2,2,4,96,768]{4,3,2,1,0:T(8,128)}, f32[2,2,4,96,768]{4,3,2,1,0:T(8,128)}, u32[]{:S(2)}, u32[]{:S(2)}) collective-permute-start(f32[2,2,4,96,768]{4,3,2,1,0:T(8,128)} %bitcast.80), channel_id=1, source_target_pairs={{0,4},{4,0},{8,12},{12,8},{16,20},{20,16},{24,28},{28,24},{1,5},{5... | collective-permute-start | bytes 14155784 | tf_op jit(solution)/shard_map/ppermute | solution.py:52
  257.9 37.1 %collective-permute-start.38 = (f32[2,2,4,96,768]{4,3,2,1,0:T(8,128)}, f32[2,2,4,96,768]{4,3,2,1,0:T(8,128)}, u32[]{:S(2)}, u32[]{:S(2)}) collective-permute-start(f32[2,2,4,96,768]{4,3,2,1,0:T(8,128)} %bitcast.81), channel_id=1, source_target_pairs={{0,4},{4,0},{8,12},{12,8},{16,20},{20,16},{24,28},{28,24},{1,5},{5... | collective-permute-start | bytes 14155784 | tf_op jit(solution)/shard_map/ppermute | solution.py:52
  337.6 43.4 %collective-permute-start.45 = (f32[4,2,96,768]{3,2,1,0:T(8,128)}, f32[4,2,96,768]{3,2,1,0:T(8,128)}, u32[]{:S(2)}, u32[]{:S(2)}) collective-permute-start(f32[4,2,96,768]{3,2,1,0:T(8,128)} %get-tuple-element.113), channel_id=1, source_target_pairs={{0,4},{4,0},{8,12},{12,8},{16,20},{20,16},{24,28},{28,24},{1,5},{5... | collective-permute-start | bytes 7077896 | tf_op jit(solution)/shard_map/ppermute | solution.py:52
  341.2 53.5 %collective-permute-start.51 = (f32[2,4,96,768]{3,2,1,0:T(8,128)}, f32[2,4,96,768]{3,2,1,0:T(8,128)}, u32[]{:S(2)}, u32[]{:S(2)}) collective-permute-start(f32[2,4,96,768]{3,2,1,0:T(8,128)} %slice_bitcast_fusion), channel_id=1, source_target_pairs={{0,16},{4,20},{8,24},{12,28},{16,0},{20,4},{24,8},{28,12},{1,17},{... | collective-permute-start | bytes 7077896 | tf_op jit(solution)/shard_map/ppermute | solution.py:52
  344.4 53.8 %collective-permute-start.49 = (f32[2,4,96,768]{3,2,1,0:T(8,128)}, f32[2,4,96,768]{3,2,1,0:T(8,128)}, u32[]{:S(2)}, u32[]{:S(2)}) collective-permute-start(f32[2,4,96,768]{3,2,1,0:T(8,128)} %slice_bitcast_fusion.1), channel_id=1, source_target_pairs={{0,8},{4,12},{8,0},{12,4},{16,24},{20,28},{24,16},{28,20},{1,9},{5... | collective-permute-start | bytes 7077896 | tf_op jit(solution)/shard_map/ppermute | solution.py:52
  378.9 35.4 %collective-permute-start.39 = (f32[192,1024]{1,0:T(8,128)}, f32[192,1024]{1,0:T(8,128)}, u32[]{:S(2)}, u32[]{:S(2)}) collective-permute-start(f32[192,1024]{1,0:T(8,128)} %get-tuple-element.228), channel_id=1, source_target_pairs={{0,1},{1,0},{2,3},{3,2},{4,5},{5,4},{6,7},{7,6},{8,9},{9,8},{10,11... | collective-permute-start | bytes 2359304 | tf_op jit(solution)/shard_map/ppermute | solution.py:382
  381.0 32.8 %collective-permute-start.42 = (f32[192,1024]{1,0:T(8,128)}, f32[192,1024]{1,0:T(8,128)S(1)}, u32[]{:S(2)}, u32[]{:S(2)}) collective-permute-start(f32[192,1024]{1,0:T(8,128)} %get-tuple-element.227), channel_id=1, source_target_pairs={{0,1},{3,2},{4,5},{7,6},{8,9},{11,10},{12,13},{15,14},{16,17},{19,... | collective-permute-start | bytes 2359304 | tf_op jit(solution)/shard_map/ppermute | solution.py:383
  401.9 50.5 %collective-permute-start.55 = (f32[2,2,96,768]{3,2,1,0:T(8,128)S(1)}, f32[2,2,96,768]{3,2,1,0:T(8,128)S(1)}, u32[]{:S(2)}, u32[]{:S(2)}) collective-permute-start(f32[2,2,96,768]{3,2,1,0:T(8,128)S(1)} %slice_bitcast_fusion.2), channel_id=1, source_target_pairs={{0,8},{4,12},{8,0},{12,4},{16,24},{20,28},{24,16},{28,20},{1,9},{5... | collective-permute-start | bytes 3538952 | tf_op jit(solution)/shard_map/ppermute | solution.py:52
  413.8 38.8 %collective-permute-start.50 = (f32[4,96,768]{2,1,0:T(8,128)S(1)}, f32[4,96,768]{2,1,0:T(8,128)S(1)}, u32[]{:S(2)}, u32[]{:S(2)}) collective-permute-start(f32[4,96,768]{2,1,0:T(8,128)S(1)} %fusion.32), channel_id=1, source_target_pairs={{0,16},{4,20},{8,24},{12,28},{16,0},{20,4},{24,8},{28,12},{1,17},{... | collective-permute-start | bytes 3538952 | tf_op jit(solution)/shard_map/ppermute | solution.py:52
  414.4 49.4 %collective-permute-start.44 = (f32[192,1024]{1,0:T(8,128)S(1)}, f32[192,1024]{1,0:T(8,128)S(1)}, u32[]{:S(2)}, u32[]{:S(2)}) collective-permute-start(f32[192,1024]{1,0:T(8,128)S(1)} %copy-done.49), channel_id=1, source_target_pairs={{0,1},{3,2},{4,5},{7,6},{8,9},{11,10},{12,13},{15,14},{16,17},{19,... | collective-permute-start | bytes 2359304 | tf_op jit(solution)/shard_map/ppermute | solution.py:388
  423.7 42.3 %collective-permute-start.43 = (f32[192,1024]{1,0:T(8,128)S(1)}, f32[192,1024]{1,0:T(8,128)S(1)}, u32[]{:S(2)}, u32[]{:S(2)}) collective-permute-start(f32[192,1024]{1,0:T(8,128)S(1)} %add.656), channel_id=1, source_target_pairs={{1,2},{2,1},{5,6},{6,5},{9,10},{10,9},{13,14},{14,13},{17,18},{18,... | collective-permute-start | bytes 2359304 | tf_op jit(solution)/shard_map/ppermute | solution.py:389
  427.2 35.8 %collective-permute-start.47 = (f32[2,96,768]{2,1,0:T(8,128)S(1)}, f32[2,96,768]{2,1,0:T(8,128)S(1)}, u32[]{:S(2)}, u32[]{:S(2)}) collective-permute-start(f32[2,96,768]{2,1,0:T(8,128)S(1)} %fusion.54), channel_id=1, source_target_pairs={{0,8},{4,12},{8,0},{12,4},{16,24},{20,28},{24,16},{28,20},{1,9},{5... | collective-permute-start | bytes 1769480 | tf_op jit(solution)/shard_map/ppermute | solution.py:52
  463.0 35.6 %collective-permute-start.57 = (f32[192,768]{1,0:T(8,128)S(1)}, f32[192,768]{1,0:T(8,128)S(1)}, u32[]{:S(2)}, u32[]{:S(2)}) collective-permute-start(f32[192,768]{1,0:T(8,128)S(1)} %get-tuple-element.230), channel_id=1, source_target_pairs={{0,2},{1,3},{2,0},{3,1},{4,6},{5,7},{6,4},{7,5},{8,10},{9,11},{10,... | collective-permute-start | bytes 1769480 | tf_op jit(solution)/shard_map/ppermute | solution.py:62
  463.7 36.4 %collective-permute-start.58 = (f32[192,768]{1,0:T(8,128)S(1)}, f32[192,768]{1,0:T(8,128)S(1)}, u32[]{:S(2)}, u32[]{:S(2)}) collective-permute-start(f32[192,768]{1,0:T(8,128)S(1)} %get-tuple-element.231), channel_id=1, source_target_pairs={{0,3},{1,0},{2,1},{3,2},{4,7},{5,4},{6,5},{7,6},{8,11},{9,8},{10,9... | collective-permute-start | bytes 1769480 | tf_op jit(solution)/shard_map/ppermute | solution.py:62
  463.9 40.9 %collective-permute-start.48 = (f32[96,768]{1,0:T(8,128)S(1)}, f32[96,768]{1,0:T(8,128)S(1)}, u32[]{:S(2)}, u32[]{:S(2)}) collective-permute-start(f32[96,768]{1,0:T(8,128)S(1)} %slice_bitcast_fusion.18), channel_id=1, source_target_pairs={{0,1},{1,2},{2,3},{3,0},{4,5},{5,6},{6,7},{7,4},{8,9},{9,10},{10,1... | collective-permute-start | bytes 884744 | tf_op jit(solution)/shard_map/ppermute | solution.py:62
  465.9 58.8 %collective-permute-start.59 = (f32[96,768]{1,0:T(8,128)S(1)}, f32[96,768]{1,0:T(8,128)S(1)}, u32[]{:S(2)}, u32[]{:S(2)}) collective-permute-start(f32[96,768]{1,0:T(8,128)S(1)} %get-tuple-element.239), channel_id=1, source_target_pairs={{0,2},{1,3},{2,0},{3,1},{4,6},{5,7},{6,4},{7,5},{8,10},{9,11},{10,... | collective-permute-start | bytes 884744 | tf_op jit(solution)/shard_map/ppermute | solution.py:62
  473.2 51.5 %collective-permute-start.60 = (f32[96,768]{1,0:T(8,128)S(1)}, f32[96,768]{1,0:T(8,128)S(1)}, u32[]{:S(2)}, u32[]{:S(2)}) collective-permute-start(f32[96,768]{1,0:T(8,128)S(1)} %get-tuple-element.240), channel_id=1, source_target_pairs={{0,3},{1,0},{2,1},{3,2},{4,7},{5,4},{6,5},{7,6},{8,11},{9,8},{10,9... | collective-permute-start | bytes 884744 | tf_op jit(solution)/shard_map/ppermute | solution.py:62
  498.5 45.3 %collective-permute-start.40 = (f32[192,1024]{1,0:T(8,128)}, f32[192,1024]{1,0:T(8,128)}, u32[]{:S(2)}, u32[]{:S(2)}) collective-permute-start(f32[192,1024]{1,0:T(8,128)} %bitcast_add_fusion.1), channel_id=1, source_target_pairs={{1,2},{2,1},{5,6},{6,5},{9,10},{10,9},{13,14},{14,13},{17,18},{18,... | collective-permute-start | bytes 2359304 | tf_op jit(solution)/shard_map/ppermute | solution.py:387
  532.4 31.9 %collective-permute-start.70 = (f32[2,192,768]{2,1,0:T(8,128)}, f32[2,192,768]{2,1,0:T(8,128)S(1)}, u32[]{:S(2)}, u32[]{:S(2)}) collective-permute-start(f32[2,192,768]{2,1,0:T(8,128)} %pad_maximum_fusion.9), channel_id=1, source_target_pairs={{0,16},{4,20},{8,24},{12,28},{16,0},{20,4},{24,8},{28,12},{1,17},{... | collective-permute-start | bytes 3538952 | tf_op jit(solution)/shard_map/ppermute | solution.py:52
  (137 other events, 1489.5 us)
Sparse Core Ops, SparseCore 0:
  267.3 113.7 all-gather.1

commit v3 on v2

v3 whole, which is shorter than its diff:
```python
import jax
import jax.numpy as jnp
from jax import lax
from jax.experimental import pallas as pl
from jax.experimental.pallas import tpu as pltpu
from jax.sharding import PartitionSpec as P

HD = 64
EPS = 1e-05
MASKED = -1000000000.0
BITS = 3
INNER = 1 << BITS
F32 = jnp.float32
BF16 = jnp.bfloat16


def layer_norm(hidden, gain, shift):
    center = hidden - jnp.mean(hidden, -1, keepdims=True)
    spread = jnp.mean(center * center, -1, keepdims=True)
    return center * lax.rsqrt(spread + EPS) * gain + shift


def exact_gelu(inputs):
    return jax.nn.gelu(inputs, approximate=False)


def nn(left, right):
    return lax.dot_general(left, right, (((1,), (0,)), ((), ())), preferred_element_type=F32)


def nt(left, right):
    return lax.dot_general(left, right, (((1,), (1,)), ((), ())), preferred_element_type=F32)


def tn(left, right):
    return lax.dot_general(left, right, (((0,), (0,)), ((), ())), preferred_element_type=F32)


APART = [c | (x << 1) | (y << 2) for c in (0, 1) for y in (0, 1) for x in (0, 1)]


def unit(lengths):
    return jnp.where(lengths[0] > 0, 1.0, 0.0).astype(F32)


def after(x, *others):
    return lax.optimization_barrier((x, others))[0]


def flip(x, bit):
    size = lax.axis_size("dp")
    return lax.ppermute(x, "dp", [(i, i ^ (1 << bit)) for i in range(size)])


def from_next(x, step):
    size = lax.axis_size("tensor")
    return lax.ppermute(x, "tensor", [((i + step) % size, i) for i in range(size)])


def to_next(x, step):
    size = lax.axis_size("tensor")
    return lax.ppermute(x, "tensor", [(i, (i + step) % size) for i in range(size)])


def relative(x, axis):
    me = lax.axis_index("dp") % INNER
    return jnp.concatenate([lax.dynamic_slice_in_dim(x, me ^ apart, 1, axis) for apart in APART], axis)


def owner(core, step, me_ref):
    return me_ref[0] ^ (core | ((step % 2) << 1) | ((step // 2) << 2))


def heads_kernel(me_ref, near_a_ref, near_b_ref, *refs):
    parts, out_ref = (refs[:4], refs[4:8]), refs[8]
    kinds, places, heads = out_ref.shape[:3]
    sub = near_a_ref.shape[2]

    def block(near_ref, held, kind, at, head):
        if at == 0:
            return near_ref[kind * heads + head, 0]
        rows = pl.ds((kind % 2 * heads + head) * sub, sub)
        return held[kind // 2][0, at - 1, rows, :]

    for step in range(4):

        @pl.when(pl.program_id(0) == step)
        def _():
            own, other = [(held[step // 2], held[2 + step % 2]) for held in parts]
            for kind in range(kinds):
                for at in range(places):
                    for head in range(heads):
                        pair = [
                            block(near_a_ref, own, kind, at, head),
                            block(near_b_ref, other, kind, at, head),
                        ]
                        out_ref[kind, at, head, 0] = jnp.concatenate(pair, 0).astype(BF16)


def part_specs(parts):
    by_x = pl.BlockSpec((1,) + parts[0].shape[1:], lambda k, me_ref: (k % 2, 0, 0, 0))
    by_y = pl.BlockSpec((1,) + parts[2].shape[1:], lambda k, me_ref: (k // 2, 0, 0, 0))
    return [by_x, by_x, by_y, by_y]


def heads_together(me, near, own, other):
    count, _, sub, width = near.shape
    heads = count // 4
    near_spec = lambda core: pl.BlockSpec(
        (count, 1, sub, width), lambda k, me_ref: (0, owner(core, k, me_ref), 0, 0)
    )
    full = pl.pallas_call(
        heads_kernel,
        grid_spec=pltpu.PrefetchScalarGridSpec(
            num_scalar_prefetch=1,
            grid=(4,),
            in_specs=[near_spec(0), near_spec(1)] + part_specs(own) + part_specs(other),
            out_specs=pl.BlockSpec((4, 4, heads, 1, 2 * sub, width), lambda k, me_ref: (0, 0, 0, k, 0, 0)),
        ),
        out_shape=jax.ShapeDtypeStruct((4, 4, heads, 4, 2 * sub, width), BF16),
        compiler_params=pltpu.CompilerParams(vmem_limit_bytes=48 * 2**20),
    )(me, near, near, *own, *other)
    return full.reshape(4, 4 * heads * INNER * sub, width)


def units_kernel(me_ref, near_ref, a_ref, a_far_ref, b_ref, b_far_ref, out_ref):
    step = pl.program_id(0)
    half = a_ref.shape[2]
    out_ref[0, 0] = near_ref[0]

    @pl.when(step < 2)
    def _():
        out_ref[0, 1:, :half] = a_ref[0].astype(BF16)

    @pl.when(step >= 2)
    def _():
        out_ref[0, 1:, :half] = a_far_ref[0].astype(BF16)

    @pl.when(step % 2 == 0)
    def _():
        out_ref[0, 1:, half:] = b_ref[0].astype(BF16)

    @pl.when(step % 2 == 1)
    def _():
        out_ref[0, 1:, half:] = b_far_ref[0].astype(BF16)


def units_together(me, near, core, parts):
    count, width = near.shape[1:]
    full = pl.pallas_call(
        units_kernel,
        grid_spec=pltpu.PrefetchScalarGridSpec(
            num_scalar_prefetch=1,
            grid=(4,),
            in_specs=[pl.BlockSpec((1, count, width), lambda k, me_ref: (owner(core, k, me_ref), 0, 0))]
            + part_specs(parts),
            out_specs=pl.BlockSpec((1, 4, count, width), lambda k, me_ref: (k, 0, 0, 0)),
        ),
        out_shape=jax.ShapeDtypeStruct((4, 4, count, width), BF16),
        compiler_params=pltpu.CompilerParams(vmem_limit_bytes=48 * 2**20),
    )(me, near, *parts)
    return full.reshape(16 * count, width)


def gather_halves(piece, half):
    places = [from_next(piece, step) for step in (1, 2, 3)]
    return [jnp.stack([place[:half] for place in places]), jnp.stack([place[half:] for place in places])]


def both_first(places, recv=lambda x: x):
    return [jnp.stack([held, recv(flip(held, bit))]) for held, bit in zip(places, (1, 2))]


def both_second(held, recv=lambda x: x):
    return [held[0], recv(flip(held[0], 2)), held[1], recv(flip(held[1], 1))]


def scatter_first(held, route, recv=lambda x: x):
    if route:
        got = recv(flip(held[:, 1], 1))
        return held[0, 0] + got[0], held[1, 0] + got[1]
    got = recv(flip(held[1], 2))
    return held[0, 0] + got[0], held[0, 1] + got[1]


def scatter_second(parts, route, recv=lambda x: x):
    return parts[0] + recv(flip(parts[1], 2 if route else 1))


def scatter_place(total, places, step, recv=lambda x: x):
    return places[step] + recv(to_next(total, 1))


def scatter_outer(total):
    bit = BITS
    while (1 << bit) < lax.axis_size("dp"):
        total = total + flip(total, bit)
        bit += 1
    return total


def gather_in_order(piece, order, others=()):
    held = piece[None]
    for bit in (*order, 0):
        if bit == 0 and others:
            held = after(held, others)
        held = jnp.concatenate([held, flip(held, bit)], 0)
    me = lax.axis_index("dp") % INNER
    blocks = []
    for index in range(INNER):
        apart = me ^ index
        place = sum(((apart >> bit) & 1) << at for at, bit in enumerate((*order, 0)))
        blocks.append(lax.dynamic_index_in_dim(held, place, 0))
    return jnp.concatenate(blocks, 0)


def sum_everywhere(x, others):
    others = list(others)
    for axis in ("dp", "tensor"):
        size = lax.axis_size(axis)
        step = 1
        while step < size:
            got = lax.ppermute(x, axis, [(i, i ^ step) for i in range(size)])
            x = x + (after(got, others.pop(0)) if others else got)
            step *= 2
    return x


CHUNK = 256


def lane_masks(width):
    lane = lax.broadcasted_iota(jnp.int32, (1, width), 1)
    return [(lane >= start) & (lane < start + HD) for start in range(0, width, HD)]


def keep(mask, x):
    return jnp.where(mask, x, jnp.zeros_like(x))


def softmax_turned(keys, query, valid):
    scores = jnp.where(valid, nt(keys, query), MASKED)
    expo = jnp.exp(scores - jnp.max(scores, 0, keepdims=True))
    return expo * (1.0 / jnp.sum(expo, 0, keepdims=True))


def forward_kernel(length_ref, q_ref, k_ref, v_ref, mixed_ref):
    keys = k_ref.shape[0]
    valid = lax.broadcasted_iota(jnp.int32, (keys, 1), 0) < length_ref[0]
    masks = lane_masks(q_ref.shape[1])
    turned = v_ref[...].T
    for start in range(0, q_ref.shape[0], CHUNK):
        rows = pl.ds(start, CHUNK)
        for head, mask in enumerate(masks):
            probs = softmax_turned(k_ref[...], keep(mask, q_ref[rows, :]), valid).astype(BF16)
            own = slice(head * HD, (head + 1) * HD)
            mixed_ref[own, rows] = nn(turned[own, :], probs).astype(BF16)


def backward_kernel(
    scalars_ref,
    q_ref,
    k_ref,
    v_ref,
    dm_ref,
    mixed_ref,
    wq_ref,
    wk_ref,
    wv_ref,
    own_ref,
    seq_ref,
    da_ref,
    first_ref,
    near_ref,
    far_ref,
    sums_ref,
    seq_part_ref,
    own_part_ref,
    dk_sum,
    dv_sum,
    dq_all,
    dq_turned,
):
    keys = k_ref.shape[0]
    queries = q_ref.shape[0]
    step = pl.program_id(0)
    valid = lax.broadcasted_iota(jnp.int32, (keys, 1), 0) < scalars_ref[0]
    masks = lane_masks(q_ref.shape[1])
    turned = k_ref[...].T
    for start in range(0, queries, CHUNK):
        rows = pl.ds(start, CHUNK)
        parts = []
        for head, mask in enumerate(masks):
            query = keep(mask, q_ref[rows, :])
            d_mixed = keep(mask, dm_ref[rows, :])
            probs = softmax_turned(k_ref[...], query, valid)
            d_values = nn(probs.astype(BF16), d_mixed)
            d_probs = nt(v_ref[...], d_mixed)
            row_dot = jnp.sum(d_probs * probs, 0, keepdims=True)
            d_scores = (probs * (d_probs - row_dot)).astype(BF16)
            d_keys = nn(d_scores, query)
            parts.append(nn(turned[head * HD : (head + 1) * HD, :], d_scores))
            if start == 0 and head == 0:
                dk_sum[...] = d_keys
                dv_sum[...] = d_values
            else:
                dk_sum[...] += d_keys
                dv_sum[...] += d_values
        part = jnp.concatenate(parts, 0) * HD ** (-0.5)
        dq_turned[:, rows] = part.astype(BF16)
        dq_all[rows, :] = part.T.astype(BF16)
    d_queries = dq_all[...]
    d_keys = dk_sum[...].astype(BF16)
    d_values = dv_sum[...].astype(BF16)
    keys_turned, values_turned = d_keys.T, d_values.T
    sums_ref[0, 0:1] = jnp.sum(d_queries.astype(F32), 0, keepdims=True)
    sums_ref[0, 1:2] = jnp.sum(d_values.astype(F32), 0, keepdims=True)

    sub = HD // INNER
    heads = near_ref.shape[2] // (4 * sub)
    grads = [
        nn(dq_turned[...], own_ref[...]),
        nn(keys_turned, seq_ref[...]),
        nn(values_turned, seq_ref[...]),
        nn(mixed_ref[...], da_ref[...]),
    ]
    for which in range(2):
        head = 2 * step + which
        place = head // heads
        for kind, grad in enumerate(grads):
            rows = pl.ds(pl.multiple_of((kind * heads + head % heads) * sub, sub), sub)
            for block in range(INNER):
                target = far_ref if block % 2 else near_ref
                at = which * HD + block * sub
                target[block // 2, place, rows, :] = grad[at : at + sub, :]

    own_part = tn(wq_ref[...], dq_turned[...])
    seq_part = tn(wk_ref[...], keys_turned) + tn(wv_ref[...], values_turned)

    @pl.when(step == 0)
    def _():
        own_part_ref[...] = own_part + first_ref[...].T
        seq_part_ref[...] = seq_part

    @pl.when(step > 0)
    def _():
        own_part_ref[...] += own_part
        seq_part_ref[...] += seq_part

    @pl.when(step == pl.num_programs(0) - 1)
    def _():
        own = pl.ds(pl.multiple_of(scalars_ref[1], CHUNK), queries)
        seq_part_ref[:, own] += own_part_ref[...]


def attention_forward(length, queries, keys, values):
    count, width = queries.shape
    columns = lambda array: pl.BlockSpec((array.shape[0], 2 * HD), lambda j: (0, j))
    return pl.pallas_call(
        forward_kernel,
        grid=(width // (2 * HD),),
        in_specs=[pl.BlockSpec(memory_space=pltpu.SMEM)]
        + [columns(array) for array in (queries, keys, values)],
        out_specs=pl.BlockSpec((2 * HD, count), lambda j: (j, 0)),
        out_shape=jax.ShapeDtypeStruct((width, count), BF16),
        compiler_params=pltpu.CompilerParams(vmem_limit_bytes=48 * 2**20),
        cost_estimate=pl.CostEstimate(flops=count * width, bytes_accessed=2**20, transcendentals=0),
    )(length, queries, keys, values)


def attention_backward(scalars, in_pairs, weights, whole):
    queries, keys, values, d_mixed, mixed = in_pairs
    count, width = queries.shape
    long = keys.shape[0]
    pairs = width // (2 * HD)
    columns = lambda array: pl.BlockSpec((array.shape[0], 2 * HD), lambda j: (0, j))
    of_rows = lambda array: pl.BlockSpec((2 * HD, array.shape[1]), lambda j: (j, 0))
    full = lambda array: pl.BlockSpec(array.shape, lambda j: (0,) * len(array.shape))
    sent = jax.ShapeDtypeStruct((INNER // 2, 4, width // INNER, width), F32)
    part = jax.ShapeDtypeStruct((width, long), F32)
    return pl.pallas_call(
        backward_kernel,
        grid=(pairs,),
        in_specs=[pl.BlockSpec(memory_space=pltpu.SMEM)]
        + [columns(array) for array in (queries, keys, values, d_mixed)]
        + [of_rows(array) for array in (mixed, *weights)]
        + [full(array) for array in whole],
        out_specs=[full(sent), full(sent), pl.BlockSpec((1, 2, 2 * HD), lambda j: (j, 0, 0)), full(part)],
        out_shape=[sent, sent, jax.ShapeDtypeStruct((pairs, 2, 2 * HD), F32), part],
        scratch_shapes=[
            pltpu.VMEM((width, count), F32),
            pltpu.VMEM((long, 2 * HD), F32),
            pltpu.VMEM((long, 2 * HD), F32),
            pltpu.VMEM((count, 2 * HD), BF16),
            pltpu.VMEM((2 * HD, count), BF16),
        ],
        compiler_params=pltpu.CompilerParams(vmem_limit_bytes=56 * 2**20),
        cost_estimate=pl.CostEstimate(flops=count * width, bytes_accessed=2**20, transcendentals=0),
    )(scalars, queries, keys, values, d_mixed, mixed, *weights, *whole)


class ShareInputs:
    def __init__(self, part):
        quarters = part.reshape((4, part.shape[0] // 4, part.shape[1]))
        place = lax.axis_index("tensor")
        self.flipped = place >= 2
        end = jnp.where(self.flipped, 3, 0)
        near = lambda i: lax.dynamic_index_in_dim(quarters, jnp.abs(end - i), 0, keepdims=False)
        self.near = [near(i) for i in range(4)]
        self.outer = (place == 0) | (place == 3)
        swap = [(0, 1), (1, 0), (2, 3), (3, 2)]
        self.first = lax.ppermute(near(jnp.where(self.outer, 3, 0)), "tensor", swap)
        self.second = lax.ppermute(self.near[2], "tensor", [(0, 1), (3, 2)])

    def second_there(self, first):
        self.far_sum = self.near[3] + first
        self.far = lax.ppermute(self.far_sum, "tensor", [(1, 2), (2, 1)])
        self.third = lax.ppermute(self.near[1], "tensor", [(0, 1), (3, 2)])

    def middle(self):
        self.across = lax.ppermute(self.near[2] + self.second, "tensor", [(1, 2), (2, 1)])

    def result(self):
        last = lax.ppermute(self.far, "tensor", [(2, 3), (1, 0)])
        mine = jnp.where(self.outer, self.near[0] + self.first, self.near[1] + self.third)
        theirs = jnp.where(self.outer, last, self.across)
        return jnp.concatenate(
            [jnp.where(self.flipped, theirs, mine), jnp.where(self.flipped, mine, theirs)], 1
        )


def on_device(
    tokens,
    lengths,
    cotangent,
    qkv_weight,
    qv_bias,
    out_weight,
    out_bias,
    first_gain,
    first_shift,
    up_weight,
    up_bias,
    down_weight,
    down_bias,
    second_gain,
    second_shift,
):
    rows, width = tokens.shape
    seq = rows // lengths.shape[0]
    columns = qkv_weight.shape[2]
    heads = columns // HD
    units = up_weight.shape[1]
    share = rows // 4
    sub = HD // INNER
    count = units // INNER
    scale = jnp.asarray(HD ** (-0.5), BF16)
    place = lax.axis_index("tensor")
    me = lax.axis_index("dp") % INNER
    one = unit(lengths)

    few = heads * sub
    all_heads = jnp.concatenate([qkv_weight.transpose(0, 2, 1), out_weight[None]]).astype(F32) * one
    all_heads = all_heads.reshape(4 * heads, INNER, sub, width)
    qv_heads = qv_bias.reshape(2, heads, INNER, sub)
    up_turned = up_weight.T.reshape(INNER, count, width)
    down_blocks = down_weight.reshape(INNER, count, width)
    up_bias_blocks = up_bias.reshape(INNER, count)
    mine = lambda x, axis: lax.dynamic_index_in_dim(x, me, axis, keepdims=False)
    vectors = jnp.concatenate([mine(up_bias_blocks, 0), mine(qv_heads, 2).reshape(-1)])
    heads_piece = mine(all_heads, 1).reshape(4 * few, width)
    vector_rows = jnp.pad(vectors[None], ((0, 7), (0, width - vectors.shape[0])))
    heads_piece = jnp.concatenate([heads_piece[: 2 * few], vector_rows, heads_piece[2 * few :]])
    up_piece = mine(up_turned, 0).astype(F32) * one
    down_piece = mine(down_blocks, 0).astype(F32) * one

    heads_places = gather_halves(heads_piece, 2 * few + 8)
    heads_first = both_first(heads_places)
    up_places = gather_halves(after(up_piece, heads_places), count // 2)
    heads_far = both_second(heads_first)
    heads_other = [flip(part, 0) for part in heads_far]

    spot = (slice(None), slice(None), 2 * few, slice(vectors.shape[0]))
    small_far = jnp.stack([jnp.stack([part[spot] for part in far[:2]]) for far in (heads_far, heads_other)])
    up_bias_near = relative(up_bias_blocks, 0).reshape(2, 2, 2, 1, count)
    up_bias_full = jnp.concatenate([up_bias_near, small_far[..., :count]], 3).reshape(2, 2 * units)
    qv_far = small_far[..., count:].reshape(2, 2, 2, 3, 2, heads, sub)
    qv_near = relative(qv_heads, 2).reshape(2, heads, 2, 2, 2, sub).transpose(0, 1, 3, 4, 2, 5)
    qv_full = [qv_near.reshape(2, columns), qv_far.transpose(4, 3, 5, 1, 2, 0, 6).reshape(2, 3 * columns)]
    qv_full = jnp.concatenate(qv_full, 1)

    def heads_apart(array, places):
        trail = array.shape[1:]
        both = array.reshape((places, heads, 2, 2, 2, sub) + trail)
        both = both.transpose((4, 2, 3, 0, 1, 5) + tuple(range(6, 6 + len(trail))))
        return both.reshape((2, 2, 2, places, few) + trail)

    which = place // 2
    length = lax.dynamic_slice_in_dim(lengths, which, 1, 0)
    seq_tokens = lax.dynamic_slice_in_dim(tokens, which * seq, seq, 0)
    own_tokens = lax.dynamic_slice_in_dim(tokens, place * share, share, 0)
    own_cotangent = lax.dynamic_slice_in_dim(cotangent, place * share, share, 0)
    whole_heads = heads_together(me[None], all_heads, heads_far, heads_other)
    down_places = gather_halves(after(down_piece, up_places, whole_heads), count // 2)
    up_first = both_first(after(up_places, heads_far), lambda x: after(x, whole_heads))
    q_rows, k_rows, v_rows, out_rows = after(whole_heads, up_first)
    queries = (nt(own_tokens, q_rows) + qv_full[0]).astype(BF16) * scale
    keys = nt(seq_tokens, k_rows).astype(BF16)
    values = (nt(seq_tokens, v_rows) + qv_full[1]).astype(BF16)
    turned_mixed = attention_forward(length, after(queries, down_places, keys, values), keys, values)
    late = lambda x: after(x, turned_mixed)
    up_far = both_second(up_first, late)
    down_first = both_first(after(down_places, up_first), late)
    turned_mixed = after(turned_mixed, up_far, down_first)
    up_other = [flip(part, 0) for part in up_far]
    first = own_tokens.astype(F32) + (tn(turned_mixed, out_rows) + out_bias)
    normed, first_back = jax.vjp(layer_norm, first, first_gain, first_shift)
    normed_low = normed.astype(BF16)

    up_full = [units_together(me[None], up_turned, core, parts) for core, parts in enumerate((up_far, up_other))]
    hidden, active, gelu_back = [], [], []
    down_far = None
    for core in range(2):
        hidden.append(nt(normed_low, up_full[core]) + up_bias_full[core])
        value, back = jax.vjp(exact_gelu, hidden[core])
        active.append(value.astype(BF16))
        gelu_back.append(back)
        if core == 0:
            down_far = both_second(down_first, lambda x: after(x, active[0]))
        normed_low = after(normed_low, active[core], down_far)
    down_other = [flip(part, 0) for part in down_far]
    down_full = [units_together(me[None], down_blocks, 0, down_far)]
    branch = nn(after(active[0], active[1]), down_full[0])
    down_full.append(units_together(me[None], down_blocks, 1, after(down_other, branch)))
    branch = branch + nn(active[1], down_full[1])
    second = normed + (branch + down_bias)
    result, second_back = jax.vjp(layer_norm, second, second_gain, second_shift)
    gathered = lax.all_gather(result, "tensor", axis=0, tiled=True)

    d_second, grad_second_gain, grad_second_shift = second_back(own_cotangent.astype(F32))
    d_branch = d_second.astype(BF16)
    grad_down_bias = jnp.sum(d_branch.astype(F32), 0)

    blocks = (2, 2, 4, count, width)
    down_sent = tn(active[1], d_branch)
    d_branch = after(d_branch, down_sent)
    d_hidden = [None, gelu_back[1](nt(d_branch, down_full[1]))[0].astype(BF16)]
    up_sent = tn(d_hidden[1], normed_low)
    d_branch = after(d_branch, up_sent)
    d_hidden[0] = gelu_back[0](nt(d_branch, down_full[0]))[0].astype(BF16)
    down_held = (tn(active[0], after(d_branch, d_hidden[0])) + flip(down_sent, 0)).reshape(blocks)
    up_held = (tn(d_hidden[0], after(normed_low, down_held)) + flip(up_sent, 0)).reshape(blocks)
    d_hidden = after(d_hidden, up_held)
    d_normed = nn(d_hidden[0], up_full[0]) + nn(d_hidden[1], up_full[1]) + d_second
    grad_up_bias = jnp.concatenate([jnp.sum(part.astype(F32), 0) for part in d_hidden])
    d_first, grad_first_gain, grad_first_shift = first_back(d_normed)
    d_attended = d_first.astype(BF16)
    grad_out_bias = jnp.sum(d_attended.astype(F32), 0)
    d_mixed = nt(d_attended, out_rows).astype(BF16)

    d_mixed = after(d_mixed, up_held)
    scalars = jnp.concatenate([length, ((place % 2) * share)[None]])
    near, far, column_sums, input_part = attention_backward(
        scalars,
        (queries, keys, values, d_mixed, turned_mixed),
        (q_rows, k_rows, v_rows),
        (own_tokens, seq_tokens, d_attended, d_first),
    )

    late = lambda x: after(x, input_part)
    down_held = scatter_first(down_held, 0, late)
    up_held = scatter_first(up_held, 1, late)
    near, far, column_sums, input_part = after(
        (near, far, column_sums, input_part), down_held, up_held, gathered
    )
    output = (gathered * one).astype(BF16)
    got = flip(far, 0)
    cut = lambda array, half: array[:, 2 * half : 2 * half + 2].reshape((2, 2, 2) + array.shape[2:])
    attn_held = [cut(near, half) + cut(got, half) for half in range(2)]
    attn_sent = attn_held
    share_inputs = ShareInputs(input_part)
    late = lambda x: after(x, attn_held)
    down_held = scatter_second(down_held, 0, late)
    up_held = scatter_second(up_held, 1, late)
    mlp_places = jnp.concatenate([up_held, down_held], 1)
    share_inputs.second_there(after(share_inputs.first, mlp_places))
    mlp_sums = scatter_place(mlp_places[3], mlp_places, 2)
    late = lambda x: after(x, share_inputs.far_sum)
    attn_held = [scatter_first(held, half, late) for half, held in enumerate(attn_held)]
    mlp_sums = scatter_place(after(mlp_sums, attn_held), mlp_places, 1)
    late = lambda x: after(x, mlp_sums)
    attn_held = [scatter_second(held, half, late) for half, held in enumerate(attn_held)]
    qv_sums = column_sums.transpose(0, 2, 1).reshape(width, 2)
    qv_sums = heads_apart(qv_sums, 4).transpose(0, 1, 2, 3, 5, 4).reshape(4 * INNER, 2 * few)
    vector_blocks = jnp.concatenate([grad_up_bias.reshape(4 * INNER, count), qv_sums], 1)
    index = jnp.arange(4 * INNER, dtype=jnp.int32)
    apart = (index % INNER) ^ me
    step = (index // INNER + 4 - place) % 4
    order = (apart & 1) * 16 + (apart >> 2) * 8 + ((apart >> 1) & 1) * 4 + step
    vector_blocks = jnp.take(vector_blocks, order, axis=0)
    vectors = [
        grad_out_bias,
        grad_first_gain,
        grad_first_shift,
        grad_down_bias,
        grad_second_gain,
        grad_second_shift,
    ]
    small_sum = sum_everywhere(
        jnp.concatenate([vector_blocks.reshape(-1), *vectors]).reshape(-1, 128),
        (attn_sent, mlp_places, mlp_sums),
    )
    small = small_sum.reshape(-1)
    attn_held = after(attn_held, small_sum)
    attn_places = [held[i] for held in attn_held for i in range(2)]
    share_inputs.middle()
    mlp_sums = scatter_place(mlp_sums, mlp_places, 0, lambda x: after(x, attn_places))
    mlp_sums = scatter_outer(mlp_sums)
    attn_sums = attn_places[3]
    for step in (2, 1, 0):
        attn_sums = scatter_place(attn_sums, attn_places, step)
    attn_sums = scatter_outer(attn_sums)
    mlp_all = gather_in_order(mlp_sums, (1, 2))
    grad_up = mlp_all[:, :count].reshape(units, width).T
    grad_down = mlp_all[:, count:].reshape(units, width)
    attn_all = gather_in_order(after(attn_sums, output), (2, 1), (grad_up, grad_down))
    grad_tokens = share_inputs.result().T
    attn_all = attn_all.reshape(INNER, 4, heads, sub, width).transpose(1, 2, 0, 3, 4)
    attn_all = attn_all.reshape(4, columns, width)

    blocks = small[: vector_blocks.size].reshape(4, INNER, -1)
    blocks = lax.dynamic_index_in_dim(blocks, place, 0, keepdims=False)
    qv_all = blocks[:, count:].reshape(INNER, 2, heads, sub)
    small = small[small.size - 6 * width :].reshape(6, width)
    return (
        output,
        grad_tokens,
        attn_all[:3].transpose(0, 2, 1),
        qv_all.transpose(1, 2, 0, 3).reshape(2, columns),
        attn_all[3],
        small[0],
        small[1],
        small[2],
        grad_up,
        blocks[:, :count].reshape(-1),
        grad_down,
        small[3],
        small[4],
        small[5],
    )


def solution(mesh):
    placed = (
        P("dp", None),
        P("dp"),
        P("dp", None),
        P(None, None, "tensor"),
        P(None, "tensor"),
        P("tensor", None),
        P(),
        P(),
        P(),
        P(None, "tensor"),
        P("tensor"),
        P("tensor", None),
        P(),
        P(),
        P(),
    )
    return jax.shard_map(
        on_device,
        mesh=mesh,
        in_specs=placed,
        out_specs=(
            P("dp", None),
            P("dp", "tensor"),
            P(None, None, "tensor"),
            P(None, "tensor"),
            P("tensor", None),
            P(),
            P(),
            P(),
            P(None, "tensor"),
            P("tensor"),
            P("tensor", None),
            P(),
            P(),
            P(),
        ),
        check_vma=False,
    )
```

time: 614 us -> 576 us (0.938)
  other arithmetic: 79.6 us -> 62.1 us
  waiting for transfers between devices: 219 us -> 204 us
  local copies, waits for them, and re-layouts: 55.5 us -> 43.8 us
  starting transfers between devices: 72.1 us -> 80.5 us
    ppermute x15 -> x9, waiting for transfers between devices: 54.5 us -> 33.2 us  [from_next(): lax.ppermute(x, 'tensor', [((i + step) % size, i) for i in range(size)])]
    ppermute x15 -> x9, starting transfers between devices: 17.1 us -> 35.4 us  [from_next(): lax.ppermute(x, 'tensor', [((i + step) % size, i) for i in range(size)])]
    all_gather x1, waiting for transfers between devices: 0.02 us -> 12 us  [on_device(): gathered = lax.all_gather(result, 'tensor', axis=0, tiled=True)]
    unnamed x211 -> x122, local copies, waits for them, and re-layouts: 20.6 us -> 8.92 us
    convert_element_type x6 -> x1, other arithmetic: 12.7 us -> 2.26 us  [on_device(): output = (gathered * one).astype(BF16)]
    ppermute x6, waiting for transfers between devices: 53.1 us -> 42.8 us  [to_next(): lax.ppermute(x, 'tensor', [(i, (i + step) % size) for i in range(size)])]
    ppermute x40 -> x41, waiting for transfers between devices: 84.9 us -> 75.2 us  [flip(): return lax.ppermute(x, 'dp', [(i, i ^ 1 << bit) for i in range(size)])]
    dot_general x7 -> x4, matrix products: 17.2 us -> 9.2 us  [nn(): lax.dot_general(left, right, (((1,), (0,)), ((), ())), preferred_element_...]
  transfers between devices with their start and end apart: 73 -> 68, of which waited for: 29 -> 28; matrix products, arithmetic and copies ran while one was open for 28% -> 26% of each run, Pallas kernels for 16% -> 16%
where the time goes in v3:
time: 576 us; the launch traced here: 568 us
  waiting for transfers between devices  204 us (35%)
  Pallas kernels  93.7 us (16%)
  starting transfers between devices  80.5 us (14%)
  matrix products  68.1 us (12%)
  other arithmetic  62.1 us (11%)
  local copies, waits for them, and re-layouts  43.8 us (8%)
  between operations  16.5 us (3%)
    ppermute x41, waiting for transfers between devices, flip(): return lax.ppermute(x, 'dp', [(i, i ^ 1 << bit) for i in range(size)])  75.2 us
    pallas_call x1, Pallas kernels, attention_backward(): pl.pallas_call(backward_kernel, grid=(pairs,), in_specs=[pl.BlockSpec(mem...  51.3 us
    ppermute x6, waiting for transfers between devices, to_next(): lax.ppermute(x, 'tensor', [(i, (i + step) % size) for i in range(size)])  42.8 us
    dot_general x8, matrix products, nt(): lax.dot_general(left, right, (((1,), (1,)), ((), ())), preferred_element_...  41.1 us
    ppermute x9, starting transfers between devices, from_next(): lax.ppermute(x, 'tensor', [((i + step) % size, i) for i in range(size)])  35.4 us
    ppermute x41, starting transfers between devices, flip(): return lax.ppermute(x, 'dp', [(i, i ^ 1 << bit) for i in range(size)])  33.5 us
    ppermute x9, waiting for transfers between devices, from_next(): lax.ppermute(x, 'tensor', [((i + step) % size, i) for i in range(size)])  33.2 us
    pallas_call x1, Pallas kernels, attention_forward(): pl.pallas_call(forward_kernel, grid=(width // (2 * HD),), in_specs=[pl.Bl...  22.9 us
  transfers between devices with their start and end apart: 68, of which 28 were waited for; matrix products, arithmetic and copies ran while one was open for 26% of the time, Pallas kernels for 16%

profile of v3, /device:TPU:0, one launch (start us, length us, event | category | flops | bytes accessed | tf_op | source)
XLA Modules:
  0.0 568.4 jit_solution(13733062728987834553)
XLA Ops:
  19.8 6.6 %collective-permute-done.2 = f32[104,768]{1,0:T(8,128)S(1)} collective-permute-done((f32[104,768]{1,0:T(8,128)S(1)}, f32[104,768]{1,0:T(8,128)S(1)}, u32[]{:S(2)}, u32[]{:S(2)}) %collective-permute-start.2) | collective-permute-done | bytes 319520 | tf_op jit(solution)/shard_map/ppermute | solution.py:57
  26.4 12.8 %collective-permute-done.1 = f32[104,768]{1,0:T(8,128)S(1)} collective-permute-done((f32[104,768]{1,0:T(8,128)S(1)}, f32[104,768]{1,0:T(8,128)S(1)}, u32[]{:S(2)}, u32[]{:S(2)}) %collective-permute-start.1) | collective-permute-done | bytes 319520 | tf_op jit(solution)/shard_map/ppermute | solution.py:57
  46.7 7.5 %collective-permute-done.3 = f32[3,56,768]{2,1,0:T(8,128)} collective-permute-done((f32[3,56,768]{2,1,0:T(8,128)}, f32[3,56,768]{2,1,0:T(8,128)}, u32[]{:S(2)}, u32[]{:S(2)}) %collective-permute-start.3) | collective-permute-done | bytes 516128 | tf_op jit(solution)/shard_map/ppermute | solution.py:52
  63.1 7.4 %collective-permute-start.11 = (f32[96,768]{1,0:T(8,128)}, f32[96,768]{1,0:T(8,128)}, u32[]{:S(2)}, u32[]{:S(2)}) collective-permute-start(f32[96,768]{1,0:T(8,128)} %multiply_bitcast_fusion.1), channel_id=1, source_target_pairs={{1,0},{2,1},{3,2},{0,3},{5,4},{6,5},{7,6},{4,7},{9,8},{10,9},{11,1... | collective-permute-start | bytes 884744 | tf_op jit(solution)/shard_map/ppermute | solution.py:57
  77.1 16.2 %collective-permute-start.13 = (f32[96,768]{1,0:T(8,128)}, f32[96,768]{1,0:T(8,128)S(1)}, u32[]{:S(2)}, u32[]{:S(2)}) collective-permute-start(f32[96,768]{1,0:T(8,128)} %multiply_bitcast_fusion.1), channel_id=1, source_target_pairs={{3,0},{0,1},{1,2},{2,3},{7,4},{4,5},{5,6},{6,7},{11,8},{8,9},{9,10... | collective-permute-start | bytes 884744 | tf_op jit(solution)/shard_map/ppermute | solution.py:57
  103.0 7.0 %shard_map.254 = bf16[4,4,3,4,16,768]{5,4,3,2,1,0:T(8,128)(2,1)} custom-call(s32[1]{0:T(128)} %bitcast.me_ref, f32[12,8,8,768]{3,2,1,0:T(8,128)} %bitcast.295, f32[12,8,8,768]{3,2,1,0:T(8,128)} %bitcast.296, f32[2,3,56,768]{3,2,1,0:T(8,128)} %pad_maximum_fusion.3.refs_0_, f32[2,3,56,768]{3,2,1,0:T(8,128)} %collective-permute-done.4.refs_1_, ...), custom_call_target="tpu_custom_call" | custom-call | tf_op jit(solution)/shard_map/pallas_call | solution.py:112
  127.1 9.0 %collective-permute-done.17 = f32[96,768]{1,0:T(8,128)} collective-permute-done((f32[96,768]{1,0:T(8,128)S(1)}, f32[96,768]{1,0:T(8,128)}, u32[]{:S(2)}, u32[]{:S(2)}) %collective-permute-start.17) | collective-permute-done | bytes 294944 | tf_op jit(solution)/shard_map/ppermute | solution.py:57
  144.7 22.9 %shard_map.255.mixed_ref = bf16[768,512]{1,0:T(8,128)(2,1)S(1)} custom-call(s32[1]{0:T(128)} %get-tuple-element.244.length_ref, bf16[512,768]{1,0:T(8,128)(2,1)S(1)} %copy-done.6, bf16[1024,768]{1,0:T(8,128)(2,1)S(1)} %convolution_convert_fusion.k_ref, bf16[1024,768]{1,0:T(8,128)(2,1)S(1)} %add_convert_fusion.2.v_ref), custom_call_target="tpu_custom_call" | custom-call | flops 393216 | bytes 1048576 | tf_op jit(solution)/shard_map/pallas_call | solution.py:359
  173.2 4.6 shard_map.256
  180.8 10.3 %collective-permute-done.24.b_far_ref = f32[2,3,48,768]{3,2,1,0:T(8,128)S(1)} collective-permute-done((f32[2,3,48,768]{3,2,1,0:T(8,128)S(1)}, f32[2,3,48,768]{3,2,1,0:T(8,128)S(1)}, u32[]{:S(2)}, u32[]{:S(2)}) %collective-permute-start.24) | collective-permute-done | bytes 884768 | tf_op jit(solution)/shard_map/ppermute | solution.py:52
  191.1 9.8 %multiply_convert_fusion.2 = (bf16[512,1536]{1,0:T(8,128)(2,1)}, f32[512,1536]{1,0:T(8,128)}, f32[512,1536]{1,0:T(8,128)}) fusion(f32[1536]{0:T(1024)S(1)} %add.581, bf16[512,768]{1,0:T(8,128)(2,1)S(1)} %fusion.17, bf16[1536,768]{1,0:T(8,128)(2,1)S(1)} %bitcast.317), kind=kOutput, calls=%fused_computation.37 | convolution fusion | flops 1259864064 | bytes 11016192 | tf_op jit(solution)/shard_map/dot_general | solution.py:32
  207.5 11.1 %multiply_convert_fusion.1 = (bf16[512,1536]{1,0:T(8,128)(2,1)S(1)}, f32[512,1536]{1,0:T(8,128)}, f32[512,1536]{1,0:T(8,128)}) fusion(f32[1536]{0:T(1024)S(1)} %add.584, bf16[512,768]{1,0:T(8,128)(2,1)S(1)} %fusion.17, bf16[1536,768]{1,0:T(8,128)(2,1)} %bitcast.319), kind=kOutput, calls=%fused_computation.24 | convolution fusion | flops 1259864064 | bytes 11016192 | tf_op jit(solution)/shard_map/dot_general | solution.py:32
  237.2 5.1 add_convert_fusion.1
  247.3 4.3 slice_bitcast_fusion.6
  252.5 4.2 add_convert_fusion
  256.8 4.3 convolution_add_fusion.1
  281.4 51.3 %shard_map.260 = (f32[4,4,96,768]{3,2,1,0:T(8,128)}, f32[4,4,96,768]{3,2,1,0:T(8,128)}, f32[6,2,128]{2,1,0:T(2,128)}, f32[768,1024]{1,0:T(8,128)}) custom-call(s32[2]{0:T(128)} %pad_add_fusion.scalars_ref, bf16[512,768]{1,0:T(8,128)(2,1)} %fusion.16.q_ref, bf16[1024,768]{1,0:T(8,128)(2,1)} %copy-done.3, bf16[1024,768]{1,0:T(8,128)(2,1)} %copy-done.4, ...), custom_call_target="tpu_custom_call" | custom-call | flops 393216 | bytes 1048576 | tf_op jit(solution)/shard_map/pallas_call | solution.py:381
  340.1 12.0 %all-gather.2.cloned.1.call-done = f32[2048,768]{1,0:T(8,128)} async-done(((f32[512,768]{1,0:T(8,128)}), f32[2048,768]{1,0:T(8,128)}) %all-gather.2.cloned.1.call-update) | async-done | bytes 6291472 | tf_op jit(solution)/shard_map/all_gather | solution.py:538
  360.4 4.4 slice_add_fusion
  366.6 14.9 %collective-permute-done.38 = f32[4,96,768]{2,1,0:T(8,128)S(1)} collective-permute-done((f32[4,96,768]{2,1,0:T(8,128)}, f32[4,96,768]{2,1,0:T(8,128)S(1)}, u32[]{:S(2)}, u32[]{:S(2)}) %collective-permute-start.38) | collective-permute-done | bytes 1179680 | tf_op jit(solution)/shard_map/ppermute | solution.py:52
  389.5 14.1 %collective-permute-done.48 = f32[192,768]{1,0:T(8,128)S(1)} collective-permute-done((f32[192,768]{1,0:T(8,128)S(1)}, f32[192,768]{1,0:T(8,128)S(1)}, u32[]{:S(2)}, u32[]{:S(2)}) %collective-permute-start.48) | collective-permute-done | bytes 589856 | tf_op jit(solution)/shard_map/ppermute | solution.py:62
  403.6 4.4 collective-permute-done.49
  408.2 4.9 collective-permute-done.46
  418.4 11.1 %collective-permute-done.50 = f32[192,768]{1,0:T(8,128)S(1)} collective-permute-done((f32[192,768]{1,0:T(8,128)S(1)}, f32[192,768]{1,0:T(8,128)S(1)}, u32[]{:S(2)}, u32[]{:S(2)}) %collective-permute-start.50) | collective-permute-done | bytes 589856 | tf_op jit(solution)/shard_map/ppermute | solution.py:62
  433.7 11.7 %collective-permute-done.55 = f32[72,128]{1,0:T(8,128)S(1)} collective-permute-done((f32[72,128]{1,0:T(8,128)S(1)}, f32[72,128]{1,0:T(8,128)S(1)}, u32[]{:S(2)}, u32[]{:S(2)}) %collective-permute-start.55) | collective-permute-done | bytes 36896 | tf_op jit(solution)/shard_map/ppermute | solution.py:223
  451.9 13.0 %collective-permute-done.63 = f32[1,192,768]{2,1,0:T(8,128)S(1)} collective-permute-done((f32[1,192,768]{2,1,0:T(8,128)S(1)}, f32[1,192,768]{2,1,0:T(8,128)S(1)}, u32[]{:S(2)}, u32[]{:S(2)}) %collective-permute-start.63) | collective-permute-done | bytes 589856 | tf_op jit(solution)/shard_map/ppermute | solution.py:52
  466.5 8.7 %collective-permute-done.57 = f32[96,768]{1,0:T(8,128)S(1)} collective-permute-done((f32[96,768]{1,0:T(8,128)S(1)}, f32[96,768]{1,0:T(8,128)S(1)}, u32[]{:S(2)}, u32[]{:S(2)}) %collective-permute-start.57) | collective-permute-done | bytes 294944 | tf_op jit(solution)/shard_map/ppermute | solution.py:62
  475.4 15.9 %collective-permute-done.64 = f32[2,192,768]{2,1,0:T(8,128)S(1)} collective-permute-done((f32[2,192,768]{2,1,0:T(8,128)S(1)}, f32[2,192,768]{2,1,0:T(8,128)S(1)}, u32[]{:S(2)}, u32[]{:S(2)}) %collective-permute-start.64) | collective-permute-done | bytes 1179680 | tf_op jit(solution)/shard_map/ppermute | solution.py:52
  495.2 8.9 %collective-permute-done.59 = f32[96,768]{1,0:T(8,128)S(1)} collective-permute-done((f32[96,768]{1,0:T(8,128)S(1)}, f32[96,768]{1,0:T(8,128)S(1)}, u32[]{:S(2)}, u32[]{:S(2)}) %collective-permute-start.59) | collective-permute-done | bytes 294944 | tf_op jit(solution)/shard_map/ppermute | solution.py:62
  516.5 8.7 %collective-permute-done.43 = f32[192,1024]{1,0:T(8,128)} collective-permute-done((f32[192,1024]{1,0:T(8,128)}, f32[192,1024]{1,0:T(8,128)}, u32[]{:S(2)}, u32[]{:S(2)}) %collective-permute-start.43) | collective-permute-done | bytes 786464 | tf_op jit(solution)/shard_map/ppermute | solution.py:413
  535.2 5.6 collective-permute-done.45
  540.8 7.1 %collective-permute-done.42 = f32[192,1024]{1,0:T(8,128)S(1)} collective-permute-done((f32[192,1024]{1,0:T(8,128)}, f32[192,1024]{1,0:T(8,128)S(1)}, u32[]{:S(2)}, u32[]{:S(2)}) %collective-permute-start.42) | collective-permute-done | bytes 786464 | tf_op jit(solution)/shard_map/ppermute | solution.py:424
  (406 shorter events, 212.0 us)
Async XLA Ops:
  7.2 345.0 %all-gather.2.cloned.1.call-start = ((), (), s32[]{:S(2)}) async-start(), calls=%async_computation | async-start | bytes 7864320 | tf_op jit(solution)/shard_map/all_gather | solution.py:538
  15.9 23.4 %collective-permute-start.1 = (f32[104,768]{1,0:T(8,128)S(1)}, f32[104,768]{1,0:T(8,128)S(1)}, u32[]{:S(2)}, u32[]{:S(2)}) collective-permute-start(f32[104,768]{1,0:T(8,128)S(1)} %fusion.43), channel_id=1, source_target_pairs={{2,0},{3,1},{0,2},{1,3},{6,4},{7,5},{4,6},{5,7},{10,8},{11,9},{8,1... | collective-permute-start | bytes 958472 | tf_op jit(solution)/shard_map/ppermute | solution.py:57
  18.4 20.8 %collective-permute-start = (f32[104,768]{1,0:T(8,128)S(1)}, f32[104,768]{1,0:T(8,128)S(1)}, u32[]{:S(2)}, u32[]{:S(2)}) collective-permute-start(f32[104,768]{1,0:T(8,128)S(1)} %fusion.43), channel_id=1, source_target_pairs={{1,0},{2,1},{3,2},{0,3},{5,4},{6,5},{7,6},{4,7},{9,8},{10,9},{11,1... | collective-permute-start | bytes 958472 | tf_op jit(solution)/shard_map/ppermute | solution.py:57
  56.4 40.8 %collective-permute-start.4 = (f32[2,3,56,768]{3,2,1,0:T(8,128)}, f32[2,3,56,768]{3,2,1,0:T(8,128)}, u32[]{:S(2)}, u32[]{:S(2)}) collective-permute-start(f32[2,3,56,768]{3,2,1,0:T(8,128)} %pad_maximum_fusion.3.refs_0_), channel_id=1, source_target_pairs={{0,16},{4,20},{8,24},{12,28},{16,0},{20,4},{24,8},{28,12},{1,17},{... | collective-permute-start | bytes 3096584 | tf_op jit(solution)/shard_map/ppermute | solution.py:52
  59.9 36.8 %collective-permute-start.6 = (f32[2,3,48,768]{3,2,1,0:T(8,128)}, f32[2,3,48,768]{3,2,1,0:T(8,128)}, u32[]{:S(2)}, u32[]{:S(2)}) collective-permute-start(f32[2,3,48,768]{3,2,1,0:T(8,128)} %pad_maximum_fusion.6.refs_2_), channel_id=1, source_target_pairs={{0,8},{4,12},{8,0},{12,4},{16,24},{20,28},{24,16},{28,20},{1,9},{5... | collective-permute-start | bytes 2654216 | tf_op jit(solution)/shard_map/ppermute | solution.py:52
  72.7 23.9 %collective-permute-start.12 = (f32[96,768]{1,0:T(8,128)}, f32[96,768]{1,0:T(8,128)S(1)}, u32[]{:S(2)}, u32[]{:S(2)}) collective-permute-start(f32[96,768]{1,0:T(8,128)} %multiply_bitcast_fusion.1), channel_id=1, source_target_pairs={{2,0},{3,1},{0,2},{1,3},{6,4},{7,5},{4,6},{5,7},{10,8},{11,9},{8,1... | collective-permute-start | bytes 884744 | tf_op jit(solution)/shard_map/ppermute | solution.py:57
  74.1 25.2 %collective-permute-start.7 = (f32[2,3,56,768]{3,2,1,0:T(8,128)}, f32[2,3,56,768]{3,2,1,0:T(8,128)}, u32[]{:S(2)}, u32[]{:S(2)}) collective-permute-start(f32[2,3,56,768]{3,2,1,0:T(8,128)} %pad_maximum_fusion.3.refs_0_), channel_id=1, source_target_pairs={{0,4},{4,0},{8,12},{12,8},{16,20},{20,16},{24,28},{28,24},{1,5},{5... | collective-permute-start | bytes 3096584 | tf_op jit(solution)/shard_map/ppermute | solution.py:52
  110.2 25.9 %collective-permute-start.17 = (f32[96,768]{1,0:T(8,128)S(1)}, f32[96,768]{1,0:T(8,128)}, u32[]{:S(2)}, u32[]{:S(2)}) collective-permute-start(f32[96,768]{1,0:T(8,128)S(1)} %multiply_bitcast_fusion), channel_id=1, source_target_pairs={{2,0},{3,1},{0,2},{1,3},{6,4},{7,5},{4,6},{5,7},{10,8},{11,9},{8,1... | collective-permute-start | bytes 884744 | tf_op jit(solution)/shard_map/ppermute | solution.py:57
  113.3 23.8 %collective-permute-start.18 = (f32[96,768]{1,0:T(8,128)S(1)}, f32[96,768]{1,0:T(8,128)}, u32[]{:S(2)}, u32[]{:S(2)}) collective-permute-start(f32[96,768]{1,0:T(8,128)S(1)} %multiply_bitcast_fusion), channel_id=1, source_target_pairs={{3,0},{0,1},{1,2},{2,3},{7,4},{4,5},{5,6},{6,7},{11,8},{8,9},{9,10... | collective-permute-start | bytes 884744 | tf_op jit(solution)/shard_map/ppermute | solution.py:57
  114.3 57.3 %collective-permute-start.20 = (f32[2,3,48,768]{3,2,1,0:T(8,128)}, f32[2,3,48,768]{3,2,1,0:T(8,128)}, u32[]{:S(2)}, u32[]{:S(2)}) collective-permute-start(f32[2,3,48,768]{3,2,1,0:T(8,128)} %pad_maximum_fusion.8.b_ref), channel_id=1, source_target_pairs={{0,8},{4,12},{8,0},{12,4},{16,24},{20,28},{24,16},{28,20},{1,9},{5... | collective-permute-start | bytes 2654216 | tf_op jit(solution)/shard_map/ppermute | solution.py:52
  116.7 56.5 %collective-permute-start.19 = (f32[2,3,48,768]{3,2,1,0:T(8,128)}, f32[2,3,48,768]{3,2,1,0:T(8,128)}, u32[]{:S(2)}, u32[]{:S(2)}) collective-permute-start(f32[2,3,48,768]{3,2,1,0:T(8,128)} %pad_maximum_fusion.7.a_ref), channel_id=1, source_target_pairs={{0,16},{4,20},{8,24},{12,28},{16,0},{20,4},{24,8},{28,12},{1,17},{... | collective-permute-start | bytes 2654216 | tf_op jit(solution)/shard_map/ppermute | solution.py:52
  126.0 77.4 %collective-permute-start.27 = (f32[2,3,48,768]{3,2,1,0:T(8,128)}, f32[2,3,48,768]{3,2,1,0:T(8,128)}, u32[]{:S(2)}, u32[]{:S(2)}) collective-permute-start(f32[2,3,48,768]{3,2,1,0:T(8,128)} %pad_maximum_fusion.8.b_ref), channel_id=1, source_target_pairs={{0,4},{4,0},{8,12},{12,8},{16,20},{20,16},{24,28},{28,24},{1,5},{5... | collective-permute-start | bytes 2654216 | tf_op jit(solution)/shard_map/ppermute | solution.py:52
  139.7 28.0 %collective-permute-start.22 = (f32[3,48,768]{2,1,0:T(8,128)}, f32[3,48,768]{2,1,0:T(8,128)}, u32[]{:S(2)}, u32[]{:S(2)}) collective-permute-start(f32[3,48,768]{2,1,0:T(8,128)} %pad_maximum_fusion.17), channel_id=1, source_target_pairs={{0,16},{4,20},{8,24},{12,28},{16,0},{20,4},{24,8},{28,12},{1,17},{... | collective-permute-start | bytes 1327112 | tf_op jit(solution)/shard_map/ppermute | solution.py:52
  140.2 27.5 %collective-permute-start.21 = (f32[3,48,768]{2,1,0:T(8,128)}, f32[3,48,768]{2,1,0:T(8,128)}, u32[]{:S(2)}, u32[]{:S(2)}) collective-permute-start(f32[3,48,768]{2,1,0:T(8,128)} %pad_maximum_fusion.16), channel_id=1, source_target_pairs={{0,8},{4,12},{8,0},{12,4},{16,24},{20,28},{24,16},{28,20},{1,9},{5... | collective-permute-start | bytes 1327112 | tf_op jit(solution)/shard_map/ppermute | solution.py:52
  167.7 35.8 %collective-permute-start.25 = (f32[2,3,48,768]{3,2,1,0:T(8,128)}, f32[2,3,48,768]{3,2,1,0:T(8,128)S(1)}, u32[]{:S(2)}, u32[]{:S(2)}) collective-permute-start(f32[2,3,48,768]{3,2,1,0:T(8,128)} %pad_maximum_fusion.7.a_ref), channel_id=1, source_target_pairs={{0,4},{4,0},{8,12},{12,8},{16,20},{20,16},{24,28},{28,24},{1,5},{5... | collective-permute-start | bytes 2654216 | tf_op jit(solution)/shard_map/ppermute | solution.py:52
  169.3 21.8 %collective-permute-start.24 = (f32[2,3,48,768]{3,2,1,0:T(8,128)S(1)}, f32[2,3,48,768]{3,2,1,0:T(8,128)S(1)}, u32[]{:S(2)}, u32[]{:S(2)}) collective-permute-start(f32[2,3,48,768]{3,2,1,0:T(8,128)S(1)} %pad_maximum_fusion.10.b_ref), channel_id=1, source_target_pairs={{0,8},{4,12},{8,0},{12,4},{16,24},{20,28},{24,16},{28,20},{1,9},{5... | collective-permute-start | bytes 2654216 | tf_op jit(solution)/shard_map/ppermute | solution.py:52
  171.6 29.3 %collective-permute-start.23 = (f32[2,3,48,768]{3,2,1,0:T(8,128)S(1)}, f32[2,3,48,768]{3,2,1,0:T(8,128)S(1)}, u32[]{:S(2)}, u32[]{:S(2)}) collective-permute-start(f32[2,3,48,768]{3,2,1,0:T(8,128)S(1)} %pad_maximum_fusion.9.a_ref), channel_id=1, source_target_pairs={{0,16},{4,20},{8,24},{12,28},{16,0},{20,4},{24,8},{28,12},{1,17},{... | collective-permute-start | bytes 2654216 | tf_op jit(solution)/shard_map/ppermute | solution.py:52
  173.2 30.7 %collective-permute-start.28 = (f32[2,3,48,768]{3,2,1,0:T(8,128)}, f32[2,3,48,768]{3,2,1,0:T(8,128)S(1)}, u32[]{:S(2)}, u32[]{:S(2)}) collective-permute-start(f32[2,3,48,768]{3,2,1,0:T(8,128)} %collective-permute-done.20.b_far_ref), channel_id=1, source_target_pairs={{0,4},{4,0},{8,12},{12,8},{16,20},{20,16},{24,28},{28,24},{1,5},{5... | collective-permute-start | bytes 2654216 | tf_op jit(solution)/shard_map/ppermute | solution.py:52
  233.6 23.1 %collective-permute-start.33 = (f32[1536,768]{1,0:T(8,128)}, f32[1536,768]{1,0:T(8,128)}, u32[]{:S(2)}, u32[]{:S(2)}) collective-permute-start(f32[1536,768]{1,0:T(8,128)} %fusion.83), channel_id=1, source_target_pairs={{0,4},{4,0},{8,12},{12,8},{16,20},{20,16},{24,28},{28,24},{1,5},{5... | collective-permute-start | bytes 14155784 | tf_op jit(solution)/shard_map/ppermute | solution.py:52
  270.0 62.6 %collective-permute-start.36 = (f32[2,4,96,768]{3,2,1,0:T(8,128)}, f32[2,4,96,768]{3,2,1,0:T(8,128)}, u32[]{:S(2)}, u32[]{:S(2)}) collective-permute-start(f32[2,4,96,768]{3,2,1,0:T(8,128)} %slice_bitcast_fusion), channel_id=1, source_target_pairs={{0,8},{4,12},{8,0},{12,4},{16,24},{20,28},{24,16},{28,20},{1,9},{5... | collective-permute-start | bytes 7077896 | tf_op jit(solution)/shard_map/ppermute | solution.py:52
  271.2 61.4 %collective-permute-start.35 = (f32[2,4,96,768]{3,2,1,0:T(8,128)}, f32[2,4,96,768]{3,2,1,0:T(8,128)}, u32[]{:S(2)}, u32[]{:S(2)}) collective-permute-start(f32[2,4,96,768]{3,2,1,0:T(8,128)} %bitcast.67), channel_id=1, source_target_pairs={{0,16},{4,20},{8,24},{12,28},{16,0},{20,4},{24,8},{28,12},{1,17},{... | collective-permute-start | bytes 7077896 | tf_op jit(solution)/shard_map/ppermute | solution.py:52
  353.0 28.5 %collective-permute-start.38 = (f32[4,96,768]{2,1,0:T(8,128)}, f32[4,96,768]{2,1,0:T(8,128)S(1)}, u32[]{:S(2)}, u32[]{:S(2)}) collective-permute-start(f32[4,96,768]{2,1,0:T(8,128)} %get-tuple-element.183), channel_id=1, source_target_pairs={{0,16},{4,20},{8,24},{12,28},{16,0},{20,4},{24,8},{28,12},{1,17},{... | collective-permute-start | bytes 3538952 | tf_op jit(solution)/shard_map/ppermute | solution.py:52
  354.4 29.5 %collective-permute-start.40 = (f32[4,96,768]{2,1,0:T(8,128)}, f32[4,96,768]{2,1,0:T(8,128)}, u32[]{:S(2)}, u32[]{:S(2)}) collective-permute-start(f32[4,96,768]{2,1,0:T(8,128)} %get-tuple-element.185), channel_id=1, source_target_pairs={{0,8},{4,12},{8,0},{12,4},{16,24},{20,28},{24,16},{28,20},{1,9},{5... | collective-permute-start | bytes 3538952 | tf_op jit(solution)/shard_map/ppermute | solution.py:52
  360.2 26.8 %collective-permute-start.37 = (f32[192,1024]{1,0:T(8,128)S(1)}, f32[192,1024]{1,0:T(8,128)S(1)}, u32[]{:S(2)}, u32[]{:S(2)}) collective-permute-start(f32[192,1024]{1,0:T(8,128)S(1)} %get-tuple-element.198), channel_id=1, source_target_pairs={{0,1},{1,0},{2,3},{3,2},{4,5},{5,4},{6,7},{7,6},{8,9},{9,8},{10,11... | collective-permute-start | bytes 2359304 | tf_op jit(solution)/shard_map/ppermute | solution.py:412
  364.9 43.1 %collective-permute-start.49 = (f32[2,2,96,768]{3,2,1,0:T(8,128)S(1)}, f32[2,2,96,768]{3,2,1,0:T(8,128)S(1)}, u32[]{:S(2)}, u32[]{:S(2)}) collective-permute-start(f32[2,2,96,768]{3,2,1,0:T(8,128)S(1)} %slice_bitcast_fusion.1), channel_id=1, source_target_pairs={{0,8},{4,12},{8,0},{12,4},{16,24},{20,28},{24,16},{28,20},{1,9},{5... | collective-permute-start | bytes 3538952 | tf_op jit(solution)/shard_map/ppermute | solution.py:52
  385.4 27.7 %collective-permute-start.46 = (f32[2,2,96,768]{3,2,1,0:T(8,128)S(1)}, f32[2,2,96,768]{3,2,1,0:T(8,128)S(1)}, u32[]{:S(2)}, u32[]{:S(2)}) collective-permute-start(f32[2,2,96,768]{3,2,1,0:T(8,128)S(1)} %slice.376), channel_id=1, source_target_pairs={{0,16},{4,20},{8,24},{12,28},{16,0},{20,4},{24,8},{28,12},{1,17},{... | collective-permute-start | bytes 3538952 | tf_op jit(solution)/shard_map/ppermute | solution.py:52
  416.4 29.9 %collective-permute-start.51 = (f32[2,96,768]{2,1,0:T(8,128)S(1)}, f32[2,96,768]{2,1,0:T(8,128)S(1)}, u32[]{:S(2)}, u32[]{:S(2)}) collective-permute-start(f32[2,96,768]{2,1,0:T(8,128)S(1)} %get-tuple-element.192), channel_id=1, source_target_pairs={{0,16},{4,20},{8,24},{12,28},{16,0},{20,4},{24,8},{28,12},{1,17},{... | collective-permute-start | bytes 1769480 | tf_op jit(solution)/shard_map/ppermute | solution.py:52
  417.8 28.5 %collective-permute-start.47 = (f32[2,96,768]{2,1,0:T(8,128)S(1)}, f32[2,96,768]{2,1,0:T(8,128)S(1)}, u32[]{:S(2)}, u32[]{:S(2)}) collective-permute-start(f32[2,96,768]{2,1,0:T(8,128)S(1)} %get-tuple-element.194), channel_id=1, source_target_pairs={{0,8},{4,12},{8,0},{12,4},{16,24},{20,28},{24,16},{28,20},{1,9},{5... | collective-permute-start | bytes 1769480 | tf_op jit(solution)/shard_map/ppermute | solution.py:52
  465.0 26.2 %collective-permute-start.64 = (f32[2,192,768]{2,1,0:T(8,128)S(1)}, f32[2,192,768]{2,1,0:T(8,128)S(1)}, u32[]{:S(2)}, u32[]{:S(2)}) collective-permute-start(f32[2,192,768]{2,1,0:T(8,128)S(1)} %pad_maximum_fusion.5), channel_id=1, source_target_pairs={{0,16},{4,20},{8,24},{12,28},{16,0},{20,4},{24,8},{28,12},{1,17},{... | collective-permute-start | bytes 3538952 | tf_op jit(solution)/shard_map/ppermute | solution.py:52
  492.8 38.1 %collective-permute-start.65 = (f32[4,192,768]{2,1,0:T(8,128)}, f32[4,192,768]{2,1,0:T(8,128)}, u32[]{:S(2)}, u32[]{:S(2)}) collective-permute-start(f32[4,192,768]{2,1,0:T(8,128)} %pad_maximum_fusion.2), channel_id=1, source_target_pairs={{0,4},{4,0},{8,12},{12,8},{16,20},{20,16},{24,28},{28,24},{1,5},{5... | collective-permute-start | bytes 7077896 | tf_op jit(solution)/shard_map/ppermute | solution.py:52
  515.2 25.6 %collective-permute-start.45 = (f32[192,1024]{1,0:T(8,128)}, f32[192,1024]{1,0:T(8,128)S(1)}, u32[]{:S(2)}, u32[]{:S(2)}) collective-permute-start(f32[192,1024]{1,0:T(8,128)} %get-tuple-element.196), channel_id=1, source_target_pairs={{0,1},{3,2},{4,5},{7,6},{8,9},{11,10},{12,13},{15,14},{16,17},{19,... | collective-permute-start | bytes 2359304 | tf_op jit(solution)/shard_map/ppermute | solution.py:418
  535.2 21.6 %collective-permute-start.66 = (f32[4,96,768]{2,1,0:T(8,128)}, f32[4,96,768]{2,1,0:T(8,128)}, u32[]{:S(2)}, u32[]{:S(2)}) collective-permute-start(f32[4,96,768]{2,1,0:T(8,128)} %pad_maximum_fusion.4), channel_id=1, source_target_pairs={{0,4},{4,0},{8,12},{12,8},{16,20},{20,16},{24,28},{28,24},{1,5},{5... | collective-permute-start | bytes 3538952 | tf_op jit(solution)/shard_map/ppermute | solution.py:52
  (86 other events, 1093.2 us)
Sparse Core Ops, SparseCore 0:
  237.4 114.7 all-gather.1

commit v4 on v3

--- a/solution.py
+++ b/solution.py
@@ -199,34 +199,35 @@
     return total
 
 
-def gather_in_order(piece, order, others=()):
-    held = piece[None]
-    for bit in (*order, 0):
-        if bit == 0 and others:
-            held = after(held, others)
-        held = jnp.concatenate([held, flip(held, bit)], 0)
-    me = lax.axis_index("dp") % INNER
-    blocks = []
-    for index in range(INNER):
-        apart = me ^ index
-        place = sum(((apart >> bit) & 1) << at for at, bit in enumerate((*order, 0)))
-        blocks.append(lax.dynamic_index_in_dim(held, place, 0))
-    return jnp.concatenate(blocks, 0)
-
-
-def sum_everywhere(x, others):
-    others = list(others)
-    for axis in ("dp", "tensor"):
-        size = lax.axis_size(axis)
-        step = 1
-        while step < size:
-            got = lax.ppermute(x, axis, [(i, i ^ step) for i in range(size)])
-            x = x + (after(got, others.pop(0)) if others else got)
-            step *= 2
-    return x
-
-
-CHUNK = 256
+class GatherInOrder:
+    def __init__(self, piece):
+        self.held, self.bits = piece[None], []
+
+    def hop(self, bit, *others):
+        got = flip(self.held, bit)
+        self.held = jnp.concatenate([self.held, after(got, others) if others else got], 0)
+        self.bits.append(bit)
+
+    def result(self):
+        me = lax.axis_index("dp") % INNER
+        blocks = []
+        for index in range(INNER):
+            apart = me ^ index
+            place = sum(((apart >> bit) & 1) << at for at, bit in enumerate(self.bits))
+            blocks.append(lax.dynamic_index_in_dim(self.held, place, 0))
+        return jnp.concatenate(blocks, 0)
+
+
+class SumEverywhere:
+    def __init__(self, x):
+        self.total = x
+
+    def hop(self, axis, bit):
+        pairs = [(i, i ^ (1 << bit)) for i in range(lax.axis_size(axis))]
+        self.total = self.total + lax.ppermute(self.total, axis, pairs)
+
+
+CHUNK = 512
 
 
 def lane_masks(width):
@@ -238,13 +239,7 @@
     return jnp.where(mask, x, jnp.zeros_like(x))
 
 
-def softmax_turned(keys, query, valid):
-    scores = jnp.where(valid, nt(keys, query), MASKED)
-    expo = jnp.exp(scores - jnp.max(scores, 0, keepdims=True))
-    return expo * (1.0 / jnp.sum(expo, 0, keepdims=True))
-
-
-def forward_kernel(length_ref, q_ref, k_ref, v_ref, mixed_ref):
+def forward_kernel(length_ref, q_ref, k_ref, v_ref, mixed_ref, log_ref):
     keys = k_ref.shape[0]
     valid = lax.broadcasted_iota(jnp.int32, (keys, 1), 0) < length_ref[0]
     masks = lane_masks(q_ref.shape[1])
@@ -252,7 +247,12 @@
     for start in range(0, q_ref.shape[0], CHUNK):
         rows = pl.ds(start, CHUNK)
         for head, mask in enumerate(masks):
-            probs = softmax_turned(k_ref[...], keep(mask, q_ref[rows, :]), valid).astype(BF16)
+            scores = jnp.where(valid, nt(k_ref[...], keep(mask, q_ref[rows, :])), MASKED)
+            highest = jnp.max(scores, 0, keepdims=True)
+            expo = jnp.exp(scores - highest)
+            totals = jnp.sum(expo, 0, keepdims=True)
+            log_ref[0, head : head + 1, rows] = highest + jnp.log(totals)
+            probs = (expo * (1.0 / totals)).astype(BF16)
             own = slice(head * HD, (head + 1) * HD)
             mixed_ref[own, rows] = nn(turned[own, :], probs).astype(BF16)
 
@@ -263,6 +263,7 @@
     k_ref,
     v_ref,
     dm_ref,
+    log_ref,
     mixed_ref,
     wq_ref,
     wk_ref,
@@ -293,7 +294,8 @@
         for head, mask in enumerate(masks):
             query = keep(mask, q_ref[rows, :])
             d_mixed = keep(mask, dm_ref[rows, :])
-            probs = softmax_turned(k_ref[...], query, valid)
+            scores = jnp.where(valid, nt(k_ref[...], query), MASKED)
+            probs = jnp.exp(scores - log_ref[0, head : head + 1, rows])
             d_values = nn(probs.astype(BF16), d_mixed)
             d_probs = nt(v_ref[...], d_mixed)
             row_dot = jnp.sum(d_probs * probs, 0, keepdims=True)
@@ -361,15 +363,18 @@
         grid=(width // (2 * HD),),
         in_specs=[pl.BlockSpec(memory_space=pltpu.SMEM)]
         + [columns(array) for array in (queries, keys, values)],
-        out_specs=pl.BlockSpec((2 * HD, count), lambda j: (j, 0)),
-        out_shape=jax.ShapeDtypeStruct((width, count), BF16),
+        out_specs=[pl.BlockSpec((2 * HD, count), lambda j: (j, 0)), pl.BlockSpec((1, 2, count), lambda j: (j, 0, 0))],
+        out_shape=[
+            jax.ShapeDtypeStruct((width, count), BF16),
+            jax.ShapeDtypeStruct((width // (2 * HD), 2, count), F32),
+        ],
         compiler_params=pltpu.CompilerParams(vmem_limit_bytes=48 * 2**20),
         cost_estimate=pl.CostEstimate(flops=count * width, bytes_accessed=2**20, transcendentals=0),
     )(length, queries, keys, values)
 
 
 def attention_backward(scalars, in_pairs, weights, whole):
-    queries, keys, values, d_mixed, mixed = in_pairs
+    queries, keys, values, d_mixed, logs, mixed = in_pairs
     count, width = queries.shape
     long = keys.shape[0]
     pairs = width // (2 * HD)
@@ -383,6 +388,7 @@
         grid=(pairs,),
         in_specs=[pl.BlockSpec(memory_space=pltpu.SMEM)]
         + [columns(array) for array in (queries, keys, values, d_mixed)]
+        + [pl.BlockSpec((1, 2, count), lambda j: (j, 0, 0))]
         + [of_rows(array) for array in (mixed, *weights)]
         + [full(array) for array in whole],
         out_specs=[full(sent), full(sent), pl.BlockSpec((1, 2, 2 * HD), lambda j: (j, 0, 0)), full(part)],
@@ -396,7 +402,7 @@
         ],
         compiler_params=pltpu.CompilerParams(vmem_limit_bytes=56 * 2**20),
         cost_estimate=pl.CostEstimate(flops=count * width, bytes_accessed=2**20, transcendentals=0),
-    )(scalars, queries, keys, values, d_mixed, mixed, *weights, *whole)
+    )(scalars, queries, keys, values, d_mixed, logs, mixed, *weights, *whole)
 
 
 class ShareInputs:
@@ -412,18 +418,19 @@
         self.first = lax.ppermute(near(jnp.where(self.outer, 3, 0)), "tensor", swap)
         self.second = lax.ppermute(self.near[2], "tensor", [(0, 1), (3, 2)])
 
-    def second_there(self, first):
-        self.far_sum = self.near[3] + first
-        self.far = lax.ppermute(self.far_sum, "tensor", [(1, 2), (2, 1)])
-        self.third = lax.ppermute(self.near[1], "tensor", [(0, 1), (3, 2)])
-
-    def middle(self):
-        self.across = lax.ppermute(self.near[2] + self.second, "tensor", [(1, 2), (2, 1)])
+    def inner(self):
+        self.far_sum, self.across_sum = self.near[3] + self.first, self.near[2] + self.second
+
+    def outward(self, others):
+        across = [(1, 2), (2, 1)]
+        far = lax.ppermute(after(self.far_sum, others), "tensor", across)
+        self.third = lax.ppermute(after(self.near[1], others), "tensor", [(0, 1), (3, 2)])
+        self.last = lax.ppermute(far, "tensor", [(2, 3), (1, 0)])
+        self.across = lax.ppermute(after(self.across_sum, far), "tensor", across)
 
     def result(self):
-        last = lax.ppermute(self.far, "tensor", [(2, 3), (1, 0)])
         mine = jnp.where(self.outer, self.near[0] + self.first, self.near[1] + self.third)
-        theirs = jnp.where(self.outer, last, self.across)
+        theirs = jnp.where(self.outer, self.last, self.across)
         return jnp.concatenate(
             [jnp.where(self.flipped, theirs, mine), jnp.where(self.flipped, mine, theirs)], 1
         )
@@ -507,7 +514,7 @@
     queries = (nt(own_tokens, q_rows) + qv_full[0]).astype(BF16) * scale
     keys = nt(seq_tokens, k_rows).astype(BF16)
     values = (nt(seq_tokens, v_rows) + qv_full[1]).astype(BF16)
-    turned_mixed = attention_forward(length, after(queries, down_places, keys, values), keys, values)
+    turned_mixed, logs = attention_forward(length, after(queries, down_places, keys, values), keys, values)
     late = lambda x: after(x, turned_mixed)
     up_far = both_second(up_first, late)
     down_first = both_first(after(down_places, up_first), late)
@@ -562,7 +569,7 @@
     scalars = jnp.concatenate([length, ((place % 2) * share)[None]])
     near, far, column_sums, input_part = attention_backward(
         scalars,
-        (queries, keys, values, d_mixed, turned_mixed),
+        (queries, keys, values, d_mixed, logs, turned_mixed),
         (q_rows, k_rows, v_rows),
         (own_tokens, seq_tokens, d_attended, d_first),
     )
@@ -571,7 +578,7 @@
     down_held = scatter_first(down_held, 0, late)
     up_held = scatter_first(up_held, 1, late)
     near, far, column_sums, input_part = after(
-        (near, far, column_sums, input_part), down_held, up_held, gathered
+        (near, far, column_sums, input_part), down_held, up_held
     )
     output = (gathered * one).astype(BF16)
     got = flip(far, 0)
@@ -583,13 +590,23 @@
     down_held = scatter_second(down_held, 0, late)
     up_held = scatter_second(up_held, 1, late)
     mlp_places = jnp.concatenate([up_held, down_held], 1)
-    share_inputs.second_there(after(share_inputs.first, mlp_places))
-    mlp_sums = scatter_place(mlp_places[3], mlp_places, 2)
-    late = lambda x: after(x, share_inputs.far_sum)
+    share_inputs.inner()
+    late = lambda x: after(x, share_inputs.far_sum, share_inputs.across_sum, gathered)
+    mlp_sums = scatter_place(mlp_places[3], mlp_places, 2, late)
+    late = lambda x: after(x, mlp_sums)
     attn_held = [scatter_first(held, half, late) for half, held in enumerate(attn_held)]
-    mlp_sums = scatter_place(after(mlp_sums, attn_held), mlp_places, 1)
-    late = lambda x: after(x, mlp_sums)
-    attn_held = [scatter_second(held, half, late) for half, held in enumerate(attn_held)]
+    mlp_sums = scatter_place(mlp_sums, mlp_places, 1, lambda x: after(x, attn_held))
+    attn_held = [scatter_second(held, half) for half, held in enumerate(attn_held)]
+    attn_places = [held[i] for held in attn_held for i in range(2)]
+    mlp_sums = scatter_place(mlp_sums, mlp_places, 0, lambda x: after(x, attn_places))
+    attn_sums = attn_places[3]
+    for step in (2, 1, 0):
+        attn_sums = scatter_place(attn_sums, attn_places, step)
+    mlp_sums, attn_sums = scatter_outer(mlp_sums), scatter_outer(attn_sums)
+    up_gather, down_gather = [GatherInOrder(mlp_sums[i * count : (i + 1) * count]) for i in (0, 1)]
+    up_gather.hop(1)
+    down_gather.hop(2)
+    attn_gather = GatherInOrder(attn_sums)
     qv_sums = column_sums.transpose(0, 2, 1).reshape(width, 2)
     qv_sums = heads_apart(qv_sums, 4).transpose(0, 1, 2, 3, 5, 4).reshape(4 * INNER, 2 * few)
     vector_blocks = jnp.concatenate([grad_up_bias.reshape(4 * INNER, count), qv_sums], 1)
@@ -606,25 +623,26 @@
         grad_second_gain,
         grad_second_shift,
     ]
-    small_sum = sum_everywhere(
-        jnp.concatenate([vector_blocks.reshape(-1), *vectors]).reshape(-1, 128),
-        (attn_sent, mlp_places, mlp_sums),
-    )
-    small = small_sum.reshape(-1)
-    attn_held = after(attn_held, small_sum)
-    attn_places = [held[i] for held in attn_held for i in range(2)]
-    share_inputs.middle()
-    mlp_sums = scatter_place(mlp_sums, mlp_places, 0, lambda x: after(x, attn_places))
-    mlp_sums = scatter_outer(mlp_sums)
-    attn_sums = attn_places[3]
-    for step in (2, 1, 0):
-        attn_sums = scatter_place(attn_sums, attn_places, step)
-    attn_sums = scatter_outer(attn_sums)
-    mlp_all = gather_in_order(mlp_sums, (1, 2))
-    grad_up = mlp_all[:, :count].reshape(units, width).T
-    grad_down = mlp_all[:, count:].reshape(units, width)
-    attn_all = gather_in_order(after(attn_sums, output), (2, 1), (grad_up, grad_down))
+    small = jnp.concatenate([vector_blocks.reshape(-1), *vectors]).reshape(-1, 128)
+    small = SumEverywhere(after(small, attn_sums))
+    small.hop("dp", 0)
+    up_gather.hop(2)
+    down_gather.hop(1)
+    attn_gather.hop(2, small.total)
+    small.hop("tensor", 0)
+    small.hop("tensor", 1)
+    share_inputs.outward(small.total)
+    up_gather.hop(0)
+    down_gather.hop(0)
+    attn_gather.hop(1, small.total, up_gather.held, down_gather.held)
     grad_tokens = share_inputs.result().T
+    for bit in range(1, lax.axis_size("dp").bit_length() - 1):
+        small.hop("dp", bit)
+    small = small.total.reshape(-1)
+    grad_up = up_gather.result().reshape(units, width).T
+    grad_down = down_gather.result().reshape(units, width)
+    attn_gather.hop(0, output, grad_up, grad_down)
+    attn_all = attn_gather.result()
     attn_all = attn_all.reshape(INNER, 4, heads, sub, width).transpose(1, 2, 0, 3, 4)
     attn_all = attn_all.reshape(4, columns, width)
 

time: 576 us -> 553 us (0.960)
  waiting for transfers between devices: 204 us -> 172 us
  Pallas kernels: 93.7 us -> 77.4 us
  other arithmetic: 62.1 us -> 71.6 us
  starting transfers between devices: 80.5 us -> 89.6 us
  local copies, waits for them, and re-layouts: 43.8 us -> 50.2 us
    ppermute x41 -> x44, waiting for transfers between devices: 75.2 us -> 48.1 us  [flip(): return lax.ppermute(x, 'dp', [(i, i ^ 1 << bit) for i in range(size)])]
    ppermute x1, waiting for transfers between devices: 0.01 us -> 23.7 us  [__init__(): self.first = lax.ppermute(near(jnp.where(self.outer, 3, 0)), 'tensor', swap)]
    ppermute x9, waiting for transfers between devices: 31.9 us -> 9.81 us  [the longest x5 9.8 us: hop(): self.total = self.total + lax.ppermute(self.total, axis, pairs)]
    all_gather x1, waiting for transfers between devices: 12 us -> 0.01 us  [on_device(): gathered = lax.all_gather(result, 'tensor', axis=0, tiled=True)]
    pallas_call x1, Pallas kernels: 51.3 us -> 42.9 us  [attention_backward(): pl.pallas_call(backward_kernel, grid=(pairs,), in_specs=[pl.BlockSpec(mem...]
    ppermute x9, starting transfers between devices: 8.8 us -> 16.8 us  [the longest x1 11.6 us: outward(): lax.ppermute(after(self.near[1], others), 'tensor', [(0, 1), (3, 2)])]
    pallas_call x1, Pallas kernels: 22.9 us -> 15.1 us  [attention_forward(): pl.pallas_call(forward_kernel, grid=(width // (2 * HD),), in_specs=[pl.Bl...]
    ppermute x6, waiting for transfers between devices: 42.8 us -> 49.1 us  [to_next(): lax.ppermute(x, 'tensor', [(i, (i + step) % size) for i in range(size)])]
  transfers between devices with their start and end apart: 68 -> 71, of which waited for: 28 -> 25; matrix products, arithmetic and copies ran while one was open for 26% -> 29% of each run, Pallas kernels for 16% -> 14%
where the time goes in v4:
time: 553 us; the launch traced here: 545 us
  waiting for transfers between devices  172 us (31%)
  starting transfers between devices  89.6 us (16%)
  Pallas kernels  77.4 us (14%)
  other arithmetic  71.6 us (13%)
  matrix products  67.3 us (12%)
  local copies, waits for them, and re-layouts  50.2 us (9%)
  between operations  16.8 us (3%)
    ppermute x6, waiting for transfers between devices, to_next(): lax.ppermute(x, 'tensor', [(i, (i + step) % size) for i in range(size)])  49.1 us
    ppermute x44, waiting for transfers between devices, flip(): return lax.ppermute(x, 'dp', [(i, i ^ 1 << bit) for i in range(size)])  48.1 us
    pallas_call x1, Pallas kernels, attention_backward(): pl.pallas_call(backward_kernel, grid=(pairs,), in_specs=[pl.BlockSpec(mem...  42.9 us
    dot_general x8, matrix products, nt(): lax.dot_general(left, right, (((1,), (1,)), ((), ())), preferred_element_...  38.9 us
    ppermute x9, starting transfers between devices, from_next(): lax.ppermute(x, 'tensor', [((i + step) % size, i) for i in range(size)])  35.4 us
    ppermute x44, starting transfers between devices, flip(): return lax.ppermute(x, 'dp', [(i, i ^ 1 << bit) for i in range(size)])  34.1 us
    ppermute x9, waiting for transfers between devices, from_next(): lax.ppermute(x, 'tensor', [((i + step) % size, i) for i in range(size)])  33.1 us
    ppermute x1, waiting for transfers between devices, __init__(): self.first = lax.ppermute(near(jnp.where(self.outer, 3, 0)), 'tensor', swap)  23.7 us
  transfers between devices with their start and end apart: 71, of which 25 were waited for; matrix products, arithmetic and copies ran while one was open for 29% of the time, Pallas kernels for 14%

profile of v4, /device:TPU:0, one launch (start us, length us, event | category | flops | bytes accessed | tf_op | source)
XLA Modules:
  0.0 544.6 jit_solution(9791788648656173025)
XLA Ops:
  19.8 6.6 %collective-permute-done.2 = f32[104,768]{1,0:T(8,128)S(1)} collective-permute-done((f32[104,768]{1,0:T(8,128)S(1)}, f32[104,768]{1,0:T(8,128)S(1)}, u32[]{:S(2)}, u32[]{:S(2)}) %collective-permute-start.2) | collective-permute-done | bytes 319520 | tf_op jit(solution)/shard_map/ppermute | solution.py:57
  26.4 12.8 %collective-permute-done.1 = f32[104,768]{1,0:T(8,128)S(1)} collective-permute-done((f32[104,768]{1,0:T(8,128)S(1)}, f32[104,768]{1,0:T(8,128)S(1)}, u32[]{:S(2)}, u32[]{:S(2)}) %collective-permute-start.1) | collective-permute-done | bytes 319520 | tf_op jit(solution)/shard_map/ppermute | solution.py:57
  46.7 7.5 %collective-permute-done.3 = f32[3,56,768]{2,1,0:T(8,128)} collective-permute-done((f32[3,56,768]{2,1,0:T(8,128)}, f32[3,56,768]{2,1,0:T(8,128)}, u32[]{:S(2)}, u32[]{:S(2)}) %collective-permute-start.3) | collective-permute-done | bytes 516128 | tf_op jit(solution)/shard_map/ppermute | solution.py:52
  63.1 7.4 %collective-permute-start.11 = (f32[96,768]{1,0:T(8,128)}, f32[96,768]{1,0:T(8,128)}, u32[]{:S(2)}, u32[]{:S(2)}) collective-permute-start(f32[96,768]{1,0:T(8,128)} %multiply_bitcast_fusion.1), channel_id=1, source_target_pairs={{1,0},{2,1},{3,2},{0,3},{5,4},{6,5},{7,6},{4,7},{9,8},{10,9},{11,1... | collective-permute-start | bytes 884744 | tf_op jit(solution)/shard_map/ppermute | solution.py:57
  77.2 16.2 %collective-permute-start.13 = (f32[96,768]{1,0:T(8,128)}, f32[96,768]{1,0:T(8,128)S(1)}, u32[]{:S(2)}, u32[]{:S(2)}) collective-permute-start(f32[96,768]{1,0:T(8,128)} %multiply_bitcast_fusion.1), channel_id=1, source_target_pairs={{3,0},{0,1},{1,2},{2,3},{7,4},{4,5},{5,6},{6,7},{11,8},{8,9},{9,10... | collective-permute-start | bytes 884744 | tf_op jit(solution)/shard_map/ppermute | solution.py:57
  103.0 7.0 %shard_map.254 = bf16[4,4,3,4,16,768]{5,4,3,2,1,0:T(8,128)(2,1)} custom-call(s32[1]{0:T(128)} %bitcast.me_ref, f32[12,8,8,768]{3,2,1,0:T(8,128)} %bitcast.296, f32[12,8,8,768]{3,2,1,0:T(8,128)} %bitcast.297, f32[2,3,56,768]{3,2,1,0:T(8,128)} %pad_maximum_fusion.3.refs_0_, f32[2,3,56,768]{3,2,1,0:T(8,128)} %collective-permute-done.4.refs_1_, ...), custom_call_target="tpu_custom_call" | custom-call | tf_op jit(solution)/shard_map/pallas_call | solution.py:112
  127.2 9.0 %collective-permute-done.17 = f32[96,768]{1,0:T(8,128)} collective-permute-done((f32[96,768]{1,0:T(8,128)S(1)}, f32[96,768]{1,0:T(8,128)}, u32[]{:S(2)}, u32[]{:S(2)}) %collective-permute-start.17) | collective-permute-done | bytes 294944 | tf_op jit(solution)/shard_map/ppermute | solution.py:57
  144.2 15.1 %shard_map.255 = (bf16[768,512]{1,0:T(8,128)(2,1)S(1)}, f32[6,2,512]{2,1,0:T(2,128)S(1)}) custom-call(s32[1]{0:T(128)} %get-tuple-element.244.length_ref, bf16[512,768]{1,0:T(8,128)(2,1)S(1)} %copy-done.6, bf16[1024,768]{1,0:T(8,128)(2,1)S(1)} %convolution_convert_fusion.k_ref, bf16[1024,768]{1,0:T(8,128)(2,1)S(1)} %add_convert_fusion.2.v_ref), custom_call_target="tpu_custom_call" | custom-call | flops 393216 | bytes 1048576 | tf_op jit(solution)/shard_map/pallas_call | solution.py:361
  165.4 4.6 shard_map.256
  173.0 10.4 %collective-permute-done.24.b_far_ref = f32[2,3,48,768]{3,2,1,0:T(8,128)S(1)} collective-permute-done((f32[2,3,48,768]{3,2,1,0:T(8,128)S(1)}, f32[2,3,48,768]{3,2,1,0:T(8,128)S(1)}, u32[]{:S(2)}, u32[]{:S(2)}) %collective-permute-start.24) | collective-permute-done | bytes 884768 | tf_op jit(solution)/shard_map/ppermute | solution.py:52
  183.3 9.8 %multiply_convert_fusion.2 = (bf16[512,1536]{1,0:T(8,128)(2,1)}, f32[512,1536]{1,0:T(8,128)}, f32[512,1536]{1,0:T(8,128)}) fusion(f32[1536]{0:T(1024)S(1)} %add.605, bf16[512,768]{1,0:T(8,128)(2,1)S(1)} %fusion.17, bf16[1536,768]{1,0:T(8,128)(2,1)S(1)} %bitcast.319), kind=kOutput, calls=%fused_computation.33 | convolution fusion | flops 1259864064 | bytes 11016192 | tf_op jit(solution)/shard_map/dot_general | solution.py:32
  199.8 11.3 %multiply_convert_fusion.1 = (bf16[512,1536]{1,0:T(8,128)(2,1)}, f32[512,1536]{1,0:T(8,128)}, f32[512,1536]{1,0:T(8,128)}) fusion(f32[1536]{0:T(1024)S(1)} %add.608, bf16[512,768]{1,0:T(8,128)(2,1)S(1)} %fusion.17, bf16[1536,768]{1,0:T(8,128)(2,1)} %bitcast.321), kind=kOutput, calls=%fused_computation.20 | convolution fusion | flops 1259864064 | bytes 11016192 | tf_op jit(solution)/shard_map/dot_general | solution.py:32
  238.0 4.0 slice_bitcast_fusion.6
  243.2 4.1 add_convert_fusion
  247.3 5.0 convolution_add_fusion.1
  252.4 4.6 convolution_add_fusion
  272.3 42.9 %shard_map.260 = (f32[4,4,96,768]{3,2,1,0:T(8,128)}, f32[4,4,96,768]{3,2,1,0:T(8,128)}, f32[6,2,128]{2,1,0:T(2,128)}, f32[768,1024]{1,0:T(8,128)}) custom-call(s32[2]{0:T(128)} %pad_add_fusion.scalars_ref, bf16[512,768]{1,0:T(8,128)(2,1)} %fusion.16.q_ref, bf16[1024,768]{1,0:T(8,128)(2,1)} %copy-done.3, bf16[1024,768]{1,0:T(8,128)(2,1)} %copy-done.4, ...), custom_call_target="tpu_custom_call" | custom-call | flops 393216 | bytes 1048576 | tf_op jit(solution)/shard_map/pallas_call | solution.py:386
  315.4 4.0 fusion.18
  331.7 4.4 slice_add_fusion.1
  344.0 8.4 %collective-permute-done.41 = f32[4,96,768]{2,1,0:T(8,128)} collective-permute-done((f32[4,96,768]{2,1,0:T(8,128)}, f32[4,96,768]{2,1,0:T(8,128)}, u32[]{:S(2)}, u32[]{:S(2)}) %collective-permute-start.41) | collective-permute-done | bytes 1179680 | tf_op jit(solution)/shard_map/ppermute | solution.py:52
  358.0 7.8 %collective-permute-done.43 = f32[192,1024]{1,0:T(8,128)} collective-permute-done((f32[192,1024]{1,0:T(8,128)}, f32[192,1024]{1,0:T(8,128)}, u32[]{:S(2)}, u32[]{:S(2)}) %collective-permute-start.43) | collective-permute-done | bytes 786464 | tf_op jit(solution)/shard_map/ppermute | solution.py:419
  368.2 23.7 %collective-permute-done.37 = f32[192,1024]{1,0:T(8,128)} collective-permute-done((f32[192,1024]{1,0:T(8,128)}, f32[192,1024]{1,0:T(8,128)}, u32[]{:S(2)}, u32[]{:S(2)}) %collective-permute-start.37) | collective-permute-done | bytes 786464 | tf_op jit(solution)/shard_map/ppermute | solution.py:418
  394.3 13.8 %collective-permute-done.42 = f32[192,768]{1,0:T(8,128)S(1)} collective-permute-done((f32[192,768]{1,0:T(8,128)}, f32[192,768]{1,0:T(8,128)S(1)}, u32[]{:S(2)}, u32[]{:S(2)}) %collective-permute-start.42) | collective-permute-done | bytes 589856 | tf_op jit(solution)/shard_map/ppermute | solution.py:62
  413.8 10.8 %collective-permute-done.46 = f32[2,96,768]{2,1,0:T(8,128)S(1)} collective-permute-done((f32[2,96,768]{2,1,0:T(8,128)S(1)}, f32[2,96,768]{2,1,0:T(8,128)S(1)}, u32[]{:S(2)}, u32[]{:S(2)}) %collective-permute-start.46) | collective-permute-done | bytes 589856 | tf_op jit(solution)/shard_map/ppermute | solution.py:52
  430.8 7.0 %collective-permute-done.47 = f32[96,768]{1,0:T(8,128)S(1)} collective-permute-done((f32[96,768]{1,0:T(8,128)S(1)}, f32[96,768]{1,0:T(8,128)S(1)}, u32[]{:S(2)}, u32[]{:S(2)}) %collective-permute-start.47) | collective-permute-done | bytes 294944 | tf_op jit(solution)/shard_map/ppermute | solution.py:62
  437.9 17.4 %collective-permute-done.48 = f32[96,768]{1,0:T(8,128)S(1)} collective-permute-done((f32[96,768]{1,0:T(8,128)S(1)}, f32[96,768]{1,0:T(8,128)S(1)}, u32[]{:S(2)}, u32[]{:S(2)}) %collective-permute-start.48) | collective-permute-done | bytes 294944 | tf_op jit(solution)/shard_map/ppermute | solution.py:62
  456.3 8.4 %collective-permute-done.49 = f32[96,768]{1,0:T(8,128)S(1)} collective-permute-done((f32[96,768]{1,0:T(8,128)S(1)}, f32[96,768]{1,0:T(8,128)S(1)}, u32[]{:S(2)}, u32[]{:S(2)}) %collective-permute-start.49) | collective-permute-done | bytes 294944 | tf_op jit(solution)/shard_map/ppermute | solution.py:62
  466.1 3.9 collective-permute-done.51
  470.3 4.6 collective-permute-done.52
  481.0 4.9 multiply_convert_fusion
  486.0 11.6 %collective-permute-start.56 = (f32[192,1024]{1,0:T(8,128)}, f32[192,1024]{1,0:T(8,128)}, u32[]{:S(2)}, u32[]{:S(2)}) collective-permute-start(f32[192,1024]{1,0:T(8,128)} %get-tuple-element.122), channel_id=1, source_target_pairs={{0,1},{3,2},{4,5},{7,6},{8,9},{11,10},{12,13},{15,14},{16,17},{19,... | collective-permute-start | bytes 2359304 | tf_op jit(solution)/shard_map/ppermute | solution.py:427
  505.8 8.6 %collective-permute-done.65 = f32[2,96,768]{2,1,0:T(8,128)} collective-permute-done((f32[2,96,768]{2,1,0:T(8,128)}, f32[2,96,768]{2,1,0:T(8,128)}, u32[]{:S(2)}, u32[]{:S(2)}) %collective-permute-start.65) | collective-permute-done | bytes 589856 | tf_op jit(solution)/shard_map/ppermute | solution.py:52
  (445 shorter events, 209.9 us)
Async XLA Ops:
  7.2 387.1 %all-gather.2.cloned.1.call-start = ((), (), s32[]{:S(2)}) async-start(), calls=%async_computation | async-start | bytes 7864320 | tf_op jit(solution)/shard_map/all_gather | solution.py:545
  15.9 23.4 %collective-permute-start.1 = (f32[104,768]{1,0:T(8,128)S(1)}, f32[104,768]{1,0:T(8,128)S(1)}, u32[]{:S(2)}, u32[]{:S(2)}) collective-permute-start(f32[104,768]{1,0:T(8,128)S(1)} %fusion.41), channel_id=1, source_target_pairs={{2,0},{3,1},{0,2},{1,3},{6,4},{7,5},{4,6},{5,7},{10,8},{11,9},{8,1... | collective-permute-start | bytes 958472 | tf_op jit(solution)/shard_map/ppermute | solution.py:57
  18.4 20.8 %collective-permute-start = (f32[104,768]{1,0:T(8,128)S(1)}, f32[104,768]{1,0:T(8,128)S(1)}, u32[]{:S(2)}, u32[]{:S(2)}) collective-permute-start(f32[104,768]{1,0:T(8,128)S(1)} %fusion.41), channel_id=1, source_target_pairs={{1,0},{2,1},{3,2},{0,3},{5,4},{6,5},{7,6},{4,7},{9,8},{10,9},{11,1... | collective-permute-start | bytes 958472 | tf_op jit(solution)/shard_map/ppermute | solution.py:57
  56.4 40.8 %collective-permute-start.4 = (f32[2,3,56,768]{3,2,1,0:T(8,128)}, f32[2,3,56,768]{3,2,1,0:T(8,128)}, u32[]{:S(2)}, u32[]{:S(2)}) collective-permute-start(f32[2,3,56,768]{3,2,1,0:T(8,128)} %pad_maximum_fusion.3.refs_0_), channel_id=1, source_target_pairs={{0,16},{4,20},{8,24},{12,28},{16,0},{20,4},{24,8},{28,12},{1,17},{... | collective-permute-start | bytes 3096584 | tf_op jit(solution)/shard_map/ppermute | solution.py:52
  60.0 36.8 %collective-permute-start.6 = (f32[2,3,48,768]{3,2,1,0:T(8,128)}, f32[2,3,48,768]{3,2,1,0:T(8,128)}, u32[]{:S(2)}, u32[]{:S(2)}) collective-permute-start(f32[2,3,48,768]{3,2,1,0:T(8,128)} %pad_maximum_fusion.7.refs_2_), channel_id=1, source_target_pairs={{0,8},{4,12},{8,0},{12,4},{16,24},{20,28},{24,16},{28,20},{1,9},{5... | collective-permute-start | bytes 2654216 | tf_op jit(solution)/shard_map/ppermute | solution.py:52
  72.7 23.9 %collective-permute-start.12 = (f32[96,768]{1,0:T(8,128)}, f32[96,768]{1,0:T(8,128)S(1)}, u32[]{:S(2)}, u32[]{:S(2)}) collective-permute-start(f32[96,768]{1,0:T(8,128)} %multiply_bitcast_fusion.1), channel_id=1, source_target_pairs={{2,0},{3,1},{0,2},{1,3},{6,4},{7,5},{4,6},{5,7},{10,8},{11,9},{8,1... | collective-permute-start | bytes 884744 | tf_op jit(solution)/shard_map/ppermute | solution.py:57
  74.1 25.2 %collective-permute-start.7 = (f32[2,3,56,768]{3,2,1,0:T(8,128)}, f32[2,3,56,768]{3,2,1,0:T(8,128)}, u32[]{:S(2)}, u32[]{:S(2)}) collective-permute-start(f32[2,3,56,768]{3,2,1,0:T(8,128)} %pad_maximum_fusion.3.refs_0_), channel_id=1, source_target_pairs={{0,4},{4,0},{8,12},{12,8},{16,20},{20,16},{24,28},{28,24},{1,5},{5... | collective-permute-start | bytes 3096584 | tf_op jit(solution)/shard_map/ppermute | solution.py:52
  77.2 20.8 %collective-permute-start.13 = (f32[96,768]{1,0:T(8,128)}, f32[96,768]{1,0:T(8,128)S(1)}, u32[]{:S(2)}, u32[]{:S(2)}) collective-permute-start(f32[96,768]{1,0:T(8,128)} %multiply_bitcast_fusion.1), channel_id=1, source_target_pairs={{3,0},{0,1},{1,2},{2,3},{7,4},{4,5},{5,6},{6,7},{11,8},{8,9},{9,10... | collective-permute-start | bytes 884744 | tf_op jit(solution)/shard_map/ppermute | solution.py:57
  110.3 25.9 %collective-permute-start.17 = (f32[96,768]{1,0:T(8,128)S(1)}, f32[96,768]{1,0:T(8,128)}, u32[]{:S(2)}, u32[]{:S(2)}) collective-permute-start(f32[96,768]{1,0:T(8,128)S(1)} %multiply_bitcast_fusion), channel_id=1, source_target_pairs={{2,0},{3,1},{0,2},{1,3},{6,4},{7,5},{4,6},{5,7},{10,8},{11,9},{8,1... | collective-permute-start | bytes 884744 | tf_op jit(solution)/shard_map/ppermute | solution.py:57
  113.3 23.8 %collective-permute-start.18 = (f32[96,768]{1,0:T(8,128)S(1)}, f32[96,768]{1,0:T(8,128)}, u32[]{:S(2)}, u32[]{:S(2)}) collective-permute-start(f32[96,768]{1,0:T(8,128)S(1)} %multiply_bitcast_fusion), channel_id=1, source_target_pairs={{3,0},{0,1},{1,2},{2,3},{7,4},{4,5},{5,6},{6,7},{11,8},{8,9},{9,10... | collective-permute-start | bytes 884744 | tf_op jit(solution)/shard_map/ppermute | solution.py:57
  114.3 49.5 %collective-permute-start.20 = (f32[2,3,48,768]{3,2,1,0:T(8,128)}, f32[2,3,48,768]{3,2,1,0:T(8,128)}, u32[]{:S(2)}, u32[]{:S(2)}) collective-permute-start(f32[2,3,48,768]{3,2,1,0:T(8,128)} %pad_maximum_fusion.9.b_ref), channel_id=1, source_target_pairs={{0,8},{4,12},{8,0},{12,4},{16,24},{20,28},{24,16},{28,20},{1,9},{5... | collective-permute-start | bytes 2654216 | tf_op jit(solution)/shard_map/ppermute | solution.py:52
  116.8 48.6 %collective-permute-start.19 = (f32[2,3,48,768]{3,2,1,0:T(8,128)}, f32[2,3,48,768]{3,2,1,0:T(8,128)}, u32[]{:S(2)}, u32[]{:S(2)}) collective-permute-start(f32[2,3,48,768]{3,2,1,0:T(8,128)} %pad_maximum_fusion.8.a_ref), channel_id=1, source_target_pairs={{0,16},{4,20},{8,24},{12,28},{16,0},{20,4},{24,8},{28,12},{1,17},{... | collective-permute-start | bytes 2654216 | tf_op jit(solution)/shard_map/ppermute | solution.py:52
  126.1 69.5 %collective-permute-start.27 = (f32[2,3,48,768]{3,2,1,0:T(8,128)}, f32[2,3,48,768]{3,2,1,0:T(8,128)}, u32[]{:S(2)}, u32[]{:S(2)}) collective-permute-start(f32[2,3,48,768]{3,2,1,0:T(8,128)} %pad_maximum_fusion.9.b_ref), channel_id=1, source_target_pairs={{0,4},{4,0},{8,12},{12,8},{16,20},{20,16},{24,28},{28,24},{1,5},{5... | collective-permute-start | bytes 2654216 | tf_op jit(solution)/shard_map/ppermute | solution.py:52
  160.0 35.7 %collective-permute-start.25 = (f32[2,3,48,768]{3,2,1,0:T(8,128)}, f32[2,3,48,768]{3,2,1,0:T(8,128)S(1)}, u32[]{:S(2)}, u32[]{:S(2)}) collective-permute-start(f32[2,3,48,768]{3,2,1,0:T(8,128)} %pad_maximum_fusion.8.a_ref), channel_id=1, source_target_pairs={{0,4},{4,0},{8,12},{12,8},{16,20},{20,16},{24,28},{28,24},{1,5},{5... | collective-permute-start | bytes 2654216 | tf_op jit(solution)/shard_map/ppermute | solution.py:52
  161.5 21.8 %collective-permute-start.24 = (f32[2,3,48,768]{3,2,1,0:T(8,128)S(1)}, f32[2,3,48,768]{3,2,1,0:T(8,128)S(1)}, u32[]{:S(2)}, u32[]{:S(2)}) collective-permute-start(f32[2,3,48,768]{3,2,1,0:T(8,128)S(1)} %pad_maximum_fusion.11.b_ref), channel_id=1, source_target_pairs={{0,8},{4,12},{8,0},{12,4},{16,24},{20,28},{24,16},{28,20},{1,9},{5... | collective-permute-start | bytes 2654216 | tf_op jit(solution)/shard_map/ppermute | solution.py:52
  163.8 29.4 %collective-permute-start.23 = (f32[2,3,48,768]{3,2,1,0:T(8,128)S(1)}, f32[2,3,48,768]{3,2,1,0:T(8,128)S(1)}, u32[]{:S(2)}, u32[]{:S(2)}) collective-permute-start(f32[2,3,48,768]{3,2,1,0:T(8,128)S(1)} %pad_maximum_fusion.10.a_ref), channel_id=1, source_target_pairs={{0,16},{4,20},{8,24},{12,28},{16,0},{20,4},{24,8},{28,12},{1,17},{... | collective-permute-start | bytes 2654216 | tf_op jit(solution)/shard_map/ppermute | solution.py:52
  165.4 30.7 %collective-permute-start.28 = (f32[2,3,48,768]{3,2,1,0:T(8,128)}, f32[2,3,48,768]{3,2,1,0:T(8,128)S(1)}, u32[]{:S(2)}, u32[]{:S(2)}) collective-permute-start(f32[2,3,48,768]{3,2,1,0:T(8,128)} %collective-permute-done.20.b_far_ref), channel_id=1, source_target_pairs={{0,4},{4,0},{8,12},{12,8},{16,20},{20,16},{24,28},{28,24},{1,5},{5... | collective-permute-start | bytes 2654216 | tf_op jit(solution)/shard_map/ppermute | solution.py:52
  261.5 53.8 %collective-permute-start.36 = (f32[2,4,96,768]{3,2,1,0:T(8,128)}, f32[2,4,96,768]{3,2,1,0:T(8,128)}, u32[]{:S(2)}, u32[]{:S(2)}) collective-permute-start(f32[2,4,96,768]{3,2,1,0:T(8,128)} %slice_bitcast_fusion), channel_id=1, source_target_pairs={{0,8},{4,12},{8,0},{12,4},{16,24},{20,28},{24,16},{28,20},{1,9},{5... | collective-permute-start | bytes 7077896 | tf_op jit(solution)/shard_map/ppermute | solution.py:52
  262.2 53.2 %collective-permute-start.35 = (f32[2,4,96,768]{3,2,1,0:T(8,128)}, f32[2,4,96,768]{3,2,1,0:T(8,128)}, u32[]{:S(2)}, u32[]{:S(2)}) collective-permute-start(f32[2,4,96,768]{3,2,1,0:T(8,128)} %bitcast.67), channel_id=1, source_target_pairs={{0,16},{4,20},{8,24},{12,28},{16,0},{20,4},{24,8},{28,12},{1,17},{... | collective-permute-start | bytes 7077896 | tf_op jit(solution)/shard_map/ppermute | solution.py:52
  323.3 29.1 %collective-permute-start.41 = (f32[4,96,768]{2,1,0:T(8,128)}, f32[4,96,768]{2,1,0:T(8,128)}, u32[]{:S(2)}, u32[]{:S(2)}) collective-permute-start(f32[4,96,768]{2,1,0:T(8,128)} %get-tuple-element.189), channel_id=1, source_target_pairs={{0,8},{4,12},{8,0},{12,4},{16,24},{20,28},{24,16},{28,20},{1,9},{5... | collective-permute-start | bytes 3538952 | tf_op jit(solution)/shard_map/ppermute | solution.py:52
  324.7 29.2 %collective-permute-start.40 = (f32[4,96,768]{2,1,0:T(8,128)}, f32[4,96,768]{2,1,0:T(8,128)}, u32[]{:S(2)}, u32[]{:S(2)}) collective-permute-start(f32[4,96,768]{2,1,0:T(8,128)} %get-tuple-element.187), channel_id=1, source_target_pairs={{0,16},{4,20},{8,24},{12,28},{16,0},{20,4},{24,8},{28,12},{1,17},{... | collective-permute-start | bytes 3538952 | tf_op jit(solution)/shard_map/ppermute | solution.py:52
  328.8 37.1 %collective-permute-start.43 = (f32[192,1024]{1,0:T(8,128)}, f32[192,1024]{1,0:T(8,128)}, u32[]{:S(2)}, u32[]{:S(2)}) collective-permute-start(f32[192,1024]{1,0:T(8,128)} %get-tuple-element.195), channel_id=1, source_target_pairs={{0,1},{3,2},{4,5},{7,6},{8,9},{11,10},{12,13},{15,14},{16,17},{19,... | collective-permute-start | bytes 2359304 | tf_op jit(solution)/shard_map/ppermute | solution.py:419
  331.7 60.2 %collective-permute-start.37 = (f32[192,1024]{1,0:T(8,128)}, f32[192,1024]{1,0:T(8,128)}, u32[]{:S(2)}, u32[]{:S(2)}) collective-permute-start(f32[192,1024]{1,0:T(8,128)} %get-tuple-element.196), channel_id=1, source_target_pairs={{0,1},{1,0},{2,3},{3,2},{4,5},{5,4},{6,7},{7,6},{8,9},{9,8},{10,11... | collective-permute-start | bytes 2359304 | tf_op jit(solution)/shard_map/ppermute | solution.py:418
  338.6 69.6 %collective-permute-start.45 = (f32[2,2,96,768]{3,2,1,0:T(8,128)}, f32[2,2,96,768]{3,2,1,0:T(8,128)}, u32[]{:S(2)}, u32[]{:S(2)}) collective-permute-start(f32[2,2,96,768]{3,2,1,0:T(8,128)} %slice_bitcast_fusion.1), channel_id=1, source_target_pairs={{0,8},{4,12},{8,0},{12,4},{16,24},{20,28},{24,16},{28,20},{1,9},{5... | collective-permute-start | bytes 3538952 | tf_op jit(solution)/shard_map/ppermute | solution.py:52
  356.2 51.9 %collective-permute-start.42 = (f32[192,768]{1,0:T(8,128)}, f32[192,768]{1,0:T(8,128)S(1)}, u32[]{:S(2)}, u32[]{:S(2)}) collective-permute-start(f32[192,768]{1,0:T(8,128)} %fusion.34), channel_id=1, source_target_pairs={{0,1},{1,2},{2,3},{3,0},{4,5},{5,6},{6,7},{7,4},{8,9},{9,10},{10,1... | collective-permute-start | bytes 1769480 | tf_op jit(solution)/shard_map/ppermute | solution.py:62
  356.3 54.7 %collective-permute-start.39 = (f32[2,2,96,768]{3,2,1,0:T(8,128)}, f32[2,2,96,768]{3,2,1,0:T(8,128)}, u32[]{:S(2)}, u32[]{:S(2)}) collective-permute-start(f32[2,2,96,768]{3,2,1,0:T(8,128)} %slice.375), channel_id=1, source_target_pairs={{0,16},{4,20},{8,24},{12,28},{16,0},{20,4},{24,8},{28,12},{1,17},{... | collective-permute-start | bytes 3538952 | tf_op jit(solution)/shard_map/ppermute | solution.py:52
  430.7 24.7 %collective-permute-start.60 = (f32[192,768]{1,0:T(8,128)S(1)}, f32[192,768]{1,0:T(8,128)S(1)}, u32[]{:S(2)}, u32[]{:S(2)}) collective-permute-start(f32[192,768]{1,0:T(8,128)S(1)} %fusion.36), channel_id=1, source_target_pairs={{0,1},{1,2},{2,3},{3,0},{4,5},{5,6},{6,7},{7,4},{8,9},{9,10},{10,1... | collective-permute-start | bytes 1769480 | tf_op jit(solution)/shard_map/ppermute | solution.py:62
  455.5 21.1 %collective-permute-start.61 = (f32[1,96,768]{2,1,0:T(8,128)S(1)}, f32[1,96,768]{2,1,0:T(8,128)S(1)}, u32[]{:S(2)}, u32[]{:S(2)}) collective-permute-start(f32[1,96,768]{2,1,0:T(8,128)S(1)} %get-tuple-element.201), channel_id=1, source_target_pairs={{0,8},{4,12},{8,0},{12,4},{16,24},{20,28},{24,16},{28,20},{1,9},{5... | collective-permute-start | bytes 884744 | tf_op jit(solution)/shard_map/ppermute | solution.py:52
  470.1 27.4 %collective-permute-start.64 = (f32[1,96,768]{2,1,0:T(8,128)S(1)}, f32[1,96,768]{2,1,0:T(8,128)S(1)}, u32[]{:S(2)}, u32[]{:S(2)}) collective-permute-start(f32[1,96,768]{2,1,0:T(8,128)S(1)} %get-tuple-element.200), channel_id=1, source_target_pairs={{0,16},{4,20},{8,24},{12,28},{16,0},{20,4},{24,8},{28,12},{1,17},{... | collective-permute-start | bytes 884744 | tf_op jit(solution)/shard_map/ppermute | solution.py:52
  477.4 27.0 %collective-permute-start.62 = (f32[2,96,768]{2,1,0:T(8,128)}, f32[2,96,768]{2,1,0:T(8,128)}, u32[]{:S(2)}, u32[]{:S(2)}) collective-permute-start(f32[2,96,768]{2,1,0:T(8,128)} %pad_maximum_fusion.14), channel_id=1, source_target_pairs={{0,16},{4,20},{8,24},{12,28},{16,0},{20,4},{24,8},{28,12},{1,17},{... | collective-permute-start | bytes 1769480 | tf_op jit(solution)/shard_map/ppermute | solution.py:52
  478.9 21.6 %collective-permute-start.57 = (f32[1,96,768]{2,1,0:T(8,128)S(1)}, f32[1,96,768]{2,1,0:T(8,128)S(1)}, u32[]{:S(2)}, u32[]{:S(2)}) collective-permute-start(f32[1,96,768]{2,1,0:T(8,128)S(1)} %bitcast.312), channel_id=1, source_target_pairs={{0,16},{4,20},{8,24},{12,28},{16,0},{20,4},{24,8},{28,12},{1,17},{... | collective-permute-start | bytes 884744 | tf_op jit(solution)/shard_map/ppermute | solution.py:52
  486.0 31.2 %collective-permute-start.56 = (f32[192,1024]{1,0:T(8,128)}, f32[192,1024]{1,0:T(8,128)}, u32[]{:S(2)}, u32[]{:S(2)}) collective-permute-start(f32[192,1024]{1,0:T(8,128)} %get-tuple-element.122), channel_id=1, source_target_pairs={{0,1},{3,2},{4,5},{7,6},{8,9},{11,10},{12,13},{15,14},{16,17},{19,... | collective-permute-start | bytes 2359304 | tf_op jit(solution)/shard_map/ppermute | solution.py:427
  (101 other events, 1041.5 us)
Sparse Core Ops, SparseCore 0:
  247.4 136.8 all-gather.1

commit v5 on v4

--- a/solution.py
+++ b/solution.py
@@ -482,7 +482,7 @@
     down_piece = mine(down_blocks, 0).astype(F32) * one
 
     heads_places = gather_halves(heads_piece, 2 * few + 8)
-    heads_first = both_first(heads_places)
+    heads_first = both_first(heads_places, lambda x: after(x, up_piece, down_piece))
     up_places = gather_halves(after(up_piece, heads_places), count // 2)
     heads_far = both_second(heads_first)
     heads_other = [flip(part, 0) for part in heads_far]

time: 553 us -> 548 us (level)
  starting transfers between devices: 89.6 us -> 72.1 us
  waiting for transfers between devices: 172 us -> 187 us
    ppermute x9, starting transfers between devices: 35.4 us -> 18 us  [from_next(): lax.ppermute(x, 'tensor', [((i + step) % size, i) for i in range(size)])]
    ppermute x9, waiting for transfers between devices: 33.1 us -> 49.5 us  [from_next(): lax.ppermute(x, 'tensor', [((i + step) % size, i) for i in range(size)])]
  transfers between devices with their start and end apart: 71 -> 71, of which waited for: 25 -> 24; matrix products, arithmetic and copies ran while one was open for 29% -> 29% of each run, Pallas kernels for 14% -> 14%
where the time goes in v5:
time: 548 us; the launch traced here: 539 us
  waiting for transfers between devices  187 us (34%)
  Pallas kernels  77.4 us (14%)
  starting transfers between devices  72.1 us (13%)
  other arithmetic  71.1 us (13%)
  matrix products  67.3 us (12%)
  local copies, waits for them, and re-layouts  47.9 us (9%)
  between operations  16.9 us (3%)
    ppermute x9, waiting for transfers between devices, from_next(): lax.ppermute(x, 'tensor', [((i + step) % size, i) for i in range(size)])  49.5 us
    ppermute x6, waiting for transfers between devices, to_next(): lax.ppermute(x, 'tensor', [(i, (i + step) % size) for i in range(size)])  49.1 us
    ppermute x44, waiting for transfers between devices, flip(): return lax.ppermute(x, 'dp', [(i, i ^ 1 << bit) for i in range(size)])  47 us
    pallas_call x1, Pallas kernels, attention_backward(): pl.pallas_call(backward_kernel, grid=(pairs,), in_specs=[pl.BlockSpec(mem...  42.9 us
    dot_general x8, matrix products, nt(): lax.dot_general(left, right, (((1,), (1,)), ((), ())), preferred_element_...  38.9 us
    ppermute x44, starting transfers between devices, flip(): return lax.ppermute(x, 'dp', [(i, i ^ 1 << bit) for i in range(size)])  33.7 us
    ppermute x1, waiting for transfers between devices, __init__(): self.first = lax.ppermute(near(jnp.where(self.outer, 3, 0)), 'tensor', swap)  22.5 us
    dot_general x5, matrix products, tn(): lax.dot_general(left, right, (((0,), (0,)), ((), ())), preferred_element_...  19.1 us
  transfers between devices with their start and end apart: 71, of which 24 were waited for; matrix products, arithmetic and copies ran while one was open for 29% of the time, Pallas kernels for 14%

profile of v5, /device:TPU:0, one launch (start us, length us, event | category | flops | bytes accessed | tf_op | source)
XLA Modules:
  0.0 539.5 jit_solution(13724314386962272134)
XLA Ops:
  19.8 6.6 %collective-permute-done.2 = f32[104,768]{1,0:T(8,128)S(1)} collective-permute-done((f32[104,768]{1,0:T(8,128)S(1)}, f32[104,768]{1,0:T(8,128)S(1)}, u32[]{:S(2)}, u32[]{:S(2)}) %collective-permute-start.2) | collective-permute-done | bytes 319520 | tf_op jit(solution)/shard_map/ppermute | solution.py:57
  26.4 12.8 %collective-permute-done.1 = f32[104,768]{1,0:T(8,128)S(1)} collective-permute-done((f32[104,768]{1,0:T(8,128)S(1)}, f32[104,768]{1,0:T(8,128)S(1)}, u32[]{:S(2)}, u32[]{:S(2)}) %collective-permute-start.1) | collective-permute-done | bytes 319520 | tf_op jit(solution)/shard_map/ppermute | solution.py:57
  48.6 5.6 %collective-permute-done.3 = f32[3,56,768]{2,1,0:T(8,128)} collective-permute-done((f32[3,56,768]{2,1,0:T(8,128)}, f32[3,56,768]{2,1,0:T(8,128)}, u32[]{:S(2)}, u32[]{:S(2)}) %collective-permute-start.3) | collective-permute-done | bytes 516128 | tf_op jit(solution)/shard_map/ppermute | solution.py:52
  58.0 7.4 %collective-permute-start.11 = (f32[96,768]{1,0:T(8,128)}, f32[96,768]{1,0:T(8,128)S(1)}, u32[]{:S(2)}, u32[]{:S(2)}) collective-permute-start(f32[96,768]{1,0:T(8,128)} %get-tuple-element.75), channel_id=1, source_target_pairs={{1,0},{2,1},{3,2},{0,3},{5,4},{6,5},{7,6},{4,7},{9,8},{10,9},{11,1... | collective-permute-start | bytes 884744 | tf_op jit(solution)/shard_map/ppermute | solution.py:57
  73.0 18.8 %collective-permute-done.12 = f32[96,768]{1,0:T(8,128)} collective-permute-done((f32[96,768]{1,0:T(8,128)}, f32[96,768]{1,0:T(8,128)}, u32[]{:S(2)}, u32[]{:S(2)}) %collective-permute-start.12) | collective-permute-done | bytes 294944 | tf_op jit(solution)/shard_map/ppermute | solution.py:57
  99.3 7.0 %shard_map.254 = bf16[4,4,3,4,16,768]{5,4,3,2,1,0:T(8,128)(2,1)} custom-call(s32[1]{0:T(128)} %bitcast.me_ref, f32[12,8,8,768]{3,2,1,0:T(8,128)} %bitcast.296, f32[12,8,8,768]{3,2,1,0:T(8,128)} %bitcast.297, f32[2,3,56,768]{3,2,1,0:T(8,128)} %pad_maximum_fusion.3.refs_0_, f32[2,3,56,768]{3,2,1,0:T(8,128)} %collective-permute-done.4.refs_1_, ...), custom_call_target="tpu_custom_call" | custom-call | tf_op jit(solution)/shard_map/pallas_call | solution.py:112
  121.2 11.2 %collective-permute-done.17 = f32[96,768]{1,0:T(8,128)} collective-permute-done((f32[96,768]{1,0:T(8,128)}, f32[96,768]{1,0:T(8,128)}, u32[]{:S(2)}, u32[]{:S(2)}) %collective-permute-start.17) | collective-permute-done | bytes 294944 | tf_op jit(solution)/shard_map/ppermute | solution.py:57
  140.0 15.1 %shard_map.255 = (bf16[768,512]{1,0:T(8,128)(2,1)S(1)}, f32[6,2,512]{2,1,0:T(2,128)S(1)}) custom-call(s32[1]{0:T(128)} %get-tuple-element.248.length_ref, bf16[512,768]{1,0:T(8,128)(2,1)S(1)} %copy-done.6, bf16[1024,768]{1,0:T(8,128)(2,1)S(1)} %convolution_convert_fusion.k_ref, bf16[1024,768]{1,0:T(8,128)(2,1)S(1)} %add_convert_fusion.2.v_ref), custom_call_target="tpu_custom_call" | custom-call | flops 393216 | bytes 1048576 | tf_op jit(solution)/shard_map/pallas_call | solution.py:361
  160.3 4.6 shard_map.256
  167.8 10.8 %collective-permute-done.24.b_far_ref = f32[2,3,48,768]{3,2,1,0:T(8,128)S(1)} collective-permute-done((f32[2,3,48,768]{3,2,1,0:T(8,128)S(1)}, f32[2,3,48,768]{3,2,1,0:T(8,128)S(1)}, u32[]{:S(2)}, u32[]{:S(2)}) %collective-permute-start.24) | collective-permute-done | bytes 884768 | tf_op jit(solution)/shard_map/ppermute | solution.py:52
  178.6 9.8 %multiply_convert_fusion.2 = (bf16[512,1536]{1,0:T(8,128)(2,1)}, f32[512,1536]{1,0:T(8,128)}, f32[512,1536]{1,0:T(8,128)}) fusion(f32[1536]{0:T(1024)S(1)} %add.605, bf16[512,768]{1,0:T(8,128)(2,1)S(1)} %fusion.17, bf16[1536,768]{1,0:T(8,128)(2,1)S(1)} %bitcast.319), kind=kOutput, calls=%fused_computation.33 | convolution fusion | flops 1259864064 | bytes 11016192 | tf_op jit(solution)/shard_map/dot_general | solution.py:32
  195.1 11.3 %multiply_convert_fusion.1 = (bf16[512,1536]{1,0:T(8,128)(2,1)}, f32[512,1536]{1,0:T(8,128)}, f32[512,1536]{1,0:T(8,128)}) fusion(f32[1536]{0:T(1024)S(1)} %add.608, bf16[512,768]{1,0:T(8,128)(2,1)S(1)} %fusion.17, bf16[1536,768]{1,0:T(8,128)(2,1)} %bitcast.321), kind=kOutput, calls=%fused_computation.20 | convolution fusion | flops 1259864064 | bytes 11016192 | tf_op jit(solution)/shard_map/dot_general | solution.py:32
  233.3 4.0 slice_bitcast_fusion.6
  238.5 4.1 add_convert_fusion
  242.6 5.0 convolution_add_fusion.1
  247.7 4.7 convolution_add_fusion
  267.3 42.9 %shard_map.260 = (f32[4,4,96,768]{3,2,1,0:T(8,128)}, f32[4,4,96,768]{3,2,1,0:T(8,128)}, f32[6,2,128]{2,1,0:T(2,128)}, f32[768,1024]{1,0:T(8,128)}) custom-call(s32[2]{0:T(128)} %pad_add_fusion.scalars_ref, bf16[512,768]{1,0:T(8,128)(2,1)} %fusion.16.q_ref, bf16[1024,768]{1,0:T(8,128)(2,1)} %copy-done.3, bf16[1024,768]{1,0:T(8,128)(2,1)} %copy-done.4, ...), custom_call_target="tpu_custom_call" | custom-call | flops 393216 | bytes 1048576 | tf_op jit(solution)/shard_map/pallas_call | solution.py:386
  310.4 4.0 fusion.18
  327.9 4.4 slice_add_fusion.1
  339.1 8.3 %collective-permute-done.41 = f32[4,96,768]{2,1,0:T(8,128)} collective-permute-done((f32[4,96,768]{2,1,0:T(8,128)}, f32[4,96,768]{2,1,0:T(8,128)}, u32[]{:S(2)}, u32[]{:S(2)}) %collective-permute-start.41) | collective-permute-done | bytes 1179680 | tf_op jit(solution)/shard_map/ppermute | solution.py:52
  353.1 8.9 %collective-permute-done.43 = f32[192,1024]{1,0:T(8,128)} collective-permute-done((f32[192,1024]{1,0:T(8,128)}, f32[192,1024]{1,0:T(8,128)}, u32[]{:S(2)}, u32[]{:S(2)}) %collective-permute-start.43) | collective-permute-done | bytes 786464 | tf_op jit(solution)/shard_map/ppermute | solution.py:419
  364.4 22.5 %collective-permute-done.37 = f32[192,1024]{1,0:T(8,128)} collective-permute-done((f32[192,1024]{1,0:T(8,128)}, f32[192,1024]{1,0:T(8,128)}, u32[]{:S(2)}, u32[]{:S(2)}) %collective-permute-start.37) | collective-permute-done | bytes 786464 | tf_op jit(solution)/shard_map/ppermute | solution.py:418
  389.2 13.8 %collective-permute-done.42 = f32[192,768]{1,0:T(8,128)S(1)} collective-permute-done((f32[192,768]{1,0:T(8,128)}, f32[192,768]{1,0:T(8,128)S(1)}, u32[]{:S(2)}, u32[]{:S(2)}) %collective-permute-start.42) | collective-permute-done | bytes 589856 | tf_op jit(solution)/shard_map/ppermute | solution.py:62
  408.7 10.8 %collective-permute-done.46 = f32[2,96,768]{2,1,0:T(8,128)S(1)} collective-permute-done((f32[2,96,768]{2,1,0:T(8,128)S(1)}, f32[2,96,768]{2,1,0:T(8,128)S(1)}, u32[]{:S(2)}, u32[]{:S(2)}) %collective-permute-start.46) | collective-permute-done | bytes 589856 | tf_op jit(solution)/shard_map/ppermute | solution.py:52
  425.7 7.0 %collective-permute-done.47 = f32[96,768]{1,0:T(8,128)S(1)} collective-permute-done((f32[96,768]{1,0:T(8,128)S(1)}, f32[96,768]{1,0:T(8,128)S(1)}, u32[]{:S(2)}, u32[]{:S(2)}) %collective-permute-start.47) | collective-permute-done | bytes 294944 | tf_op jit(solution)/shard_map/ppermute | solution.py:62
  432.8 17.4 %collective-permute-done.48 = f32[96,768]{1,0:T(8,128)S(1)} collective-permute-done((f32[96,768]{1,0:T(8,128)S(1)}, f32[96,768]{1,0:T(8,128)S(1)}, u32[]{:S(2)}, u32[]{:S(2)}) %collective-permute-start.48) | collective-permute-done | bytes 294944 | tf_op jit(solution)/shard_map/ppermute | solution.py:62
  451.3 8.4 %collective-permute-done.49 = f32[96,768]{1,0:T(8,128)S(1)} collective-permute-done((f32[96,768]{1,0:T(8,128)S(1)}, f32[96,768]{1,0:T(8,128)S(1)}, u32[]{:S(2)}, u32[]{:S(2)}) %collective-permute-start.49) | collective-permute-done | bytes 294944 | tf_op jit(solution)/shard_map/ppermute | solution.py:62
  461.0 3.9 collective-permute-done.51
  465.2 4.6 collective-permute-done.52
  475.9 4.9 multiply_convert_fusion
  480.9 11.6 %collective-permute-start.56 = (f32[192,1024]{1,0:T(8,128)}, f32[192,1024]{1,0:T(8,128)}, u32[]{:S(2)}, u32[]{:S(2)}) collective-permute-start(f32[192,1024]{1,0:T(8,128)} %get-tuple-element.126), channel_id=1, source_target_pairs={{0,1},{3,2},{4,5},{7,6},{8,9},{11,10},{12,13},{15,14},{16,17},{19,... | collective-permute-start | bytes 2359304 | tf_op jit(solution)/shard_map/ppermute | solution.py:427
  500.7 8.6 %collective-permute-done.65 = f32[2,96,768]{2,1,0:T(8,128)} collective-permute-done((f32[2,96,768]{2,1,0:T(8,128)}, f32[2,96,768]{2,1,0:T(8,128)}, u32[]{:S(2)}, u32[]{:S(2)}) %collective-permute-start.65) | collective-permute-done | bytes 589856 | tf_op jit(solution)/shard_map/ppermute | solution.py:52
  (445 shorter events, 201.5 us)
Async XLA Ops:
  7.2 382.0 %all-gather.2.cloned.1.call-start = ((), (), s32[]{:S(2)}) async-start(), calls=%async_computation | async-start | bytes 7864320 | tf_op jit(solution)/shard_map/all_gather | solution.py:545
  15.9 23.4 %collective-permute-start.1 = (f32[104,768]{1,0:T(8,128)S(1)}, f32[104,768]{1,0:T(8,128)S(1)}, u32[]{:S(2)}, u32[]{:S(2)}) collective-permute-start(f32[104,768]{1,0:T(8,128)S(1)} %fusion.41), channel_id=1, source_target_pairs={{2,0},{3,1},{0,2},{1,3},{6,4},{7,5},{4,6},{5,7},{10,8},{11,9},{8,1... | collective-permute-start | bytes 958472 | tf_op jit(solution)/shard_map/ppermute | solution.py:57
  18.4 20.8 %collective-permute-start = (f32[104,768]{1,0:T(8,128)S(1)}, f32[104,768]{1,0:T(8,128)S(1)}, u32[]{:S(2)}, u32[]{:S(2)}) collective-permute-start(f32[104,768]{1,0:T(8,128)S(1)} %fusion.41), channel_id=1, source_target_pairs={{1,0},{2,1},{3,2},{0,3},{5,4},{6,5},{7,6},{4,7},{9,8},{10,9},{11,1... | collective-permute-start | bytes 958472 | tf_op jit(solution)/shard_map/ppermute | solution.py:57
  42.9 22.5 %collective-permute-start.5 = (f32[3,48,768]{2,1,0:T(8,128)}, f32[3,48,768]{2,1,0:T(8,128)}, u32[]{:S(2)}, u32[]{:S(2)}) collective-permute-start(f32[3,48,768]{2,1,0:T(8,128)} %get-tuple-element.209), channel_id=1, source_target_pairs={{0,16},{4,20},{8,24},{12,28},{16,0},{20,4},{24,8},{28,12},{1,17},{... | collective-permute-start | bytes 1327112 | tf_op jit(solution)/shard_map/ppermute | solution.py:52
  56.4 36.4 %collective-permute-start.4 = (f32[2,3,56,768]{3,2,1,0:T(8,128)}, f32[2,3,56,768]{3,2,1,0:T(8,128)}, u32[]{:S(2)}, u32[]{:S(2)}) collective-permute-start(f32[2,3,56,768]{3,2,1,0:T(8,128)} %pad_maximum_fusion.3.refs_0_), channel_id=1, source_target_pairs={{0,16},{4,20},{8,24},{12,28},{16,0},{20,4},{24,8},{28,12},{1,17},{... | collective-permute-start | bytes 3096584 | tf_op jit(solution)/shard_map/ppermute | solution.py:52
  67.5 26.1 %collective-permute-start.6 = (f32[2,3,48,768]{3,2,1,0:T(8,128)}, f32[2,3,48,768]{3,2,1,0:T(8,128)}, u32[]{:S(2)}, u32[]{:S(2)}) collective-permute-start(f32[2,3,48,768]{3,2,1,0:T(8,128)} %pad_maximum_fusion.7.refs_2_), channel_id=1, source_target_pairs={{0,8},{4,12},{8,0},{12,4},{16,24},{20,28},{24,16},{28,20},{1,9},{5... | collective-permute-start | bytes 2654216 | tf_op jit(solution)/shard_map/ppermute | solution.py:52
  70.2 21.6 %collective-permute-start.12 = (f32[96,768]{1,0:T(8,128)}, f32[96,768]{1,0:T(8,128)}, u32[]{:S(2)}, u32[]{:S(2)}) collective-permute-start(f32[96,768]{1,0:T(8,128)} %get-tuple-element.75), channel_id=1, source_target_pairs={{2,0},{3,1},{0,2},{1,3},{6,4},{7,5},{4,6},{5,7},{10,8},{11,9},{8,1... | collective-permute-start | bytes 884744 | tf_op jit(solution)/shard_map/ppermute | solution.py:57
  72.9 22.0 %collective-permute-start.7 = (f32[2,3,56,768]{3,2,1,0:T(8,128)}, f32[2,3,56,768]{3,2,1,0:T(8,128)S(1)}, u32[]{:S(2)}, u32[]{:S(2)}) collective-permute-start(f32[2,3,56,768]{3,2,1,0:T(8,128)} %pad_maximum_fusion.3.refs_0_), channel_id=1, source_target_pairs={{0,4},{4,0},{8,12},{12,8},{16,20},{20,16},{24,28},{28,24},{1,5},{5... | collective-permute-start | bytes 3096584 | tf_op jit(solution)/shard_map/ppermute | solution.py:52
  106.3 26.1 %collective-permute-start.17 = (f32[96,768]{1,0:T(8,128)}, f32[96,768]{1,0:T(8,128)}, u32[]{:S(2)}, u32[]{:S(2)}) collective-permute-start(f32[96,768]{1,0:T(8,128)} %get-tuple-element.81), channel_id=1, source_target_pairs={{2,0},{3,1},{0,2},{1,3},{6,4},{7,5},{4,6},{5,7},{10,8},{11,9},{8,1... | collective-permute-start | bytes 884744 | tf_op jit(solution)/shard_map/ppermute | solution.py:57
  106.4 27.0 %collective-permute-start.18 = (f32[96,768]{1,0:T(8,128)}, f32[96,768]{1,0:T(8,128)S(1)}, u32[]{:S(2)}, u32[]{:S(2)}) collective-permute-start(f32[96,768]{1,0:T(8,128)} %get-tuple-element.81), channel_id=1, source_target_pairs={{3,0},{0,1},{1,2},{2,3},{7,4},{4,5},{5,6},{6,7},{11,8},{8,9},{9,10... | collective-permute-start | bytes 884744 | tf_op jit(solution)/shard_map/ppermute | solution.py:57
  109.3 49.4 %collective-permute-start.20 = (f32[2,3,48,768]{3,2,1,0:T(8,128)}, f32[2,3,48,768]{3,2,1,0:T(8,128)}, u32[]{:S(2)}, u32[]{:S(2)}) collective-permute-start(f32[2,3,48,768]{3,2,1,0:T(8,128)} %pad_maximum_fusion.9.b_ref), channel_id=1, source_target_pairs={{0,8},{4,12},{8,0},{12,4},{16,24},{20,28},{24,16},{28,20},{1,9},{5... | collective-permute-start | bytes 2654216 | tf_op jit(solution)/shard_map/ppermute | solution.py:52
  111.9 48.4 %collective-permute-start.19 = (f32[2,3,48,768]{3,2,1,0:T(8,128)}, f32[2,3,48,768]{3,2,1,0:T(8,128)}, u32[]{:S(2)}, u32[]{:S(2)}) collective-permute-start(f32[2,3,48,768]{3,2,1,0:T(8,128)} %pad_maximum_fusion.8.a_ref), channel_id=1, source_target_pairs={{0,16},{4,20},{8,24},{12,28},{16,0},{20,4},{24,8},{28,12},{1,17},{... | collective-permute-start | bytes 2654216 | tf_op jit(solution)/shard_map/ppermute | solution.py:52
  120.1 70.8 %collective-permute-start.27 = (f32[2,3,48,768]{3,2,1,0:T(8,128)}, f32[2,3,48,768]{3,2,1,0:T(8,128)}, u32[]{:S(2)}, u32[]{:S(2)}) collective-permute-start(f32[2,3,48,768]{3,2,1,0:T(8,128)} %pad_maximum_fusion.9.b_ref), channel_id=1, source_target_pairs={{0,4},{4,0},{8,12},{12,8},{16,20},{20,16},{24,28},{28,24},{1,5},{5... | collective-permute-start | bytes 2654216 | tf_op jit(solution)/shard_map/ppermute | solution.py:52
  155.2 35.8 %collective-permute-start.25 = (f32[2,3,48,768]{3,2,1,0:T(8,128)}, f32[2,3,48,768]{3,2,1,0:T(8,128)S(1)}, u32[]{:S(2)}, u32[]{:S(2)}) collective-permute-start(f32[2,3,48,768]{3,2,1,0:T(8,128)} %pad_maximum_fusion.8.a_ref), channel_id=1, source_target_pairs={{0,4},{4,0},{8,12},{12,8},{16,20},{20,16},{24,28},{28,24},{1,5},{5... | collective-permute-start | bytes 2654216 | tf_op jit(solution)/shard_map/ppermute | solution.py:52
  156.8 21.8 %collective-permute-start.24 = (f32[2,3,48,768]{3,2,1,0:T(8,128)S(1)}, f32[2,3,48,768]{3,2,1,0:T(8,128)S(1)}, u32[]{:S(2)}, u32[]{:S(2)}) collective-permute-start(f32[2,3,48,768]{3,2,1,0:T(8,128)S(1)} %pad_maximum_fusion.11.b_ref), channel_id=1, source_target_pairs={{0,8},{4,12},{8,0},{12,4},{16,24},{20,28},{24,16},{28,20},{1,9},{5... | collective-permute-start | bytes 2654216 | tf_op jit(solution)/shard_map/ppermute | solution.py:52
  158.7 29.8 %collective-permute-start.23 = (f32[2,3,48,768]{3,2,1,0:T(8,128)S(1)}, f32[2,3,48,768]{3,2,1,0:T(8,128)S(1)}, u32[]{:S(2)}, u32[]{:S(2)}) collective-permute-start(f32[2,3,48,768]{3,2,1,0:T(8,128)S(1)} %pad_maximum_fusion.10.a_ref), channel_id=1, source_target_pairs={{0,16},{4,20},{8,24},{12,28},{16,0},{20,4},{24,8},{28,12},{1,17},{... | collective-permute-start | bytes 2654216 | tf_op jit(solution)/shard_map/ppermute | solution.py:52
  160.3 31.2 %collective-permute-start.28 = (f32[2,3,48,768]{3,2,1,0:T(8,128)}, f32[2,3,48,768]{3,2,1,0:T(8,128)S(1)}, u32[]{:S(2)}, u32[]{:S(2)}) collective-permute-start(f32[2,3,48,768]{3,2,1,0:T(8,128)} %collective-permute-done.20.b_far_ref), channel_id=1, source_target_pairs={{0,4},{4,0},{8,12},{12,8},{16,20},{20,16},{24,28},{28,24},{1,5},{5... | collective-permute-start | bytes 2654216 | tf_op jit(solution)/shard_map/ppermute | solution.py:52
  256.8 53.5 %collective-permute-start.36 = (f32[2,4,96,768]{3,2,1,0:T(8,128)}, f32[2,4,96,768]{3,2,1,0:T(8,128)}, u32[]{:S(2)}, u32[]{:S(2)}) collective-permute-start(f32[2,4,96,768]{3,2,1,0:T(8,128)} %slice_bitcast_fusion), channel_id=1, source_target_pairs={{0,8},{4,12},{8,0},{12,4},{16,24},{20,28},{24,16},{28,20},{1,9},{5... | collective-permute-start | bytes 7077896 | tf_op jit(solution)/shard_map/ppermute | solution.py:52
  257.0 53.4 %collective-permute-start.35 = (f32[2,4,96,768]{3,2,1,0:T(8,128)}, f32[2,4,96,768]{3,2,1,0:T(8,128)}, u32[]{:S(2)}, u32[]{:S(2)}) collective-permute-start(f32[2,4,96,768]{3,2,1,0:T(8,128)} %bitcast.67), channel_id=1, source_target_pairs={{0,16},{4,20},{8,24},{12,28},{16,0},{20,4},{24,8},{28,12},{1,17},{... | collective-permute-start | bytes 7077896 | tf_op jit(solution)/shard_map/ppermute | solution.py:52
  318.3 29.1 %collective-permute-start.41 = (f32[4,96,768]{2,1,0:T(8,128)}, f32[4,96,768]{2,1,0:T(8,128)}, u32[]{:S(2)}, u32[]{:S(2)}) collective-permute-start(f32[4,96,768]{2,1,0:T(8,128)} %get-tuple-element.193), channel_id=1, source_target_pairs={{0,8},{4,12},{8,0},{12,4},{16,24},{20,28},{24,16},{28,20},{1,9},{5... | collective-permute-start | bytes 3538952 | tf_op jit(solution)/shard_map/ppermute | solution.py:52
  320.0 28.8 %collective-permute-start.40 = (f32[4,96,768]{2,1,0:T(8,128)}, f32[4,96,768]{2,1,0:T(8,128)}, u32[]{:S(2)}, u32[]{:S(2)}) collective-permute-start(f32[4,96,768]{2,1,0:T(8,128)} %get-tuple-element.191), channel_id=1, source_target_pairs={{0,16},{4,20},{8,24},{12,28},{16,0},{20,4},{24,8},{28,12},{1,17},{... | collective-permute-start | bytes 3538952 | tf_op jit(solution)/shard_map/ppermute | solution.py:52
  324.8 37.1 %collective-permute-start.43 = (f32[192,1024]{1,0:T(8,128)}, f32[192,1024]{1,0:T(8,128)}, u32[]{:S(2)}, u32[]{:S(2)}) collective-permute-start(f32[192,1024]{1,0:T(8,128)} %get-tuple-element.199), channel_id=1, source_target_pairs={{0,1},{3,2},{4,5},{7,6},{8,9},{11,10},{12,13},{15,14},{16,17},{19,... | collective-permute-start | bytes 2359304 | tf_op jit(solution)/shard_map/ppermute | solution.py:419
  327.9 59.0 %collective-permute-start.37 = (f32[192,1024]{1,0:T(8,128)}, f32[192,1024]{1,0:T(8,128)}, u32[]{:S(2)}, u32[]{:S(2)}) collective-permute-start(f32[192,1024]{1,0:T(8,128)} %get-tuple-element.200), channel_id=1, source_target_pairs={{0,1},{1,0},{2,3},{3,2},{4,5},{5,4},{6,7},{7,6},{8,9},{9,8},{10,11... | collective-permute-start | bytes 2359304 | tf_op jit(solution)/shard_map/ppermute | solution.py:418
  334.8 68.3 %collective-permute-start.45 = (f32[2,2,96,768]{3,2,1,0:T(8,128)}, f32[2,2,96,768]{3,2,1,0:T(8,128)}, u32[]{:S(2)}, u32[]{:S(2)}) collective-permute-start(f32[2,2,96,768]{3,2,1,0:T(8,128)} %slice_bitcast_fusion.1), channel_id=1, source_target_pairs={{0,8},{4,12},{8,0},{12,4},{16,24},{20,28},{24,16},{28,20},{1,9},{5... | collective-permute-start | bytes 3538952 | tf_op jit(solution)/shard_map/ppermute | solution.py:52
  351.2 51.9 %collective-permute-start.42 = (f32[192,768]{1,0:T(8,128)}, f32[192,768]{1,0:T(8,128)S(1)}, u32[]{:S(2)}, u32[]{:S(2)}) collective-permute-start(f32[192,768]{1,0:T(8,128)} %fusion.34), channel_id=1, source_target_pairs={{0,1},{1,2},{2,3},{3,0},{4,5},{5,6},{6,7},{7,4},{8,9},{9,10},{10,1... | collective-permute-start | bytes 1769480 | tf_op jit(solution)/shard_map/ppermute | solution.py:62
  351.4 54.5 %collective-permute-start.39 = (f32[2,2,96,768]{3,2,1,0:T(8,128)}, f32[2,2,96,768]{3,2,1,0:T(8,128)}, u32[]{:S(2)}, u32[]{:S(2)}) collective-permute-start(f32[2,2,96,768]{3,2,1,0:T(8,128)} %slice.375), channel_id=1, source_target_pairs={{0,16},{4,20},{8,24},{12,28},{16,0},{20,4},{24,8},{28,12},{1,17},{... | collective-permute-start | bytes 3538952 | tf_op jit(solution)/shard_map/ppermute | solution.py:52
  425.6 24.7 %collective-permute-start.60 = (f32[192,768]{1,0:T(8,128)S(1)}, f32[192,768]{1,0:T(8,128)S(1)}, u32[]{:S(2)}, u32[]{:S(2)}) collective-permute-start(f32[192,768]{1,0:T(8,128)S(1)} %fusion.36), channel_id=1, source_target_pairs={{0,1},{1,2},{2,3},{3,0},{4,5},{5,6},{6,7},{7,4},{8,9},{9,10},{10,1... | collective-permute-start | bytes 1769480 | tf_op jit(solution)/shard_map/ppermute | solution.py:62
  450.4 21.1 %collective-permute-start.61 = (f32[1,96,768]{2,1,0:T(8,128)S(1)}, f32[1,96,768]{2,1,0:T(8,128)S(1)}, u32[]{:S(2)}, u32[]{:S(2)}) collective-permute-start(f32[1,96,768]{2,1,0:T(8,128)S(1)} %get-tuple-element.205), channel_id=1, source_target_pairs={{0,8},{4,12},{8,0},{12,4},{16,24},{20,28},{24,16},{28,20},{1,9},{5... | collective-permute-start | bytes 884744 | tf_op jit(solution)/shard_map/ppermute | solution.py:52
  465.1 27.4 %collective-permute-start.64 = (f32[1,96,768]{2,1,0:T(8,128)S(1)}, f32[1,96,768]{2,1,0:T(8,128)S(1)}, u32[]{:S(2)}, u32[]{:S(2)}) collective-permute-start(f32[1,96,768]{2,1,0:T(8,128)S(1)} %get-tuple-element.204), channel_id=1, source_target_pairs={{0,16},{4,20},{8,24},{12,28},{16,0},{20,4},{24,8},{28,12},{1,17},{... | collective-permute-start | bytes 884744 | tf_op jit(solution)/shard_map/ppermute | solution.py:52
  472.4 27.0 %collective-permute-start.62 = (f32[2,96,768]{2,1,0:T(8,128)}, f32[2,96,768]{2,1,0:T(8,128)}, u32[]{:S(2)}, u32[]{:S(2)}) collective-permute-start(f32[2,96,768]{2,1,0:T(8,128)} %pad_maximum_fusion.14), channel_id=1, source_target_pairs={{0,16},{4,20},{8,24},{12,28},{16,0},{20,4},{24,8},{28,12},{1,17},{... | collective-permute-start | bytes 1769480 | tf_op jit(solution)/shard_map/ppermute | solution.py:52
  473.8 21.6 %collective-permute-start.57 = (f32[1,96,768]{2,1,0:T(8,128)S(1)}, f32[1,96,768]{2,1,0:T(8,128)S(1)}, u32[]{:S(2)}, u32[]{:S(2)}) collective-permute-start(f32[1,96,768]{2,1,0:T(8,128)S(1)} %bitcast.312), channel_id=1, source_target_pairs={{0,16},{4,20},{8,24},{12,28},{16,0},{20,4},{24,8},{28,12},{1,17},{... | collective-permute-start | bytes 884744 | tf_op jit(solution)/shard_map/ppermute | solution.py:52
  480.9 31.2 %collective-permute-start.56 = (f32[192,1024]{1,0:T(8,128)}, f32[192,1024]{1,0:T(8,128)}, u32[]{:S(2)}, u32[]{:S(2)}) collective-permute-start(f32[192,1024]{1,0:T(8,128)} %get-tuple-element.126), channel_id=1, source_target_pairs={{0,1},{3,2},{4,5},{7,6},{8,9},{11,10},{12,13},{15,14},{16,17},{19,... | collective-permute-start | bytes 2359304 | tf_op jit(solution)/shard_map/ppermute | solution.py:427
  (101 other events, 1032.4 us)
Sparse Core Ops, SparseCore 0:
  242.7 135.2 all-gather.1
